TPU v7x, 256 devices: a whole 4x4x8 slice. The times are simulated.
256 devices in a mesh: ctx: 64 (over y, x, z_lo), mp: 4 (over z_hi, core).
Axes of the slice: x: 4, y: 4, z: 8 (z_hi: 2, z_lo: 4; z = z_hi * 4 + z_lo), core: 2. Of those that a mesh axis runs over, the one named last changes fastest.
Arguments:
- query_proj: bfloat16 [4096, 16384], P('mp', 'ctx'), may hold values from -6 to 6
- key_proj: bfloat16 [4096, 16384], P('mp', 'ctx'), may hold values from -6 to 6
- value_proj: bfloat16 [4096, 16384], P('mp', 'ctx'), may hold values from -6 to 6
- short_taps: float32 [3, 256, 7], P(None, 'mp'), may hold values from -2 to 2
- long_filter: float32 [4096, 16384], P(('mp', 'ctx')), may hold values from -0.046875 to 0.046875
- skip_bias: float32 [4096], P(('mp', 'ctx')), may hold values from -4 to 4
- out_weight: bfloat16 [4096, 4096], P('ctx', 'mp'), may hold values from -0.09375 to 0.09375
Outputs:
- mixed: bfloat16 [4096, 16384], P('mp', 'ctx')
All inputs are finite; a program needn't handle non-finite values.
Results may differ from a plain program's by a relative error of at most 0.0064.
Values may be sent and summed in bfloat16 or wider, within the bound.
No kernel may reach another device: no remote copies, remote signals or barrier semaphores. Data moves between devices by JAX's collectives and lax.ppermute only.
A program may use at most 64 MiB of HBM per device.

v0:
```python
import math

import jax
import jax.numpy as jnp
from jax import lax
from jax.sharding import PartitionSpec as P

HIGHEST_PREC = lax.Precision.HIGHEST


def shifted(value, axis, steps):
    count = lax.axis_size(axis)
    leading, last = (max(0, -steps), min(count, count - steps))
    return lax.ppermute(value, axis, [(source, source + steps) for source in range(leading, last)])


def phase_table(row_count, col_count, period):
    row_ids = lax.broadcasted_iota(jnp.int32, (row_count, col_count), 0)
    col_ids = lax.broadcasted_iota(jnp.int32, (row_count, col_count), 1)
    phase = row_ids * col_ids % period
    angle = phase.astype(jnp.float32) * (2.0 * math.pi / period)
    return (jnp.cos(angle), -jnp.sin(angle))


def matmul_high(left, right):
    return jnp.matmul(left, right, precision=HIGHEST_PREC)


def forward_dft(signal, tables):
    outer_cos, outer_sin, spin_cos, spin_sin, inner_cos, inner_sin = tables
    half_outer = outer_cos.shape[1]
    inner_len = inner_cos.shape[0]
    blocks = signal.reshape(signal.shape[0], half_outer, inner_len)
    first_re = jnp.einsum("ka,cab->ckb", outer_cos, blocks, precision=HIGHEST_PREC)
    first_im = jnp.einsum("ka,cab->ckb", outer_sin, blocks, precision=HIGHEST_PREC)
    turned_re = first_re * spin_cos - first_im * spin_sin
    turned_im = first_re * spin_sin + first_im * spin_cos
    spec_re = matmul_high(turned_re, inner_cos) - matmul_high(turned_im, inner_sin)
    spec_im = matmul_high(turned_re, inner_sin) + matmul_high(turned_im, inner_cos)
    return (spec_re, spec_im)


def inverse_dft(spec_re, spec_im, tables):
    outer_cos, outer_sin, spin_cos, spin_sin, inner_cos, inner_sin = tables
    half_outer = outer_cos.shape[1]
    inner_len = inner_cos.shape[0]
    back_re = matmul_high(spec_re, inner_cos) + matmul_high(spec_im, inner_sin)
    back_im = matmul_high(spec_im, inner_cos) - matmul_high(spec_re, inner_sin)
    turned_re = back_re * spin_cos + back_im * spin_sin
    turned_im = back_im * spin_cos - back_re * spin_sin
    signal = jnp.einsum("ka,ckb->cab", outer_cos, turned_re, precision=HIGHEST_PREC)
    signal = signal + jnp.einsum("ka,ckb->cab", outer_sin, turned_im, precision=HIGHEST_PREC)
    return signal.reshape(spec_re.shape[0], half_outer * inner_len) / (2.0 * half_outer * inner_len)


def long_mix(chan_prod, long_filter, skip_bias, tables):
    signal = chan_prod.astype(jnp.float32)
    sig_re, sig_im = forward_dft(signal, tables)
    filt_re, filt_im = forward_dft(long_filter, tables)
    prod_re = sig_re * filt_re - sig_im * filt_im
    prod_im = sig_re * filt_im + sig_im * filt_re
    conv = inverse_dft(prod_re, prod_im, tables)
    return (conv + skip_bias[:, None] * signal).astype(jnp.bfloat16)


def causal_filter(signal, rim, taps):
    span_len = signal.shape[1]
    kernel = taps.shape[1]
    joined = jnp.concatenate([rim, signal], axis=1).astype(jnp.float32)
    running = jnp.zeros((signal.shape[0], span_len), jnp.float32)
    for shift_idx in range(kernel):
        start_col = kernel - 1 - shift_idx
        running = (
            running
            + taps[:, shift_idx : shift_idx + 1] * joined[:, start_col : start_col + span_len]
        )
    return running


def shards(query_proj, key_proj, value_proj, short_taps, long_filter, skip_bias, out_weight):
    local_dim = query_proj.shape[0]
    tok_len = query_proj.shape[1]
    kernel = short_taps.shape[2]
    group_size = local_dim // short_taps.shape[1]
    taps_all = jnp.repeat(short_taps, group_size, axis=1)
    edge = tok_len - (kernel - 1)
    stacked = jnp.stack([query_proj[:, edge:], key_proj[:, edge:], value_proj[:, edge:]])
    rims = shifted(stacked, "ctx", 1)
    q_feat = causal_filter(query_proj, rims[0], taps_all[0])
    k_feat = causal_filter(key_proj, rims[1], taps_all[1])
    v_feat = causal_filter(value_proj, rims[2], taps_all[2])
    product = (k_feat * v_feat).astype(jnp.bfloat16)
    chan_prod = lax.all_to_all(product, "ctx", split_axis=0, concat_axis=1, tiled=True)
    seq_len = chan_prod.shape[1]
    inner_len = min(tok_len, 128)
    outer_len = 2 * (seq_len // inner_len)
    outer_cos, outer_sin = phase_table(outer_len, outer_len // 2, outer_len)
    spin_cos, spin_sin = phase_table(outer_len, inner_len, outer_len * inner_len)
    inner_cos, inner_sin = phase_table(inner_len, inner_len, inner_len)
    tables = (outer_cos, outer_sin, spin_cos, spin_sin, inner_cos, inner_sin)
    mixed_chan = long_mix(chan_prod, long_filter, skip_bias, tables)
    returned = lax.all_to_all(mixed_chan, "ctx", split_axis=1, concat_axis=0, tiled=True)
    gated = (q_feat * returned.astype(jnp.float32)).astype(jnp.bfloat16)
    full_rows = lax.all_gather(gated, "mp", axis=0, tiled=True)
    result = lax.dot_general(
        lax.all_gather(out_weight, "ctx", axis=0, tiled=True),
        full_rows,
        (((0,), (0,)), ((), ())),
        preferred_element_type=jnp.float32,
    )
    return result.astype(jnp.bfloat16)


def solution(mesh):
    return jax.shard_map(
        shards,
        mesh=mesh,
        in_specs=(
            P("mp", "ctx"),
            P("mp", "ctx"),
            P("mp", "ctx"),
            P(None, "mp", None),
            P(("mp", "ctx"), None),
            P(("mp", "ctx")),
            P("ctx", "mp"),
        ),
        out_specs=P("mp", "ctx"),
        check_vma=False,
    )
```

profile of v0, /device:TPU:32, one launch (start us, length us, event | category | flops | bytes accessed | tf_op | source)
XLA Modules:
  0.0 562.3 jit_solution(5507468836540338351)
XLA Ops:
  6.5 1.2 slice.170
  7.8 1.1 slice.169
  9.1 1.1 slice.168
  10.4 3.8 collective-permute-start
  14.2 0.2 copy.90
  14.4 2.3 fusion.72
  16.7 3.6 fusion.77
  20.4 0.5 sine_negate_fusion
  20.9 0.6 slice_bitcast_fusion.1
  21.8 0.6 fusion.197
  22.7 5.1 fusion.2
  27.8 0.6 fusion.196
  28.4 0.9 copy.88
  29.3 0.9 copy.89
  30.3 1.7 maximum_convert_fusion.1
  32.2 6.2 %fusion.36 = bf16[1024,256]{1,0:T(8,128)(2,1)} fusion(f32[1024,262]{1,0:T(8,128)S(1)} %get-tuple-element.37, f32[1024,262]{1,0:T(8,128)S(1)} %get-tuple-element.36, f32[1024]{0:T(1024)S(1)} %bitcast.162, f32[1024]{0:T(1024)S(1)} %bitcast.163, f32[1024]{0:T(1024)S(1)} %bitcast.164, f32[1024]{0:T(1024)S(1)} %bitcast.165, f32[1024]{0:T(1024)S(1)} %bitcast.166, ...), kind=kLoop, calls=%fused_computation.40 | loop fusion | flops 7340032 | bytes 15261696 | tf_op jit(solution)/shard_map/convert_element_type | solution.py:92
  38.4 10.5 %all-to-all-start = ((bf16[64,16,256]{2,1,0:T(8,128)(2,1)}), bf16[64,16,256]{2,1,0:T(8,128)(2,1)S(1)}, u32[]{:S(2)}, u32[]{:S(2)}) async-start(bf16[64,16,256]{2,1,0:T(8,128)(2,1)} %bitcast.30), calls=%async_computation | async-start | bytes 1048576 | tf_op jit(solution)/shard_map/all_to_all | solution.py:93
  48.9 5.1 fusion
  54.2 5.8 %fusion.18 = f32[16,256,128]{2,1,0:T(8,128)} fusion(f32[16,256,128]{2,1,0:T(8,128)} %fusion.2, f32[256,16,128]{2,0,1:T(8,128)S(1)} %fusion.72, f32[256,16,128]{2,0,1:T(8,128)} %fusion.77, f32[256,128]{1,0:T(8,128)S(1)} %get-tuple-element.34, f32[256,128]{1,0:T(8,128)S(1)} %get-tuple-element.35), kind=kOutput, calls=%fused_computation.26 | convolution fusion | flops 807632896 | bytes 8650752 | tf_op jit(solution)/shard_map/dot_general | solution.py:26
  60.0 3.7 fusion.21
  63.7 2.1 all-to-all-done
  65.8 0.2 copy.58
  66.0 0.2 reshape.65
  66.1 1.5 fusion.74
  67.7 1.5 fusion.79
  69.2 4.0 fusion.65
  73.1 3.8 fusion.63
  76.9 3.8 convolution_subtract_fusion.1
  80.8 4.4 multiply_add_fusion
  85.2 2.3 fusion.99
  87.5 2.3 fusion.97
  89.8 2.3 convolution_add_fusion
  92.0 2.3 convolution_subtract_fusion
  94.3 2.6 fusion.10
  96.9 2.4 fusion.30
  99.3 0.3 copy.71
  99.7 0.3 div.13
  100.0 1.4 fusion.56
  101.4 8.5 %all-to-all-start.1 = ((bf16[16,64,256]{2,0,1:T(8,128)(2,1)}), bf16[16,64,256]{2,0,1:T(8,128)(2,1)S(1)}, u32[]{:S(2)}, u32[]{:S(2)}) async-start(bf16[16,64,256]{2,0,1:T(8,128)(2,1)} %fusion.56), calls=%async_computation.1 | async-start | bytes 1048576 | tf_op jit(solution)/shard_map/all_to_all | solution.py:102
  110.3 0.2 copy.87
  110.5 0.3 maximum_convert_fusion
  110.8 15.6 %all-to-all-done.1 = bf16[16,64,256]{2,0,1:T(8,128)(2,1)S(1)} async-done(((bf16[16,64,256]{2,0,1:T(8,128)(2,1)}), bf16[16,64,256]{2,0,1:T(8,128)(2,1)S(1)}, u32[]{:S(2)}, u32[]{:S(2)}) %all-to-all-start.1) | async-done | bytes 524320 | tf_op jit(solution)/shard_map/all_to_all | solution.py:102
  126.5 3.5 fusion.50
  130.0 0.7 all-gather.5.cloned.1.call-update
  130.7 40.6 %all-gather.3.cloned.1.call-done = bf16[4096,256]{1,0:T(8,128)(2,1)} async-done(((bf16[1024,256]{1,0:T(8,128)(2,1)}), bf16[4096,256]{1,0:T(8,128)(2,1)}) %all-gather.3.cloned.1.call-update) | async-done | bytes 2097168 | tf_op jit(solution)/shard_map/all_gather | solution.py:104
  171.3 376.6 %all-gather.5.cloned.1.call-done = bf16[4096,1024]{1,0:T(8,128)(2,1)} async-done(((bf16[64,1024]{1,0:T(8,128)(2,1)}), bf16[4096,1024]{1,0:T(8,128)(2,1)}) %all-gather.5.cloned.1.call-update) | async-done | bytes 8388624 | tf_op jit(solution)/shard_map/all_gather | solution.py:106
  547.9 6.4 %fusion.33 = bf16[1024,256]{0,1:T(8,128)(2,1)S(1)} fusion(bf16[4096,256]{1,0:T(8,128)(2,1)} %all-gather.3.cloned.1.call-done, bf16[4096,1024]{1,0:T(8,128)(2,1)} %all-gather.5.cloned.1.call-done), kind=kOutput, calls=%fused_computation.36 | convolution fusion | flops 2147745792 | bytes 11010048 | tf_op jit(solution)/shard_map/dot_general | solution.py:105
  554.3 1.0 copy.73
  (68 shorter events, 1.6 us)
Async XLA Ops:
  6.5 7.7 %copy-start.7 = (f32[16,16384]{1,0:T(8,128)S(1)}, f32[16,16384]{1,0:T(8,128)}, u32[]{:S(2)}) copy-start(f32[16,16384]{1,0:T(8,128)} %param.11) | copy-start | bytes 3145732
  10.4 18.1 %collective-permute-start = (bf16[3,1024,6]{1,2,0:T(8,128)(2,1)S(1)}, bf16[3,1024,6]{1,2,0:T(8,128)(2,1)S(1)}, u32[]{:S(2)}, u32[]{:S(2)}) collective-permute-start(bf16[3,1024,6]{1,2,0:T(8,128)(2,1)S(1)} %pad_maximum_fusion), channel_id=1, source_target_pairs={{0,4},{4,8},{8,12},{12,16},{16,20},{20,24},{24,28},{28,32},{32,36}... | collective-permute-start | bytes 110600 | tf_op jit(solution)/shard_map/ppermute | solution.py:14
  16.7 4.2 copy-start.23
  22.7 7.5 %copy-start.4 = (bf16[1024,256]{1,0:T(8,128)(2,1)S(1)}, bf16[1024,256]{1,0:T(8,128)(2,1)}, u32[]{:S(2)}) copy-start(bf16[1024,256]{1,0:T(8,128)(2,1)} %param.9) | copy-start | bytes 1572868
  22.7 7.5 %copy-start.5 = (bf16[1024,256]{1,0:T(8,128)(2,1)S(1)}, bf16[1024,256]{1,0:T(8,128)(2,1)}, u32[]{:S(2)}) copy-start(bf16[1024,256]{1,0:T(8,128)(2,1)} %param.8) | copy-start | bytes 1572868
  30.2 1.9 copy-start.9
  30.2 1.9 copy-start.10
  30.2 1.9 copy-start.11
  30.2 1.9 copy-start.12
  30.2 1.9 copy-start.13
  30.2 1.9 copy-start.14
  30.2 1.9 copy-start.15
  30.3 1.9 copy-start.16
  30.3 1.9 copy-start.17
  30.3 1.9 copy-start.18
  30.3 1.9 copy-start.19
  30.3 1.9 copy-start.20
  30.3 1.9 copy-start.21
  30.3 1.9 copy-start.22
  38.4 27.4 %all-to-all-start = ((bf16[64,16,256]{2,1,0:T(8,128)(2,1)}), bf16[64,16,256]{2,1,0:T(8,128)(2,1)S(1)}, u32[]{:S(2)}, u32[]{:S(2)}) async-start(bf16[64,16,256]{2,1,0:T(8,128)(2,1)} %bitcast.30), calls=%async_computation | async-start | bytes 1048576 | tf_op jit(solution)/shard_map/all_to_all | solution.py:93
  54.2 5.8 %copy-start = (f32[256,16,128]{2,0,1:T(8,128)S(1)}, f32[256,16,128]{2,0,1:T(8,128)}, u32[]{:S(2)}) copy-start(f32[256,16,128]{2,0,1:T(8,128)} %fusion.77) | copy-start | bytes 6291460
  54.2 5.8 %copy-start.1 = (f32[16,256,128]{2,1,0:T(8,128)S(1)}, f32[16,256,128]{2,1,0:T(8,128)}, u32[]{:S(2)}) copy-start(f32[16,256,128]{2,1,0:T(8,128)} %fusion) | copy-start | bytes 6291460
  76.9 3.8 copy-start.2
  76.9 3.8 copy-start.3
  99.3 0.7 copy-start.24
  100.0 10.0 %copy-start.8 = (f32[64,7]{0,1:T(8,128)S(1)}, f32[64,7]{0,1:T(8,128)}, u32[]{:S(2)}) copy-start(f32[64,7]{0,1:T(8,128)} %get-tuple-element.32) | copy-start | bytes 5380
  100.0 10.5 %copy-start.6 = (bf16[1024,256]{1,0:T(8,128)(2,1)S(1)}, bf16[1024,256]{1,0:T(8,128)(2,1)}, u32[]{:S(2)}) copy-start(bf16[1024,256]{1,0:T(8,128)(2,1)} %param.7) | copy-start | bytes 1572868
  101.4 25.1 %all-to-all-start.1 = ((bf16[16,64,256]{2,0,1:T(8,128)(2,1)}), bf16[16,64,256]{2,0,1:T(8,128)(2,1)S(1)}, u32[]{:S(2)}, u32[]{:S(2)}) async-start(bf16[16,64,256]{2,0,1:T(8,128)(2,1)} %fusion.56), calls=%async_computation.1 | async-start | bytes 1048576 | tf_op jit(solution)/shard_map/all_to_all | solution.py:102
  109.9 61.4 %all-gather.3.cloned.1.call-start = ((), (), s32[]{:S(2)}) async-start(), calls=%async_computation.2 | async-start | bytes 2621440 | tf_op jit(solution)/shard_map/all_gather | solution.py:104
  129.9 417.9 %all-gather.5.cloned.1.call-start = ((), (), s32[]{:S(2)}) async-start(), calls=%async_computation.3 | async-start | bytes 8519680 | tf_op jit(solution)/shard_map/all_gather | solution.py:106
Sparse Core Ops, SparseCore 0:
  130.1 41.1 all-gather.2
  173.1 374.7 all-gather.4
where the time goes:
time: 571 us; the launch traced here: 562 us
  waiting for transfers between devices  436 us (76%)
  matrix products  65 us (11%)
  starting transfers between devices  22.9 us (4%)
  between operations  14.2 us (2%)
  other arithmetic  13.7 us (2%)
  local copies, waits for them, and re-layouts  10.8 us (2%)
    all_gather x1, waiting for transfers between devices, shards(): lax.all_gather(out_weight, 'ctx', axis=0, tiled=True)  377 us
    dot_general x12, matrix products, matmul_high(): return jnp.matmul(left, right, precision=HIGHEST_PREC)  44.7 us
    all_gather x1, waiting for transfers between devices, shards(): full_rows = lax.all_gather(gated, 'mp', axis=0, tiled=True)  40.6 us
    all_to_all x1, waiting for transfers between devices, shards(): lax.all_to_all(mixed_chan, 'ctx', split_axis=1, concat_axis=0, tiled=True)  15.6 us
  transfers between devices with their start and end apart: 5, of which 4 were waited for; matrix products, arithmetic and copies ran while one was open for 5% of the time, Pallas kernels for 0%

commit v1 on v0

v1 whole, which is shorter than its diff:
```python
import math

import jax
import jax.numpy as jnp
import numpy as np
from jax import lax
from jax.experimental import pallas as pl
from jax.experimental.pallas import tpu as pltpu
from jax.sharding import Mesh, PartitionSpec as P

BF16 = jnp.bfloat16
F32 = jnp.float32
TAIL = 16
CTX = ("y", "x", "zl")
VMEM_LIMIT = 48 * 1024 * 1024


def hi_lo(table):
    hi = table.astype(np.float32).astype(jnp.bfloat16)
    lo = (table - hi.astype(np.float64)).astype(np.float32).astype(jnp.bfloat16)
    return hi, lo


def dft_tables(outer, inner):
    length = outer * inner
    freq = np.arange(outer)[:, None] + 0.25
    angle = 2.0 * np.pi * freq * np.arange(outer)[None, :] / outer
    first = np.concatenate([np.cos(angle), -np.sin(angle)], axis=0)
    spin = 2.0 * np.pi * freq * np.arange(inner)[None, :] / length
    steps = np.outer(np.arange(inner), np.arange(inner)) % inner
    turn = 2.0 * np.pi * steps / inner
    cos, sin = np.cos(turn), np.sin(turn)
    second = np.block([[cos, -sin], [sin, cos]])
    return {
        "first": hi_lo(first),
        "last": hi_lo(first.T.copy()),
        "spin": (np.cos(spin).astype(np.float32), np.sin(spin).astype(np.float32)),
        "second": hi_lo(second),
    }


def dot(left, right):
    return jnp.dot(left, right, preferred_element_type=F32)


def split_bf16(value):
    hi = value.astype(BF16)
    return hi, (value - hi.astype(F32)).astype(BF16)


def tail_kernel(q_ref, k_ref, v_ref, out_ref):
    lanes = q_ref.shape[1]
    row = lax.broadcasted_iota(jnp.int32, (TAIL, lanes), 0)
    lane = lax.broadcasted_iota(jnp.int32, (TAIL, lanes), 1)
    pick = jnp.where(lane == lanes - TAIL + row, 1.0, 0.0).astype(BF16)
    for index, ref in enumerate((q_ref, k_ref, v_ref)):
        picked = lax.dot_general(pick, ref[...], (((1,), (1,)), ((), ())), preferred_element_type=F32)
        out_ref[index] = picked.astype(BF16)


def take_tails(query, key, value):
    rows, cols = query.shape
    spec = pl.BlockSpec((rows, 128), lambda i: (0, cols // 128 - 1))
    return pl.pallas_call(
        tail_kernel,
        grid=(1,),
        in_specs=[spec] * 3,
        out_specs=pl.BlockSpec((3, TAIL, rows), lambda i: (0, 0, 0)),
        out_shape=jax.ShapeDtypeStruct((3, TAIL, rows), BF16),
        name="tails",
    )(query, key, value)


def short_kernel(taps_ref, q_ref, k_ref, v_ref, rim_ref, q_out, u_out, left_ref):
    rows, cols = q_ref.shape
    _, groups, taps = taps_ref.shape
    size = rows // groups
    row = lax.broadcasted_iota(jnp.int32, (TAIL, 128), 0)
    lane = lax.broadcasted_iota(jnp.int32, (TAIL, 128), 1)
    place = jnp.where(lane == 128 - TAIL + row, 1.0, 0.0).astype(BF16)
    for index in range(3):
        left_ref[index] = lax.dot_general(
            rim_ref[index], place, (((0,), (0,)), ((), ())), preferred_element_type=F32
        )
    lane = lax.broadcasted_iota(jnp.int32, (size, 128), 1)

    def group(g, carry):
        at = pl.ds(pl.multiple_of(g * size, size), size)
        feats = []
        for index, ref in enumerate((q_ref, k_ref, v_ref)):
            wide = ref[at, :].astype(F32)
            tiles = [left_ref[index, at, :]] + [wide[:, i * 128 : i * 128 + 128] for i in range(cols // 128)]
            sums = [taps_ref[index, g, 0] * tile for tile in tiles[1:]]
            for tap in range(1, taps):
                turned = [pltpu.roll(tile, tap, 1) for tile in tiles]
                weight = taps_ref[index, g, tap]
                for i in range(cols // 128):
                    sums[i] += weight * jnp.where(lane >= tap, turned[i + 1], turned[i])
            feats.append(sums)
        for i in range(cols // 128):
            q_out[at, i * 128 : i * 128 + 128] = feats[0][i].astype(BF16)
            u_out[at, i * 128 : i * 128 + 128] = (feats[1][i] * feats[2][i]).astype(BF16)
        return carry

    lax.fori_loop(0, groups, group, 0, unroll=2)


def short_filters(taps, query, key, value, rims):
    rows, cols = query.shape
    whole = pl.BlockSpec(memory_space=pltpu.VMEM)
    return pl.pallas_call(
        short_kernel,
        in_specs=[pl.BlockSpec(memory_space=pltpu.SMEM)] + [whole] * 4,
        out_specs=[whole] * 2,
        out_shape=[jax.ShapeDtypeStruct((rows, cols), BF16)] * 2,
        scratch_shapes=[pltpu.VMEM((3, rows, 128), F32)],
        compiler_params=pltpu.CompilerParams(vmem_limit_bytes=VMEM_LIMIT),
        cost_estimate=pl.CostEstimate(flops=3 * 14 * rows * cols, bytes_accessed=10 * rows * cols, transcendentals=0),
        name="short_filters",
    )(taps, query, key, value, rims)


def second_dft(hi, lo, second_hi, second_lo):
    return dot(hi, second_hi[...]) + dot(lo, second_hi[...]) + dot(hi, second_lo[...])


def channel_rows(ref, c, outer, chans):
    halves = ref.shape[0] // (outer * chans)
    parts = [ref[pl.ds(half * outer * chans + c, outer, stride=chans), :] for half in range(halves)]
    return jnp.concatenate(parts, axis=1)


def filter_kernel(scale, filt_ref, f_hi, f_lo, cos_ref, sin_ref, s_hi, s_lo, out_ref, rows_ref, g_hi, g_lo):
    chans, _ = filt_ref.shape
    outer, inner = cos_ref.shape
    for half in range(inner // 128):
        for a in range(outer):
            start = a * inner + half * 128
            at = (half * outer + a) * chans
            rows_ref[at : at + chans, :] = filt_ref[:, start : start + 128]

    def channel(c, carry):
        hi, lo = split_bf16(channel_rows(rows_ref, c, outer, chans) * scale)
        mixed = dot(f_hi[...], hi) + dot(f_hi[...], lo) + dot(f_lo[...], hi)
        re, im = mixed[:outer], mixed[outer:]
        at = pl.ds(pl.multiple_of(c * outer, outer), outer)
        g_hi[at, :inner], g_lo[at, :inner] = split_bf16(re * cos_ref[...] + im * sin_ref[...])
        g_hi[at, inner:], g_lo[at, inner:] = split_bf16(im * cos_ref[...] - re * sin_ref[...])
        return carry

    lax.fori_loop(0, chans, channel, 0, unroll=2)

    def block(i, carry):
        at = pl.ds(pl.multiple_of(i * 256, 256), 256)
        out_ref[at, :] = second_dft(g_hi[at, :], g_lo[at, :], s_hi, s_lo)
        return carry

    lax.fori_loop(0, chans * outer // 256, block, 0)


def filter_spectrum(long_filter, tables, outer, inner):
    chans = long_filter.shape[0]
    rows = chans * outer
    whole = pl.BlockSpec(memory_space=pltpu.VMEM)
    operands = (long_filter, *tables["first"], *tables["spin"], *tables["second"])
    return pl.pallas_call(
        lambda *refs: filter_kernel(1.0 / (outer * inner), *refs),
        in_specs=[whole] * len(operands),
        out_specs=whole,
        out_shape=jax.ShapeDtypeStruct((rows, 2 * inner), F32),
        scratch_shapes=[
            pltpu.VMEM((rows * inner // 128, 128), F32),
            pltpu.VMEM((rows, 2 * inner), BF16),
            pltpu.VMEM((rows, 2 * inner), BF16),
        ],
        compiler_params=pltpu.CompilerParams(vmem_limit_bytes=VMEM_LIMIT),
        cost_estimate=pl.CostEstimate(flops=3 * 2 * rows * 4 * inner * inner, bytes_accessed=5 * 2**20, transcendentals=0),
        name="filter_spectrum",
    )(*operands)


def conv_kernel(
    skip_ref, u_ref, spec_ref, f_hi, f_lo, l_hi, l_lo, cos_ref, sin_ref, s_hi, s_lo,
    out_ref, rows_ref, z_ref, g_hi, g_lo,
):
    outer, chans, inner = u_ref.shape
    rows = outer * chans
    halves = inner // 128
    flat = u_ref[...].reshape(rows, inner).astype(F32)
    for half in range(halves):
        rows_ref[half * rows : (half + 1) * rows, :] = flat[:, half * 128 : (half + 1) * 128]

    def channel(c, carry):
        sig = channel_rows(rows_ref, c, outer, chans).astype(BF16)
        mixed = dot(f_hi[...], sig) + dot(f_lo[...], sig)
        re, im = mixed[:outer], mixed[outer:]
        at = pl.ds(pl.multiple_of(c * outer, outer), outer)
        g_hi[at, :inner], g_lo[at, :inner] = split_bf16(re * cos_ref[...] + im * sin_ref[...])
        g_hi[at, inner:], g_lo[at, inner:] = split_bf16(im * cos_ref[...] - re * sin_ref[...])
        return carry

    lax.fori_loop(0, chans, channel, 0, unroll=2)

    def block(i, carry):
        at = pl.ds(pl.multiple_of(i * 256, 256), 256)
        sig = second_dft(g_hi[at, :], g_lo[at, :], s_hi, s_lo)
        sr, si = sig[:, :inner], sig[:, inner:]
        hr, hm = spec_ref[at, :inner], spec_ref[at, inner:]
        r_hi, r_lo = split_bf16(sr * hr - si * hm)
        i_hi, i_lo = split_bf16(-(sr * hm + si * hr))
        back = second_dft(
            jnp.concatenate([r_hi, i_hi], axis=1), jnp.concatenate([r_lo, i_lo], axis=1), s_hi, s_lo
        )
        back = back.reshape(256 // outer, outer, 2 * inner)
        re, im = back[:, :, :inner], back[:, :, inner:]
        cos, sin = cos_ref[...], sin_ref[...]
        r_hi, r_lo = split_bf16((re * cos + im * sin).reshape(256, inner))
        i_hi, i_lo = split_bf16((re * sin - im * cos).reshape(256, inner))
        g_hi[at, :inner], g_lo[at, :inner] = r_hi, r_lo
        g_hi[at, inner:], g_lo[at, inner:] = i_hi, i_lo
        return carry

    lax.fori_loop(0, chans * outer // 256, block, 0)

    def finish(c, carry):
        at = pl.ds(pl.multiple_of(c * outer, outer), outer)
        hi = jnp.concatenate([g_hi[at, :inner], g_hi[at, inner:]], axis=0)
        lo = jnp.concatenate([g_lo[at, :inner], g_lo[at, inner:]], axis=0)
        conv = dot(l_hi[...], hi) + dot(l_hi[...], lo) + dot(l_lo[...], hi)
        mixed = conv + skip_ref[c] * channel_rows(rows_ref, c, outer, chans)
        for half in range(halves):
            z_ref[pl.ds(half * rows + c, outer, stride=chans), :] = mixed[:, half * 128 : (half + 1) * 128]
        return carry

    lax.fori_loop(0, chans, finish, 0, unroll=2)
    for half in range(halves):
        result = z_ref[half * rows : (half + 1) * rows, :].astype(BF16).reshape(outer, chans, 128)
        for copy in range(out_ref.shape[1]):
            out_ref[:, copy, :, half * 128 : (half + 1) * 128] = result


def long_mix(chan_prod, spectrum, skip_bias, tables, copies):
    outer, chans, inner = chan_prod.shape
    rows = outer * chans
    whole = pl.BlockSpec(memory_space=pltpu.VMEM)
    operands = (chan_prod, spectrum, *tables["first"], *tables["last"], *tables["spin"], *tables["second"])
    return pl.pallas_call(
        conv_kernel,
        in_specs=[pl.BlockSpec(memory_space=pltpu.SMEM)] + [whole] * len(operands),
        out_specs=whole,
        out_shape=jax.ShapeDtypeStruct((outer, copies, chans, inner), BF16),
        scratch_shapes=[
            pltpu.VMEM((rows * inner // 128, 128), F32),
            pltpu.VMEM((rows * inner // 128, 128), F32),
            pltpu.VMEM((rows, 2 * inner), BF16),
            pltpu.VMEM((rows, 2 * inner), BF16),
        ],
        compiler_params=pltpu.CompilerParams(vmem_limit_bytes=VMEM_LIMIT),
        cost_estimate=pl.CostEstimate(flops=6 * 2 * rows * 4 * inner * inner, bytes_accessed=6 * 2**20, transcendentals=0),
        name="long_conv",
    )(skip_bias, *operands)


def project_kernel(place_ref, z_own, z_other, q_own, q_other, w_ref, out_ref, g_ref, gt_ref):
    ctx, halves, chans, cols = z_own.shape
    panel = ctx * chans
    unit = 4 * chans

    @pl.when(pl.program_id(0) == 0)
    def _():
        zl, zh, core = place_ref[0], place_ref[1], place_ref[2]
        for other, (z, q) in enumerate(((z_own, q_own), (z_other, q_other))):
            for half in range(halves):
                index = half * 2 + jnp.bitwise_xor(core, other)
                source = jnp.bitwise_xor(zh, half)
                for unit_at in range(ctx // 4):
                    z_part = z[unit_at * 4 : unit_at * 4 + 4, half].reshape(unit, cols).astype(F32)
                    q_part = q[source, unit_at * unit : (unit_at + 1) * unit, :].astype(F32)
                    turned = jnp.bitwise_and(zl - unit_at % 4, 3)
                    start = index * panel + (unit_at // 4) * 4 * unit + turned * unit
                    g_ref[pl.ds(pl.multiple_of(start, unit), unit), :] = (q_part * z_part).astype(BF16)
        for at in range(0, 4 * panel, 256):
            gt_ref[:, at : at + 256] = g_ref[at : at + 256, :].T

    out_ref[...] = dot(gt_ref[...], w_ref[...]).T.astype(BF16)


def project(place, z_own, z_other, q_own, q_other, weight):
    depth, width = weight.shape
    cols = z_own.shape[3]
    block = 256
    keep = lambda rank: (lambda i: (0,) * rank)
    return pl.pallas_call(
        project_kernel,
        grid=(width // block,),
        in_specs=[
            pl.BlockSpec(memory_space=pltpu.SMEM),
            pl.BlockSpec(z_own.shape, keep(4)),
            pl.BlockSpec(z_own.shape, keep(4)),
            pl.BlockSpec(q_own.shape, keep(3)),
            pl.BlockSpec(q_own.shape, keep(3)),
            pl.BlockSpec((depth, block), lambda i: (0, i)),
        ],
        out_specs=pl.BlockSpec((block, cols), lambda i: (i, 0)),
        out_shape=jax.ShapeDtypeStruct((width, cols), BF16),
        scratch_shapes=[pltpu.VMEM((depth, cols), BF16), pltpu.VMEM((cols, depth), BF16)],
        compiler_params=pltpu.CompilerParams(vmem_limit_bytes=VMEM_LIMIT),
        cost_estimate=pl.CostEstimate(flops=2 * depth * width * cols, bytes_accessed=2 * depth * (width + cols), transcendentals=0),
        name="project",
    )(place, z_own, z_other, q_own, q_other, weight)


def turned(value, axis, steps):
    count = lax.axis_size(axis)
    return lax.ppermute(value, axis, [(source, (source + steps) % count) for source in range(count)])


def shards(query_proj, key_proj, value_proj, short_taps, long_filter, skip_bias, out_weight):
    rows, cols = query_proj.shape
    ctx = lax.axis_size(CTX)
    chans = long_filter.shape[0]
    tables = dft_tables(ctx, cols)

    tails = take_tails(query_proj, key_proj, value_proj)
    rims = lax.ppermute(tails, CTX, [(source, source + 1) for source in range(ctx - 1)])

    weight_run = jnp.concatenate([out_weight] + [turned(out_weight, "zl", step) for step in (1, 2, 3)], axis=0)
    weight = lax.all_gather(weight_run, ("y", "x"), axis=0, tiled=True)

    spectrum = filter_spectrum(long_filter, tables, ctx, cols)
    q_feat, product = short_filters(short_taps, query_proj, key_proj, value_proj, rims)

    chan_prod = lax.all_to_all(product.reshape(ctx, chans, cols), CTX, split_axis=0, concat_axis=0, tiled=True)
    q_own = jnp.stack([q_feat, turned(q_feat, "zh", 1)])
    q_other = turned(q_own, "core", 1)

    mixed = long_mix(chan_prod, spectrum, skip_bias, tables, 2)
    z_own = lax.all_to_all(
        mixed.reshape(2 * ctx, chans, cols), CTX + ("zh",), split_axis=0, concat_axis=0, tiled=True
    ).reshape(ctx, 2, chans, cols)
    z_other = turned(z_own, "core", 1)

    place = jnp.stack([lax.axis_index(name) for name in ("zl", "zh", "core")]).astype(jnp.int32)
    return project(place, z_own, z_other, q_own, q_other, weight)


def solution(mesh):
    fine = Mesh(mesh.devices.reshape(4, 4, 4, 2, 2), ("y", "x", "zl", "zh", "core"))
    mp = ("zh", "core")
    return jax.shard_map(
        shards,
        mesh=fine,
        in_specs=(
            P(mp, CTX),
            P(mp, CTX),
            P(mp, CTX),
            P(None, mp, None),
            P(mp + CTX, None),
            P(mp + CTX),
            P(CTX, mp),
        ),
        out_specs=P(mp, CTX),
        check_vma=False,
    )
```

time: 571 us -> 164 us (0.29); the launches traced: 562 us -> 162 us
  waiting for transfers between devices: 436 us -> 63.9 us
  matrix products: 65 us -> 0 us
  Pallas kernels: 0 us -> 35.9 us
  other arithmetic: 13.7 us -> 1.91 us
  starting transfers between devices: 22.9 us -> 32.7 us
    all_gather x2 -> x1, waiting for transfers between devices: 417 us -> 0.01 us  [shards(): weight = lax.all_gather(weight_run, ('y', 'x'), axis=0, tiled=True)]
    dot_general x19 -> x0, matrix products: 65 us -> none  [the longest x12 44.7 us: matmul_high(): return jnp.matmul(left, right, precision=HIGHEST_PREC)]
    ppermute x1 -> x7, waiting for transfers between devices: 0.01 us -> 60.5 us  [the longest x6 56.4 us: turned(): lax.ppermute(value, axis, [(source, (source + steps) % count) for source...]
    pallas_call x0 -> x5, Pallas kernels: none -> 35.9 us  [the longest x1 10.6 us: short_filters(): pl.pallas_call(short_kernel, in_specs=[pl.BlockSpec(memory_space=pltpu.SM...]
    all_to_all x2, waiting for transfers between devices: 17.7 us -> 3.46 us  [the longest x1 3.46 us: shards(): lax.all_to_all(product.reshape(ctx, chans, cols), CTX, split_axis=0, conc...]
    convert_element_type x5 -> x0, other arithmetic: 13.1 us -> none  [the longest x1 6.2 us: shards(): product = (k_feat * v_feat).astype(jnp.bfloat16)]
    unnamed x57 -> x43, local copies, waits for them, and re-layouts: 2.69 us -> 13.5 us
    ppermute x1 -> x7, starting transfers between devices: 3.83 us -> 12.4 us  [the longest x6 10.5 us: turned(): lax.ppermute(value, axis, [(source, (source + steps) % count) for source...]
  transfers between devices with their start and end apart: 5 -> 10, of which waited for: 4 -> 8; matrix products, arithmetic and copies ran while one was open for 5% -> 1% of each run, Pallas kernels for 0% -> 17%
where the time goes in v1:
time: 164 us; the launch traced here: 162 us
  waiting for transfers between devices  63.9 us (39%)
  Pallas kernels  35.9 us (22%)
  starting transfers between devices  32.7 us (20%)
  between operations  13.6 us (8%)
  local copies, waits for them, and re-layouts  13.5 us (8%)
  other arithmetic  1.91 us (1%)
    ppermute x6, waiting for transfers between devices, turned(): lax.ppermute(value, axis, [(source, (source + steps) % count) for source...  56.4 us
    unnamed x43, local copies, waits for them, and re-layouts  13.5 us
    all_to_all x1, starting transfers between devices, shards(): lax.all_to_all(mixed.reshape(2 * ctx, chans, cols), CTX + ('zh',), split_...  10.7 us
    pallas_call x1, Pallas kernels, short_filters(): pl.pallas_call(short_kernel, in_specs=[pl.BlockSpec(memory_space=pltpu.SM...  10.6 us
    ppermute x6, starting transfers between devices, turned(): lax.ppermute(value, axis, [(source, (source + steps) % count) for source...  10.5 us
    pallas_call x1, Pallas kernels, long_mix(): pl.pallas_call(conv_kernel, in_specs=[pl.BlockSpec(memory_space=pltpu.SME...  10.4 us
    all_to_all x1, starting transfers between devices, shards(): lax.all_to_all(product.reshape(ctx, chans, cols), CTX, split_axis=0, conc...  9.53 us
    pallas_call x1, Pallas kernels, project(): pl.pallas_call(project_kernel, grid=(width // block,), in_specs=[pl.Block...  7.85 us
  transfers between devices with their start and end apart: 10, of which 8 were waited for; matrix products, arithmetic and copies ran while one was open for 1% of the time, Pallas kernels for 17%

profile of v1, /device:TPU:32, one launch (start us, length us, event | category | flops | bytes accessed | tf_op | source)
XLA Modules:
  0.0 161.5 jit_solution(6377139481243538997)
XLA Ops:
  6.6 0.0 copy-start.8
  6.6 0.0 copy-start.17
  6.6 0.0 copy-start.18
  6.6 0.0 copy-start.4
  6.6 0.0 all-gather.2.cloned.1.call-start
  6.6 2.0 %collective-permute-start.4 = (bf16[64,1024]{1,0:T(8,128)(2,1)}, bf16[64,1024]{1,0:T(8,128)(2,1)S(1)}, u32[]{:S(2)}, u32[]{:S(2)}) collective-permute-start(bf16[64,1024]{1,0:T(8,128)(2,1)} %param.21), channel_id=1, source_target_pairs={{0,4},{4,8},{8,12},{12,0},{1,5},{5,9},{9,13},{13,1},{2,6},{6,10},{... | collective-permute-start | bytes 393224 | tf_op jit(solution)/shard_map/ppermute | solution.py:315
  8.6 2.3 %collective-permute-start.5 = (bf16[64,1024]{1,0:T(8,128)(2,1)}, bf16[64,1024]{1,0:T(8,128)(2,1)S(1)}, u32[]{:S(2)}, u32[]{:S(2)}) collective-permute-start(bf16[64,1024]{1,0:T(8,128)(2,1)} %param.21), channel_id=1, source_target_pairs={{0,8},{4,12},{8,0},{12,4},{1,9},{5,13},{9,1},{13,5},{2,10},{6,14},... | collective-permute-start | bytes 393224 | tf_op jit(solution)/shard_map/ppermute | solution.py:315
  10.9 1.1 collective-permute-start.6
  12.0 6.5 %collective-permute-done.4 = bf16[64,1024]{1,0:T(8,128)(2,1)S(1)} collective-permute-done((bf16[64,1024]{1,0:T(8,128)(2,1)}, bf16[64,1024]{1,0:T(8,128)(2,1)S(1)}, u32[]{:S(2)}, u32[]{:S(2)}) %collective-permute-start.4) | collective-permute-done | bytes 131104 | tf_op jit(solution)/shard_map/ppermute | solution.py:315
  18.5 1.7 %collective-permute-done.5 = bf16[64,1024]{1,0:T(8,128)(2,1)S(1)} collective-permute-done((bf16[64,1024]{1,0:T(8,128)(2,1)}, bf16[64,1024]{1,0:T(8,128)(2,1)S(1)}, u32[]{:S(2)}, u32[]{:S(2)}) %collective-permute-start.5) | collective-permute-done | bytes 131104 | tf_op jit(solution)/shard_map/ppermute | solution.py:315
  20.1 2.0 %collective-permute-done.6 = bf16[64,1024]{1,0:T(8,128)(2,1)S(1)} collective-permute-done((bf16[64,1024]{1,0:T(8,128)(2,1)}, bf16[64,1024]{1,0:T(8,128)(2,1)S(1)}, u32[]{:S(2)}, u32[]{:S(2)}) %collective-permute-start.6) | collective-permute-done | bytes 131104 | tf_op jit(solution)/shard_map/ppermute | solution.py:315
  22.2 1.7 %pad_maximum_fusion.1 = bf16[256,1024]{1,0:T(8,128)(2,1)} fusion(bf16[64,1024]{1,0:T(8,128)(2,1)S(1)} %collective-permute-done.6, bf16[64,1024]{1,0:T(8,128)(2,1)S(1)} %collective-permute-done.5, bf16[64,1024]{1,0:T(8,128)(2,1)S(1)} %collective-permute-done.4, bf16[64,1024]{1,0:T(8,128)(2,1)} %param.21), kind=kLoop, calls=%fused_computation.1 | loop fusion | flops 2097152 | bytes 1048576 | tf_op jit(solution)/shard_map/concatenate | solution.py:327
  23.9 0.0 all-gather.2.cloned.1.call-update
  23.9 2.1 %tails.1 = bf16[3,16,1024]{2,1,0:T(8,128)(2,1)} custom-call(bf16[1024,256]{1,0:T(8,128)(2,1)} %q_ref.3, bf16[1024,256]{1,0:T(8,128)(2,1)} %k_ref.3, bf16[1024,256]{1,0:T(8,128)(2,1)} %v_ref.3), custom_call_target="tpu_custom_call" | custom-call | tf_op jit(solution)/shard_map/tails/pallas_call | solution.py:64
  26.0 1.9 %collective-permute-start = (bf16[3,16,1024]{2,1,0:T(8,128)(2,1)}, bf16[3,16,1024]{2,1,0:T(8,128)(2,1)S(1)}, u32[]{:S(2)}, u32[]{:S(2)}) collective-permute-start(bf16[3,16,1024]{2,1,0:T(8,128)(2,1)} %tails.1), channel_id=1, source_target_pairs={{0,4},{4,8},{8,12},{12,16},{16,20},{20,24},{24,28},{28,32},{32,36}... | collective-permute-start | bytes 294920 | tf_op jit(solution)/shard_map/ppermute | solution.py:325
  27.9 0.8 copy.16.taps_ref
  28.7 4.1 %collective-permute-done.rim_ref = bf16[3,16,1024]{2,1,0:T(8,128)(2,1)S(1)} collective-permute-done((bf16[3,16,1024]{2,1,0:T(8,128)(2,1)}, bf16[3,16,1024]{2,1,0:T(8,128)(2,1)S(1)}, u32[]{:S(2)}, u32[]{:S(2)}) %collective-permute-start) | collective-permute-done | bytes 98336 | tf_op jit(solution)/shard_map/ppermute | solution.py:325
  32.8 1.0 copy-done
  33.9 1.0 copy-done.1
  34.9 1.0 copy-done.2
  35.9 10.6 %short_filters.1 = (bf16[1024,256]{1,0:T(8,128)(2,1)S(1)}, bf16[1024,256]{1,0:T(8,128)(2,1)}) custom-call(f32[3,64,7]{2,1,0:T(8,128)S(1)} %copy.16.taps_ref, bf16[1024,256]{1,0:T(8,128)(2,1)S(1)} %copy-done, bf16[1024,256]{1,0:T(8,128)(2,1)S(1)} %copy-done.1, bf16[1024,256]{1,0:T(8,128)(2,1)S(1)} %copy-done.2, ...), custom_call_target="tpu_custom_call" | custom-call | flops 11010048 | bytes 2621440 | tf_op jit(solution)/shard_map/short_filters/pallas_call | solution.py:111
  46.6 9.5 %all-to-all-start = ((bf16[64,16,256]{2,1,0:T(8,128)(2,1)}), bf16[64,16,256]{2,1,0:T(8,128)(2,1)S(1)}, u32[]{:S(2)}, u32[]{:S(2)}) async-start(bf16[64,16,256]{2,1,0:T(8,128)(2,1)} %bitcast.3), calls=%async_computation | async-start | bytes 1048576 | tf_op jit(solution)/shard_map/all_to_all | solution.py:333
  56.1 0.0 copy-start.3
  56.1 1.2 copy-done.3
  57.3 1.0 copy-done.5
  58.4 1.0 copy-done.7
  59.4 0.8 copy-done.9
  60.3 0.8 copy-done.11
  61.1 0.8 copy-done.13
  61.9 0.8 copy-done.15
  62.6 4.9 %filter_spectrum.1.spec_ref = f32[1024,512]{1,0:T(8,128)S(1)} custom-call(f32[16,16384]{1,0:T(8,128)S(1)} %copy-done.3, bf16[128,64]{1,0:T(8,128)(2,1)S(1)} %copy-done.13, bf16[128,64]{1,0:T(8,128)(2,1)S(1)} %copy-done.15, f32[64,256]{1,0:T(8,128)S(1)} %copy-done.9, f32[64,256]{1,0:T(8,128)S(1)} %copy-done.11, bf16[512,512]{1,0:T(8,128)(2,1)S(1)} %copy-done.5, ...), custom_call_target="tpu_custom_call" | custom-call | flops 1610612736 | bytes 5242880 | tf_op jit(solution)/shard_map/filter_spectrum/pallas_call | solution.py:166
  67.5 0.0 copy-start.19
  67.5 1.4 copy-done.19
  68.9 3.5 %all-to-all-done.u_ref = bf16[64,16,256]{2,1,0:T(8,128)(2,1)S(1)} async-done(((bf16[64,16,256]{2,1,0:T(8,128)(2,1)}), bf16[64,16,256]{2,1,0:T(8,128)(2,1)S(1)}, u32[]{:S(2)}, u32[]{:S(2)}) %all-to-all-start) | async-done | bytes 524320 | tf_op jit(solution)/shard_map/all_to_all | solution.py:333
  72.3 0.0 copy-done.14
  72.4 1.7 %copy-done.20 = f32[1024,512]{1,0:T(8,128)S(1)} copy-done((f32[1024,512]{1,0:T(8,128)S(1)}, f32[1024,512]{1,0:T(8,128)}, u32[]{:S(2)}) %copy-start.20) | copy-done | bytes 2097176
  74.1 10.4 %long_conv.1 = bf16[64,2,16,256]{3,2,1,0:T(8,128)(2,1)} custom-call(f32[16]{0:T(128)S(1)} %copy-done.4, bf16[64,16,256]{2,1,0:T(8,128)(2,1)S(1)} %all-to-all-done.u_ref, f32[1024,512]{1,0:T(8,128)S(1)} %copy-done.20, bf16[128,64]{1,0:T(8,128)(2,1)S(1)} %copy-done.14, bf16[128,64]{1,0:T(8,128)(2,1)S(1)} %copy-done.16, bf16[64,128]{1,0:T(8,128)(2,1)S(1)} %copy-done.17, ...), custom_call_target="tpu_custom_call" | custom-call | flops 3221225472 | bytes 6291456 | tf_op jit(solution)/shard_map/long_conv/pallas_call | solution.py:247
  84.5 10.7 %all-to-all-start.1 = ((bf16[128,16,256]{2,1,0:T(8,128)(2,1)}), bf16[128,16,256]{2,1,0:T(8,128)(2,1)S(1)}, u32[]{:S(2)}, u32[]{:S(2)}) async-start(bf16[128,16,256]{2,1,0:T(8,128)(2,1)} %bitcast.4), calls=%async_computation.1 | async-start | bytes 2097152 | tf_op jit(solution)/shard_map/all_to_all | solution.py:338
  95.2 4.6 %collective-permute-start.2 = (bf16[1024,256]{1,0:T(8,128)(2,1)S(1)}, bf16[1024,256]{1,0:T(8,128)(2,1)S(1)}, u32[]{:S(2)}, u32[]{:S(2)}) collective-permute-start(bf16[1024,256]{1,0:T(8,128)(2,1)S(1)} %get-tuple-element.8), channel_id=1, source_target_pairs={{0,2},{2,0},{1,3},{3,1},{4,6},{6,4},{5,7},{7,5},{8,10},{10,8},{9,1... | collective-permute-start | bytes 1572872 | tf_op jit(solution)/shard_map/ppermute | solution.py:315
  99.8 42.5 %collective-permute-done.2 = bf16[1024,256]{1,0:T(8,128)(2,1)S(1)} collective-permute-done((bf16[1024,256]{1,0:T(8,128)(2,1)S(1)}, bf16[1024,256]{1,0:T(8,128)(2,1)S(1)}, u32[]{:S(2)}, u32[]{:S(2)}) %collective-permute-start.2) | collective-permute-done | bytes 524320 | tf_op jit(solution)/shard_map/ppermute | solution.py:315
  142.3 0.1 pad_maximum_fusion.q_own
  142.4 0.1 collective-permute-start.3
  142.5 0.0 all-to-all-done.1
  142.5 0.5 collective-permute-start.1
  143.0 0.1 pad_add_fusion.place_ref
  143.1 2.5 %collective-permute-done.3.q_other = bf16[2,1024,256]{2,1,0:T(8,128)(2,1)S(1)} collective-permute-done((bf16[2,1024,256]{2,1,0:T(8,128)(2,1)S(1)}, bf16[2,1024,256]{2,1,0:T(8,128)(2,1)S(1)}, u32[]{:S(2)}, u32[]{:S(2)}) %collective-permute-start.3) | collective-permute-done | bytes 1048608 | tf_op jit(solution)/shard_map/ppermute | solution.py:315
  145.6 1.2 collective-permute-done.1.z_other
  146.8 7.8 %project.1 = bf16[1024,256]{1,0:T(8,128)(2,1)} custom-call(s32[3]{0:T(128)S(1)} %pad_add_fusion.place_ref, bf16[64,2,16,256]{3,2,1,0:T(8,128)(2,1)S(1)} %bitcast.9, bf16[64,2,16,256]{3,2,1,0:T(8,128)(2,1)} %collective-permute-done.1.z_other, bf16[2,1024,256]{2,1,0:T(8,128)(2,1)S(1)} %pad_maximum_fusion.q_own, ...), custom_call_target="tpu_custom_call" | custom-call | flops 2147483648 | bytes 10485760 | tf_op jit(solution)/shard_map/project/pallas_call | solution.py:293
  (24 shorter events, 0.0 us)
Async XLA Ops:
  6.5 65.8 %copy-start.14 = (bf16[128,64]{1,0:T(8,128)(2,1)S(1)}, bf16[128,64]{1,0:T(8,128)(2,1)}, u32[]{:S(2)}) copy-start(bf16[128,64]{1,0:T(8,128)(2,1)} %constant.27.clone.refs_1_.f_hi) | copy-start | bytes 49156
  6.5 65.8 %copy-start.16 = (bf16[128,64]{1,0:T(8,128)(2,1)S(1)}, bf16[128,64]{1,0:T(8,128)(2,1)}, u32[]{:S(2)}) copy-start(bf16[128,64]{1,0:T(8,128)(2,1)} %constant.28.clone.refs_2_.f_lo) | copy-start | bytes 49156
  6.5 65.8 %copy-start.10 = (f32[64,256]{1,0:T(8,128)S(1)}, f32[64,256]{1,0:T(8,128)}, u32[]{:S(2)}) copy-start(f32[64,256]{1,0:T(8,128)} %constant.29.clone.refs_3_.cos_ref) | copy-start | bytes 196612
  6.5 65.8 %copy-start.12 = (f32[64,256]{1,0:T(8,128)S(1)}, f32[64,256]{1,0:T(8,128)}, u32[]{:S(2)}) copy-start(f32[64,256]{1,0:T(8,128)} %constant.30.clone.refs_4_.sin_ref) | copy-start | bytes 196612
  6.5 65.8 %copy-start.6 = (bf16[512,512]{1,0:T(8,128)(2,1)S(1)}, bf16[512,512]{1,0:T(8,128)(2,1)}, u32[]{:S(2)}) copy-start(bf16[512,512]{1,0:T(8,128)(2,1)} %constant.31.clone.refs_5_.s_hi) | copy-start | bytes 1572868
  6.6 65.8 %copy-start.8 = (bf16[512,512]{1,0:T(8,128)(2,1)S(1)}, bf16[512,512]{1,0:T(8,128)(2,1)}, u32[]{:S(2)}) copy-start(bf16[512,512]{1,0:T(8,128)(2,1)} %constant.32.clone.refs_6_.s_lo) | copy-start | bytes 1572868
  6.6 65.8 %copy-start.17 = (bf16[64,128]{1,0:T(8,128)(2,1)S(1)}, bf16[64,128]{1,0:T(8,128)(2,1)}, u32[]{:S(2)}) copy-start(bf16[64,128]{1,0:T(8,128)(2,1)} %constant.33.clone.l_hi) | copy-start | bytes 49156
  6.6 65.8 %copy-start.18 = (bf16[64,128]{1,0:T(8,128)(2,1)S(1)}, bf16[64,128]{1,0:T(8,128)(2,1)}, u32[]{:S(2)}) copy-start(bf16[64,128]{1,0:T(8,128)(2,1)} %constant.34.clone.l_lo) | copy-start | bytes 49156
  6.6 65.8 %copy-start.4 = (f32[16]{0:T(128)S(1)}, f32[16]{0:T(128)}, u32[]{:S(2)}) copy-start(f32[16]{0:T(128)} %skip_ref.1) | copy-start | bytes 196
  6.6 140.2 %all-gather.2.cloned.1.call-start = ((), (), s32[]{:S(2)}) async-start(), calls=%async_computation.2 | async-start | bytes 8912896 | tf_op jit(solution)/shard_map/all_gather | solution.py:328
  6.6 11.8 %collective-permute-start.4 = (bf16[64,1024]{1,0:T(8,128)(2,1)}, bf16[64,1024]{1,0:T(8,128)(2,1)S(1)}, u32[]{:S(2)}, u32[]{:S(2)}) collective-permute-start(bf16[64,1024]{1,0:T(8,128)(2,1)} %param.21), channel_id=1, source_target_pairs={{0,4},{4,8},{8,12},{12,0},{1,5},{5,9},{9,13},{13,1},{2,6},{6,10},{... | collective-permute-start | bytes 393224 | tf_op jit(solution)/shard_map/ppermute | solution.py:315
  8.6 11.5 %collective-permute-start.5 = (bf16[64,1024]{1,0:T(8,128)(2,1)}, bf16[64,1024]{1,0:T(8,128)(2,1)S(1)}, u32[]{:S(2)}, u32[]{:S(2)}) collective-permute-start(bf16[64,1024]{1,0:T(8,128)(2,1)} %param.21), channel_id=1, source_target_pairs={{0,8},{4,12},{8,0},{12,4},{1,9},{5,13},{9,1},{13,5},{2,10},{6,14},... | collective-permute-start | bytes 393224 | tf_op jit(solution)/shard_map/ppermute | solution.py:315
  10.9 11.2 %collective-permute-start.6 = (bf16[64,1024]{1,0:T(8,128)(2,1)}, bf16[64,1024]{1,0:T(8,128)(2,1)S(1)}, u32[]{:S(2)}, u32[]{:S(2)}) collective-permute-start(bf16[64,1024]{1,0:T(8,128)(2,1)} %param.21), channel_id=1, source_target_pairs={{0,12},{4,0},{8,4},{12,8},{1,13},{5,1},{9,5},{13,9},{2,14},{6,2},{... | collective-permute-start | bytes 393224 | tf_op jit(solution)/shard_map/ppermute | solution.py:315
  26.0 6.8 %collective-permute-start = (bf16[3,16,1024]{2,1,0:T(8,128)(2,1)}, bf16[3,16,1024]{2,1,0:T(8,128)(2,1)S(1)}, u32[]{:S(2)}, u32[]{:S(2)}) collective-permute-start(bf16[3,16,1024]{2,1,0:T(8,128)(2,1)} %tails.1), channel_id=1, source_target_pairs={{0,4},{4,8},{8,12},{12,16},{16,20},{20,24},{24,28},{28,32},{32,36}... | collective-permute-start | bytes 294920 | tf_op jit(solution)/shard_map/ppermute | solution.py:325
  32.8 1.0 copy-start
  33.9 1.0 copy-start.1
  34.9 1.0 copy-start.2
  46.6 25.8 %all-to-all-start = ((bf16[64,16,256]{2,1,0:T(8,128)(2,1)}), bf16[64,16,256]{2,1,0:T(8,128)(2,1)S(1)}, u32[]{:S(2)}, u32[]{:S(2)}) async-start(bf16[64,16,256]{2,1,0:T(8,128)(2,1)} %bitcast.3), calls=%async_computation | async-start | bytes 1048576 | tf_op jit(solution)/shard_map/all_to_all | solution.py:333
  56.1 1.2 copy-start.3
  57.3 1.0 copy-start.5
  58.4 1.0 copy-start.7
  59.4 0.8 copy-start.9
  60.3 0.8 copy-start.11
  61.1 0.8 copy-start.13
  61.9 0.8 copy-start.15
  67.5 1.4 copy-start.19
  72.4 1.7 %copy-start.20 = (f32[1024,512]{1,0:T(8,128)S(1)}, f32[1024,512]{1,0:T(8,128)}, u32[]{:S(2)}) copy-start(f32[1024,512]{1,0:T(8,128)} %copy-done.19) | copy-start | bytes 6291460
  84.5 58.0 %all-to-all-start.1 = ((bf16[128,16,256]{2,1,0:T(8,128)(2,1)}), bf16[128,16,256]{2,1,0:T(8,128)(2,1)S(1)}, u32[]{:S(2)}, u32[]{:S(2)}) async-start(bf16[128,16,256]{2,1,0:T(8,128)(2,1)} %bitcast.4), calls=%async_computation.1 | async-start | bytes 2097152 | tf_op jit(solution)/shard_map/all_to_all | solution.py:338
  95.2 47.1 %collective-permute-start.2 = (bf16[1024,256]{1,0:T(8,128)(2,1)S(1)}, bf16[1024,256]{1,0:T(8,128)(2,1)S(1)}, u32[]{:S(2)}, u32[]{:S(2)}) collective-permute-start(bf16[1024,256]{1,0:T(8,128)(2,1)S(1)} %get-tuple-element.8), channel_id=1, source_target_pairs={{0,2},{2,0},{1,3},{3,1},{4,6},{6,4},{5,7},{7,5},{8,10},{10,8},{9,1... | collective-permute-start | bytes 1572872 | tf_op jit(solution)/shard_map/ppermute | solution.py:315
  142.4 3.1 %collective-permute-start.3 = (bf16[2,1024,256]{2,1,0:T(8,128)(2,1)S(1)}, bf16[2,1024,256]{2,1,0:T(8,128)(2,1)S(1)}, u32[]{:S(2)}, u32[]{:S(2)}) collective-permute-start(bf16[2,1024,256]{2,1,0:T(8,128)(2,1)S(1)} %pad_maximum_fusion.q_own), channel_id=1, source_target_pairs={{0,1},{1,0},{2,3},{3,2},{4,5},{5,4},{6,7},{7,6},{8,9},{9,8},{10,11... | collective-permute-start | bytes 3145736 | tf_op jit(solution)/shard_map/ppermute | solution.py:315
  142.5 4.3 %collective-permute-start.1 = (bf16[64,2,16,256]{3,2,1,0:T(8,128)(2,1)S(1)}, bf16[64,2,16,256]{3,2,1,0:T(8,128)(2,1)}, u32[]{:S(2)}, u32[]{:S(2)}) collective-permute-start(bf16[64,2,16,256]{3,2,1,0:T(8,128)(2,1)S(1)} %bitcast.8), channel_id=1, source_target_pairs={{0,1},{1,0},{2,3},{3,2},{4,5},{5,4},{6,7},{7,6},{8,9},{9,8},{10,11... | collective-permute-start | bytes 3145736 | tf_op jit(solution)/shard_map/ppermute | solution.py:315
Sparse Core Ops, SparseCore 0:
  24.1 84.4 all-gather.1

commit v2 on v1

v2 whole, which is shorter than its diff:
```python
import math

import jax
import jax.numpy as jnp
import numpy as np
from jax import lax
from jax.experimental import pallas as pl
from jax.experimental.pallas import tpu as pltpu
from jax.sharding import Mesh, PartitionSpec as P

BF16 = jnp.bfloat16
F32 = jnp.float32
CTX = ("y", "x", "zl")
VMEM_LIMIT = 60 * 1024 * 1024


def hi_lo(table):
    hi = table.astype(np.float32).astype(jnp.bfloat16)
    lo = (table - hi.astype(np.float64)).astype(np.float32).astype(jnp.bfloat16)
    return hi, lo


def dft_tables(outer, inner):
    length = outer * inner
    freq = np.arange(outer)[:, None] + 0.25
    angle = 2.0 * np.pi * freq * np.arange(outer)[None, :] / outer
    first = np.concatenate([np.cos(angle), -np.sin(angle)], axis=0)
    spin = 2.0 * np.pi * freq * np.arange(inner)[None, :] / length
    steps = np.outer(np.arange(inner), np.arange(inner)) % inner
    turn = 2.0 * np.pi * steps / inner
    cos, sin = np.cos(turn), np.sin(turn)
    second = np.block([[cos, -sin], [sin, cos]])
    return {
        "first": hi_lo(first),
        "last": hi_lo(first.T.copy()),
        "spin": (np.cos(spin).astype(np.float32), np.sin(spin).astype(np.float32)),
        "second": hi_lo(second),
    }


def dot(left, right):
    return jnp.dot(left, right, preferred_element_type=F32)


def split_bf16(value):
    hi = value.astype(BF16)
    return hi, (value - hi.astype(F32)).astype(BF16)


def lane_ids(rows):
    return lax.broadcasted_iota(jnp.int32, (rows, 128), 1)


def filter_tiles(weights, before, tiles, lane):
    turned = {}
    for tap in range(1, len(weights)):
        for index, tile in enumerate(tiles):
            turned[index, tap] = pltpu.roll(tile, tap, 1)
        turned[-1, tap] = 0.0 if before is None else pltpu.roll(before, tap, 1)
    sums = []
    for index, tile in enumerate(tiles):
        total = weights[0] * tile
        for tap in range(1, len(weights)):
            total += weights[tap] * jnp.where(lane >= tap, turned[index, tap], turned[index - 1, tap])
        sums.append(total)
    return sums


def short_kernel(taps_ref, q_ref, k_ref, v_ref, out_ref):
    rows, cols = q_ref.shape
    taps = taps_ref.shape[2]
    size = out_ref.shape[1]
    first = pl.program_id(0) * (rows // size)
    lane = lane_ids(size)
    for g in range(rows // size):
        at = pl.ds(g * size, size)
        feats, edges = [], []
        for index, ref in ((1, k_ref), (2, v_ref)):
            wide = ref[at, :].astype(F32)
            tiles = [wide[:, i * 128 : i * 128 + 128] for i in range(cols // 128)]
            weights = [taps_ref[index, first + g, tap] for tap in range(taps)]
            feats.append(filter_tiles(weights, None, tiles, lane))
            shift = 8 if index == 1 else 24
            edges += [pltpu.roll(tiles[-1], shift, 1), pltpu.roll(tiles[0], shift, 1)]
        for i in range(cols // 128):
            out_ref[g, :, i * 128 : i * 128 + 128] = (feats[0][i] * feats[1][i]).astype(BF16)
        out_ref[g, :, cols : 2 * cols] = q_ref[at, :]
        edge = jnp.where(lane < 16, jnp.where(lane < 8, edges[0], edges[1]), jnp.where(lane < 24, edges[2], edges[3]))
        out_ref[g, :, 2 * cols :] = edge.astype(BF16)


def short_filters(taps, query, key, value, ctx, blocks=4):
    rows, cols = query.shape
    size = rows // ctx
    spec = pl.BlockSpec((rows // blocks, cols), lambda i: (i, 0))
    return pl.pallas_call(
        short_kernel,
        grid=(blocks,),
        in_specs=[pl.BlockSpec(memory_space=pltpu.SMEM)] + [spec] * 3,
        out_specs=pl.BlockSpec((ctx // blocks, size, 2 * cols + 128), lambda i: (i, 0, 0)),
        out_shape=jax.ShapeDtypeStruct((ctx, size, 2 * cols + 128), BF16),
        compiler_params=pltpu.CompilerParams(vmem_limit_bytes=VMEM_LIMIT),
        cost_estimate=pl.CostEstimate(flops=2 * 14 * rows * cols, bytes_accessed=10 * rows * cols, transcendentals=0),
        name="short_filters",
    )(taps, query, key, value)


def second_dft(hi, lo, second_hi, second_lo):
    return dot(hi, second_hi[...]) + dot(lo, second_hi[...]) + dot(hi, second_lo[...])


def channel_rows(ref, c, outer, chans):
    halves = ref.shape[0] // (outer * chans)
    parts = [ref[pl.ds(half * outer * chans + c, outer, stride=chans), :] for half in range(halves)]
    return jnp.concatenate(parts, axis=1)


def filter_kernel(scale, filt_ref, f_hi, f_lo, cos_ref, sin_ref, s_hi, s_lo, out_ref, rows_ref, g_hi, g_lo):
    chans, _ = filt_ref.shape
    outer, inner = cos_ref.shape
    for half in range(inner // 128):
        for a in range(outer):
            start = a * inner + half * 128
            at = (half * outer + a) * chans
            rows_ref[at : at + chans, :] = filt_ref[:, start : start + 128]

    for c in range(chans):
        hi, lo = split_bf16(channel_rows(rows_ref, c, outer, chans) * scale)
        mixed = dot(f_hi[...], hi) + dot(f_hi[...], lo) + dot(f_lo[...], hi)
        re, im = mixed[:outer], mixed[outer:]
        at = pl.ds(c * outer, outer)
        g_hi[at, :inner], g_lo[at, :inner] = split_bf16(re * cos_ref[...] + im * sin_ref[...])
        g_hi[at, inner:], g_lo[at, inner:] = split_bf16(im * cos_ref[...] - re * sin_ref[...])

    for i in range(chans * outer // 256):
        at = pl.ds(i * 256, 256)
        out_ref[at, :] = second_dft(g_hi[at, :], g_lo[at, :], s_hi, s_lo)


def filter_spectrum(long_filter, tables, outer, inner):
    chans = long_filter.shape[0]
    rows = chans * outer
    whole = lambda shape: pl.BlockSpec(shape, lambda i: (0,) * len(shape))
    operands = (long_filter, *tables["first"], *tables["spin"], *tables["second"])
    return pl.pallas_call(
        lambda *refs: filter_kernel(1.0 / (outer * inner), *refs),
        grid=(1,),
        in_specs=[whole(operand.shape) for operand in operands],
        out_specs=whole((rows, 2 * inner)),
        out_shape=jax.ShapeDtypeStruct((rows, 2 * inner), F32),
        scratch_shapes=[
            pltpu.VMEM((rows * inner // 128, 128), F32),
            pltpu.VMEM((rows, 2 * inner), BF16),
            pltpu.VMEM((rows, 2 * inner), BF16),
        ],
        compiler_params=pltpu.CompilerParams(vmem_limit_bytes=VMEM_LIMIT),
        cost_estimate=pl.CostEstimate(flops=3 * 2 * rows * 4 * inner * inner, bytes_accessed=5 * 2**20, transcendentals=0),
        name="filter_spectrum",
    )(*operands)


def conv_kernel(
    skip_ref, taps_ref, in_ref, f_hi, f_lo, l_hi, l_lo, cos_ref, sin_ref, spec_hbm, s_hi_hbm, s_lo_hbm,
    out_ref, rows_ref, z_ref, q_ref, edge_ref, g_hi, g_lo, spec_ref, s_hi, s_lo, sems,
):
    fetches = [
        pltpu.make_async_copy(source, target, sems.at[index])
        for index, (source, target) in enumerate(((spec_hbm, spec_ref), (s_hi_hbm, s_hi), (s_lo_hbm, s_lo)))
    ]
    for fetch in fetches:
        fetch.start()
    outer, chans, width = in_ref.shape
    inner = (width - 128) // 2
    halves = inner // 128
    rows = outer * chans
    taps = taps_ref.shape[1]
    blocks = 8
    step = rows // blocks
    units = outer // blocks
    lane = lane_ids(step)

    edge_ref[:chans, :] = jnp.zeros((chans, 128), F32)
    q_ref[(halves - 1) * (rows + chans) : (halves - 1) * (rows + chans) + chans, :] = jnp.zeros((chans, 128), F32)
    edge_ref[chans:, :] = in_ref[:, :, 2 * inner :].reshape(rows, 128).astype(F32)
    for half in range(halves):
        at = half * (rows + chans) + chans
        q_ref[at : at + rows, :] = (
            in_ref[:, :, inner + half * 128 : inner + half * 128 + 128].reshape(rows, 128).astype(F32)
        )

    weights = [jnp.where(lane < 16, taps_ref[1, tap], taps_ref[2, tap]) for tap in range(taps)]

    for i in range(blocks):
        at = i * step
        edge = jnp.where(jnp.bitwise_and(lane, 8) == 0, edge_ref[at : at + step, :], edge_ref[at + chans : at + chans + step, :])
        total = weights[0] * edge
        for tap in range(1, taps):
            total += weights[tap] * pltpu.roll(edge, tap, 1)
        first = (pltpu.roll(total, 120, 1) * pltpu.roll(total, 104, 1)).astype(BF16).astype(F32)
        sig = in_ref[i * units : (i + 1) * units, :, :inner].reshape(step, inner).astype(F32)
        rows_ref[at : at + step, :] = jnp.where(lane < taps - 1, first, sig[:, :128])
        for half in range(1, halves):
            rows_ref[half * rows + at : half * rows + at + step, :] = sig[:, half * 128 : half * 128 + 128]

    for c in range(chans):
        sig = channel_rows(rows_ref, c, outer, chans).astype(BF16)
        mixed = dot(f_hi[...], sig) + dot(f_lo[...], sig)
        re, im = mixed[:outer], mixed[outer:]
        at = pl.ds(c * outer, outer)
        g_hi[at, :inner], g_lo[at, :inner] = split_bf16(re * cos_ref[...] + im * sin_ref[...])
        g_hi[at, inner:], g_lo[at, inner:] = split_bf16(im * cos_ref[...] - re * sin_ref[...])

    for fetch in fetches:
        fetch.wait()

    for i in range(chans * outer // 256):
        at = pl.ds(i * 256, 256)
        sig = second_dft(g_hi[at, :], g_lo[at, :], s_hi, s_lo)
        sr, si = sig[:, :inner], sig[:, inner:]
        hr, hm = spec_ref[at, :inner], spec_ref[at, inner:]
        r_hi, r_lo = split_bf16(sr * hr - si * hm)
        i_hi, i_lo = split_bf16(-(sr * hm + si * hr))
        back = second_dft(
            jnp.concatenate([r_hi, i_hi], axis=1), jnp.concatenate([r_lo, i_lo], axis=1), s_hi, s_lo
        )
        back = back.reshape(256 // outer, outer, 2 * inner)
        re, im = back[:, :, :inner], back[:, :, inner:]
        cos, sin = cos_ref[...], sin_ref[...]
        r_hi, r_lo = split_bf16((re * cos + im * sin).reshape(256, inner))
        i_hi, i_lo = split_bf16((re * sin - im * cos).reshape(256, inner))
        for j in range(256 // outer):
            c = i * (256 // outer) + j
            part = slice(j * outer, (j + 1) * outer)
            hi = jnp.concatenate([r_hi[part], i_hi[part]], axis=0)
            lo = jnp.concatenate([r_lo[part], i_lo[part]], axis=0)
            conv = dot(l_hi[...], hi) + dot(l_hi[...], lo) + dot(l_lo[...], hi)
            mixed = conv + skip_ref[c] * channel_rows(rows_ref, c, outer, chans)
            for half in range(halves):
                z_ref[pl.ds(half * rows + c, outer, stride=chans), :] = mixed[:, half * 128 : (half + 1) * 128]

    q_taps = [taps_ref[0, tap] for tap in range(taps)]
    for i in range(blocks):
        at = i * step
        starts = [half * (rows + chans) + chans + at for half in range(halves)]
        tiles = [q_ref[start : start + step, :] for start in starts]
        start = (halves - 1) * (rows + chans) + at
        feats = filter_tiles(q_taps, q_ref[start : start + step, :], tiles, lane)
        for half in range(halves):
            mixed = z_ref[half * rows + at : half * rows + at + step, :].astype(BF16).astype(F32)
            result = (feats[half] * mixed).astype(BF16).reshape(units, chans, 128)
            for copy in range(out_ref.shape[1]):
                out_ref[i * units : (i + 1) * units, copy, :, half * 128 : (half + 1) * 128] = result


def long_mix(arrived, spectrum, skip_bias, taps, tables, copies):
    outer, chans, width = arrived.shape
    inner = (width - 128) // 2
    rows = outer * chans
    whole = lambda shape: pl.BlockSpec(shape, lambda i: (0,) * len(shape))
    scalars = pl.BlockSpec(memory_space=pltpu.SMEM)
    operands = (arrived, *tables["first"], *tables["last"], *tables["spin"])
    fetched = (spectrum, *tables["second"])
    return pl.pallas_call(
        conv_kernel,
        grid=(1,),
        in_specs=[scalars] * 2
        + [whole(operand.shape) for operand in operands]
        + [pl.BlockSpec(memory_space=pl.ANY)] * len(fetched),
        out_specs=whole((outer, copies, chans, inner)),
        out_shape=jax.ShapeDtypeStruct((outer, copies, chans, inner), BF16),
        scratch_shapes=[
            pltpu.VMEM((rows * inner // 128, 128), F32),
            pltpu.VMEM((rows * inner // 128, 128), F32),
            pltpu.VMEM(((rows + chans) * inner // 128, 128), F32),
            pltpu.VMEM((rows + chans, 128), F32),
            pltpu.VMEM((rows, 2 * inner), BF16),
            pltpu.VMEM((rows, 2 * inner), BF16),
            pltpu.VMEM((rows, 2 * inner), F32),
            pltpu.VMEM((2 * inner, 2 * inner), BF16),
            pltpu.VMEM((2 * inner, 2 * inner), BF16),
            pltpu.SemaphoreType.DMA((3,)),
        ],
        compiler_params=pltpu.CompilerParams(vmem_limit_bytes=VMEM_LIMIT),
        cost_estimate=pl.CostEstimate(flops=6 * 2 * rows * 4 * inner * inner, bytes_accessed=6 * 2**20, transcendentals=0),
        name="long_conv",
    )(skip_bias, taps, *operands, *fetched)


def project_kernel(last, place_ref, *refs):
    (z_ref, w_ref, sum_ref, out_ref, acc_ref) = refs if last else (refs[0], refs[1], None, refs[2], None)
    total_ref = acc_ref if last else out_ref
    _, _, chans, cols = z_ref.shape
    unit = 4 * chans
    step = pl.program_id(0)
    zl = place_ref[0]
    half = step // 2
    parts = []
    for x in range(2):
        for turn in range(4):
            start = (2 * (step % 2) + x) * 16 + 4 * jnp.bitwise_and(zl - turn, 3)
            parts.append(z_ref[pl.ds(start, 4), half].reshape(unit, cols))
    gated = jnp.concatenate(parts, axis=0)
    part = dot(gated.T, w_ref[...])

    @pl.when(step == 0)
    def _():
        total_ref[...] = part + sum_ref[...] if last else part

    @pl.when(step > 0)
    def _():
        total_ref[...] += part

    if last:
        @pl.when(step == pl.num_programs(0) - 1)
        def _():
            out_ref[...] = total_ref[...].T.astype(BF16)


def project(place, gated, weight, partial=None):
    depth, width = weight.shape
    cols = gated.shape[3]
    last = partial is not None
    block = depth // 8
    whole = lambda shape: pl.BlockSpec(shape, lambda i, place: (0,) * len(shape))
    in_specs = [whole(gated.shape), pl.BlockSpec((block, width), lambda i, place: (4 * (i // 2) + 2 * place[1] + i % 2, 0))]
    operands = [gated, weight]
    if last:
        in_specs.append(whole(partial.shape))
        operands.append(partial)
    return pl.pallas_call(
        lambda *refs: project_kernel(last, *refs),
        grid_spec=pltpu.PrefetchScalarGridSpec(
            num_scalar_prefetch=1,
            grid=(4,),
            in_specs=in_specs,
            out_specs=whole((width, cols) if last else (cols, width)),
            scratch_shapes=[pltpu.VMEM((cols, width), F32)] if last else [],
        ),
        out_shape=jax.ShapeDtypeStruct((width, cols), BF16) if last else jax.ShapeDtypeStruct((cols, width), F32),
        compiler_params=pltpu.CompilerParams(vmem_limit_bytes=VMEM_LIMIT),
        cost_estimate=pl.CostEstimate(flops=depth * width * cols, bytes_accessed=depth * width, transcendentals=0),
        name="project_last" if last else "project_first",
    )(place, *operands)


def turned(value, axis, steps):
    count = lax.axis_size(axis)
    return lax.ppermute(value, axis, [(source, (source + steps) % count) for source in range(count)])


def shards(query_proj, key_proj, value_proj, short_taps, long_filter, skip_bias, out_weight):
    rows, cols = query_proj.shape
    ctx = lax.axis_size(CTX)
    chans = long_filter.shape[0]
    tables = dft_tables(ctx, cols)

    pieces = [turned(out_weight, "zl", step) for step in (1, 2, 3)]
    ready = short_filters(short_taps, query_proj, key_proj, value_proj, ctx)
    ready, *pieces = lax.optimization_barrier((ready, *pieces))
    weight_run = jnp.concatenate([out_weight, *pieces], axis=0)
    weight = lax.all_gather(weight_run, ("y", "x"), axis=0, tiled=True)

    spectrum = filter_spectrum(long_filter, tables, ctx, cols)
    arrived = lax.all_to_all(ready, CTX, split_axis=0, concat_axis=0, tiled=True)
    own_taps = lax.dynamic_index_in_dim(short_taps, lax.axis_index(CTX), 1, keepdims=False)

    gated = long_mix(arrived, spectrum, skip_bias, own_taps, tables, 2)
    own = lax.all_to_all(
        gated.reshape(2 * ctx, chans, cols), CTX + ("zh",), split_axis=0, concat_axis=0, tiled=True
    ).reshape(ctx, 2, chans, cols)
    other = turned(own, "core", 1)

    zl, core = lax.axis_index("zl"), lax.axis_index("core")
    partial = project(jnp.stack([zl, core]).astype(jnp.int32), own, weight)
    return project(jnp.stack([zl, 1 - core]).astype(jnp.int32), other, weight, partial)


def solution(mesh):
    fine = Mesh(mesh.devices.reshape(4, 4, 4, 2, 2), ("y", "x", "zl", "zh", "core"))
    mp = ("zh", "core")
    return jax.shard_map(
        shards,
        mesh=fine,
        in_specs=(
            P(mp, CTX),
            P(mp, CTX),
            P(mp, CTX),
            P(None, mp, None),
            P(mp + CTX, None),
            P(mp + CTX),
            P(CTX, mp),
        ),
        out_specs=P(mp, CTX),
        check_vma=False,
    )
```

time: 164 us -> 141 us (0.86)
  blocking collectives: 0 us -> 39.5 us
  waiting for transfers between devices: 63.9 us -> 29.8 us
  starting transfers between devices: 32.7 us -> 14.9 us
  local copies, waits for them, and re-layouts: 13.5 us -> 4.65 us
    ppermute x6 -> x4, waiting for transfers between devices: 56.4 us -> 2.58 us  [turned(): lax.ppermute(value, axis, [(source, (source + steps) % count) for source...]
    all_to_all x0 -> x1, blocking collectives: none -> 39.5 us  [shards(): lax.all_to_all(gated.reshape(2 * ctx, chans, cols), CTX + ('zh',), split_...]
    all_to_all x2 -> x1, waiting for transfers between devices: 3.46 us -> 27.2 us  [shards(): lax.all_to_all(ready, CTX, split_axis=0, concat_axis=0, tiled=True)]
    all_to_all x2 -> x1, starting transfers between devices: 20.2 us -> 9.63 us  [shards(): lax.all_to_all(ready, CTX, split_axis=0, concat_axis=0, tiled=True)]
    unnamed x43 -> x11, local copies, waits for them, and re-layouts: 13.5 us -> 3.9 us
    ppermute x6 -> x4, starting transfers between devices: 10.5 us -> 5.3 us  [turned(): lax.ppermute(value, axis, [(source, (source + steps) % count) for source...]
    ppermute x1 -> x0, waiting for transfers between devices: 4.08 us -> none  [shards(): lax.ppermute(tails, CTX, [(source, source + 1) for source in range(ctx -...]
    ppermute x1 -> x0, starting transfers between devices: 1.91 us -> none  [shards(): lax.ppermute(tails, CTX, [(source, source + 1) for source in range(ctx -...]
  transfers between devices with their start and end apart: 10 -> 6, of which waited for: 8 -> 3; matrix products, arithmetic and copies ran while one was open for 1% -> 2% of each run, Pallas kernels for 17% -> 21%
where the time goes in v2:
time: 141 us; the launch traced here: 139 us
  blocking collectives  39.5 us (28%)
  Pallas kernels  35.2 us (25%)
  waiting for transfers between devices  29.8 us (21%)
  starting transfers between devices  14.9 us (11%)
  between operations  13.4 us (10%)
  local copies, waits for them, and re-layouts  4.65 us (3%)
  other arithmetic  1.57 us (1%)
    all_to_all x1, blocking collectives, shards(): lax.all_to_all(gated.reshape(2 * ctx, chans, cols), CTX + ('zh',), split_...  39.5 us
    all_to_all x1, waiting for transfers between devices, shards(): lax.all_to_all(ready, CTX, split_axis=0, concat_axis=0, tiled=True)  27.2 us
    pallas_call x2, Pallas kernels, project(): pl.pallas_call(lambda *refs: project_kernel(last, *refs), grid_spec=pltpu...  12.8 us
    pallas_call x1, Pallas kernels, long_mix(): pl.pallas_call(conv_kernel, grid=(1,), in_specs=[scalars] * 2 + [whole(op...  10.4 us
    all_to_all x1, starting transfers between devices, shards(): lax.all_to_all(ready, CTX, split_axis=0, concat_axis=0, tiled=True)  9.63 us
    pallas_call x1, Pallas kernels, short_filters(): pl.pallas_call(short_kernel, grid=(blocks,), in_specs=[pl.BlockSpec(memor...  6.14 us
    pallas_call x1, Pallas kernels, filter_spectrum(): pl.pallas_call(lambda *refs: filter_kernel(1.0 / (outer * inner), *refs),...  5.81 us
    ppermute x4, starting transfers between devices, turned(): lax.ppermute(value, axis, [(source, (source + steps) % count) for source...  5.3 us
  transfers between devices with their start and end apart: 6, of which 3 were waited for; matrix products, arithmetic and copies ran while one was open for 2% of the time, Pallas kernels for 21%

profile of v2, /device:TPU:32, one launch (start us, length us, event | category | flops | bytes accessed | tf_op | source)
XLA Modules:
  0.0 139.0 jit_solution(1293651299499813785)
XLA Ops:
  6.5 0.0 copy-start.3
  6.5 0.0 all-gather.2.cloned.1.call-start
  6.5 1.9 %collective-permute-start = (bf16[64,1024]{1,0:T(8,128)(2,1)}, bf16[64,1024]{1,0:T(8,128)(2,1)S(1)}, u32[]{:S(2)}, u32[]{:S(2)}) collective-permute-start(bf16[64,1024]{1,0:T(8,128)(2,1)} %param.21), channel_id=1, source_target_pairs={{0,4},{4,8},{8,12},{12,0},{1,5},{5,9},{9,13},{13,1},{2,6},{6,10},{... | collective-permute-start | bytes 393224 | tf_op jit(solution)/shard_map/ppermute | solution.py:348
  8.5 2.3 %collective-permute-start.1 = (bf16[64,1024]{1,0:T(8,128)(2,1)}, bf16[64,1024]{1,0:T(8,128)(2,1)S(1)}, u32[]{:S(2)}, u32[]{:S(2)}) collective-permute-start(bf16[64,1024]{1,0:T(8,128)(2,1)} %param.21), channel_id=1, source_target_pairs={{0,8},{4,12},{8,0},{12,4},{1,9},{5,13},{9,1},{13,5},{2,10},{6,14},... | collective-permute-start | bytes 393224 | tf_op jit(solution)/shard_map/ppermute | solution.py:348
  10.7 1.1 collective-permute-start.2
  11.8 1.5 %copy.17.taps_ref = f32[3,64,7]{2,1,0:T(8,128)} copy(f32[3,64,7]{1,2,0:T(8,128)} %param.18) | data formatting | bytes 10752 | tf_op args[3]
  13.3 6.1 %short_filters.1 = bf16[64,16,640]{2,1,0:T(8,128)(2,1)} custom-call(f32[3,64,7]{2,1,0:T(8,128)} %copy.17.taps_ref, bf16[1024,256]{1,0:T(8,128)(2,1)} %q_ref.1, bf16[1024,256]{1,0:T(8,128)(2,1)} %k_ref.1, bf16[1024,256]{1,0:T(8,128)(2,1)} %v_ref.1), custom_call_target="tpu_custom_call" | custom-call | flops 7340032 | bytes 2621440 | tf_op jit(solution)/shard_map/short_filters/pallas_call | solution.py:96
  19.4 0.0 copy-start.4
  19.4 0.0 collective-permute-done
  19.4 0.5 collective-permute-done.1
  20.0 2.1 %collective-permute-done.2 = bf16[64,1024]{1,0:T(8,128)(2,1)S(1)} collective-permute-done((bf16[64,1024]{1,0:T(8,128)(2,1)}, bf16[64,1024]{1,0:T(8,128)(2,1)S(1)}, u32[]{:S(2)}, u32[]{:S(2)}) %collective-permute-start.2) | collective-permute-done | bytes 131104 | tf_op jit(solution)/shard_map/ppermute | solution.py:348
  22.0 0.0 copy-done.3
  22.0 0.8 pad_maximum_fusion
  22.8 0.0 all-gather.2.cloned.1.call-update
  22.9 9.6 %all-to-all-start = ((bf16[64,16,640]{2,1,0:T(8,128)(2,1)}), bf16[64,16,640]{2,1,0:T(8,128)(2,1)S(1)}, u32[]{:S(2)}, u32[]{:S(2)}) async-start(bf16[64,16,640]{2,1,0:T(8,128)(2,1)} %short_filters.1), calls=%async_computation | async-start | bytes 2621440 | tf_op jit(solution)/shard_map/all_to_all | solution.py:364
  32.5 0.0 copy-done.4
  32.5 0.7 dynamic-slice_reduce_fusion.taps_ref
  33.3 5.8 %filter_spectrum.1.spec_hbm = f32[1024,512]{1,0:T(8,128)} custom-call(f32[16,16384]{1,0:T(8,128)} %refs_0_.1, bf16[128,64]{1,0:T(8,128)(2,1)} %constant.45.clone.refs_1_.f_hi, bf16[128,64]{1,0:T(8,128)(2,1)} %constant.46.clone.refs_2_.f_lo, f32[64,256]{1,0:T(8,128)} %constant.47.clone.refs_3_.cos_ref, f32[64,256]{1,0:T(8,128)} %constant.48.clone.refs_4_.sin_ref, ...), custom_call_target="tpu_custom_call" | custom-call | flops 1610612736 | bytes 5242880 | tf_op jit(solution)/shard_map/filter_spectrum/pallas_call | solution.py:145
  39.1 27.2 %all-to-all-done.in_ref = bf16[64,16,640]{2,1,0:T(8,128)(2,1)S(1)} async-done(((bf16[64,16,640]{2,1,0:T(8,128)(2,1)}), bf16[64,16,640]{2,1,0:T(8,128)(2,1)S(1)}, u32[]{:S(2)}, u32[]{:S(2)}) %all-to-all-start) | async-done | bytes 1310752 | tf_op jit(solution)/shard_map/all_to_all | solution.py:364
  66.2 0.0 copy-start.1
  66.2 1.1 copy-done.1
  67.3 10.4 %long_conv.1 = bf16[64,2,16,256]{3,2,1,0:T(8,128)(2,1)} custom-call(f32[16]{0:T(128)} %skip_ref.1, f32[3,7]{1,0:T(4,128)} %dynamic-slice_reduce_fusion.taps_ref, bf16[64,16,640]{2,1,0:T(8,128)(2,1)} %copy-done.1, bf16[128,64]{1,0:T(8,128)(2,1)} %constant.45.clone.refs_1_.f_hi, bf16[128,64]{1,0:T(8,128)(2,1)} %constant.46.clone.refs_2_.f_lo, ...), custom_call_target="tpu_custom_call" | custom-call | flops 3221225472 | bytes 6291456 | tf_op jit(solution)/shard_map/long_conv/pallas_call | solution.py:263
  77.7 39.5 %all_to_all.10 = bf16[128,16,256]{2,1,0:T(8,128)(2,1)S(1)} all-to-all(bf16[128,16,256]{2,1,0:T(8,128)(2,1)} %bitcast.7), channel_id=1, replica_groups=mesh['y'=4,'x'=4,'zl'=4,'zh'=2,'core'=2] {'y','x','zl','zh'}, dimensions={0} | all-to-all | bytes 2097152 | tf_op jit(solution)/shard_map/all_to_all | solution.py:368
  117.2 0.0 copy-start
  117.2 0.0 collective-permute-start.3
  117.2 0.7 pad_add_fusion
  118.0 0.0 all-gather.2.cloned.1.call-done.refs_2_
  118.0 0.3 copy-done
  118.3 6.2 %project_first.1.refs_3_ = f32[256,1024]{1,0:T(8,128)} custom-call(s32[2]{0:T(128)} %get-tuple-element.14.refs_0_, bf16[64,2,16,256]{3,2,1,0:T(8,128)(2,1)} %bitcast.6, bf16[4096,1024]{1,0:T(8,128)(2,1)} %all-gather.2.cloned.1.call-done.refs_2_), custom_call_target="tpu_custom_call" | custom-call | flops 1073741824 | bytes 4194304 | tf_op jit(solution)/shard_map/project_first/pallas_call | solution.py:330
  124.5 0.0 collective-permute-done.3.refs_1_
  124.5 0.0 copy-start.2
  124.5 1.1 copy-done.2
  125.5 6.6 %project_last.1 = bf16[1024,256]{1,0:T(8,128)(2,1)} custom-call(s32[2]{0:T(128)} %get-tuple-element.13.refs_0_, bf16[64,2,16,256]{3,2,1,0:T(8,128)(2,1)} %copy-done.2, bf16[4096,1024]{1,0:T(8,128)(2,1)} %all-gather.2.cloned.1.call-done.refs_2_, f32[256,1024]{1,0:T(8,128)} %project_first.1.refs_3_), custom_call_target="tpu_custom_call" | custom-call | flops 1073741824 | bytes 4194304 | tf_op jit(solution)/shard_map/project_last/pallas_call | solution.py:330
Async XLA Ops:
  6.5 15.5 %copy-start.3 = (bf16[64,1024]{1,0:T(8,128)(2,1)S(1)}, bf16[64,1024]{1,0:T(8,128)(2,1)}, u32[]{:S(2)}) copy-start(bf16[64,1024]{1,0:T(8,128)(2,1)} %param.21) | copy-start | bytes 393220
  6.5 111.4 %all-gather.2.cloned.1.call-start = ((), (), s32[]{:S(2)}) async-start(), calls=%async_computation.2 | async-start | bytes 8912896 | tf_op jit(solution)/shard_map/all_gather | solution.py:361
  6.5 12.9 %collective-permute-start = (bf16[64,1024]{1,0:T(8,128)(2,1)}, bf16[64,1024]{1,0:T(8,128)(2,1)S(1)}, u32[]{:S(2)}, u32[]{:S(2)}) collective-permute-start(bf16[64,1024]{1,0:T(8,128)(2,1)} %param.21), channel_id=1, source_target_pairs={{0,4},{4,8},{8,12},{12,0},{1,5},{5,9},{9,13},{13,1},{2,6},{6,10},{... | collective-permute-start | bytes 393224 | tf_op jit(solution)/shard_map/ppermute | solution.py:348
  8.5 11.5 %collective-permute-start.1 = (bf16[64,1024]{1,0:T(8,128)(2,1)}, bf16[64,1024]{1,0:T(8,128)(2,1)S(1)}, u32[]{:S(2)}, u32[]{:S(2)}) collective-permute-start(bf16[64,1024]{1,0:T(8,128)(2,1)} %param.21), channel_id=1, source_target_pairs={{0,8},{4,12},{8,0},{12,4},{1,9},{5,13},{9,1},{13,5},{2,10},{6,14},... | collective-permute-start | bytes 393224 | tf_op jit(solution)/shard_map/ppermute | solution.py:348
  10.7 11.3 %collective-permute-start.2 = (bf16[64,1024]{1,0:T(8,128)(2,1)}, bf16[64,1024]{1,0:T(8,128)(2,1)S(1)}, u32[]{:S(2)}, u32[]{:S(2)}) collective-permute-start(bf16[64,1024]{1,0:T(8,128)(2,1)} %param.21), channel_id=1, source_target_pairs={{0,12},{4,0},{8,4},{12,8},{1,13},{5,1},{9,5},{13,9},{2,14},{6,2},{... | collective-permute-start | bytes 393224 | tf_op jit(solution)/shard_map/ppermute | solution.py:348
  19.4 13.1 %copy-start.4 = (f32[3,64,7]{1,2,0:T(8,128)S(1)}, f32[3,64,7]{1,2,0:T(8,128)}, u32[]{:S(2)}) copy-start(f32[3,64,7]{1,2,0:T(8,128)} %param.18) | copy-start | bytes 16132
  22.9 43.4 %all-to-all-start = ((bf16[64,16,640]{2,1,0:T(8,128)(2,1)}), bf16[64,16,640]{2,1,0:T(8,128)(2,1)S(1)}, u32[]{:S(2)}, u32[]{:S(2)}) async-start(bf16[64,16,640]{2,1,0:T(8,128)(2,1)} %short_filters.1), calls=%async_computation | async-start | bytes 2621440 | tf_op jit(solution)/shard_map/all_to_all | solution.py:364
  66.2 1.1 copy-start.1
  117.2 1.1 copy-start
  117.2 7.2 %collective-permute-start.3 = (bf16[64,2,16,256]{3,2,1,0:T(8,128)(2,1)S(1)}, bf16[64,2,16,256]{3,2,1,0:T(8,128)(2,1)S(1)}, u32[]{:S(2)}, u32[]{:S(2)}) collective-permute-start(bf16[64,2,16,256]{3,2,1,0:T(8,128)(2,1)S(1)} %bitcast.5), channel_id=1, source_target_pairs={{0,1},{1,0},{2,3},{3,2},{4,5},{5,4},{6,7},{7,6},{8,9},{9,8},{10,11... | collective-permute-start | bytes 3145736 | tf_op jit(solution)/shard_map/ppermute | solution.py:348
  124.5 1.1 copy-start.2
Sparse Core Ops, SparseCore 0:
  23.0 92.9 all-gather.1

commit v3 on v2

--- a/solution.py
+++ b/solution.py
@@ -66,9 +66,9 @@
     return sums
 
 
-def short_kernel(taps_ref, q_ref, k_ref, v_ref, out_ref):
-    rows, cols = q_ref.shape
-    taps = taps_ref.shape[2]
+def short_kernel(taps_ref, k_ref, v_ref, out_ref):
+    rows, cols = k_ref.shape
+    taps = taps_ref.shape[1]
     size = out_ref.shape[1]
     first = pl.program_id(0) * (rows // size)
     lane = lane_ids(size)
@@ -78,31 +78,92 @@
         for index, ref in ((1, k_ref), (2, v_ref)):
             wide = ref[at, :].astype(F32)
             tiles = [wide[:, i * 128 : i * 128 + 128] for i in range(cols // 128)]
-            weights = [taps_ref[index, first + g, tap] for tap in range(taps)]
+            weights = [taps_ref[index, tap, first + g] for tap in range(taps)]
             feats.append(filter_tiles(weights, None, tiles, lane))
             shift = 8 if index == 1 else 24
             edges += [pltpu.roll(tiles[-1], shift, 1), pltpu.roll(tiles[0], shift, 1)]
         for i in range(cols // 128):
             out_ref[g, :, i * 128 : i * 128 + 128] = (feats[0][i] * feats[1][i]).astype(BF16)
-        out_ref[g, :, cols : 2 * cols] = q_ref[at, :]
         edge = jnp.where(lane < 16, jnp.where(lane < 8, edges[0], edges[1]), jnp.where(lane < 24, edges[2], edges[3]))
-        out_ref[g, :, 2 * cols :] = edge.astype(BF16)
-
-
-def short_filters(taps, query, key, value, ctx, blocks=4):
-    rows, cols = query.shape
+        out_ref[g, :, cols:] = edge.astype(BF16)
+
+
+def short_filters(taps, key, value, ctx, blocks=4):
+    rows, cols = key.shape
     size = rows // ctx
     spec = pl.BlockSpec((rows // blocks, cols), lambda i: (i, 0))
     return pl.pallas_call(
         short_kernel,
         grid=(blocks,),
-        in_specs=[pl.BlockSpec(memory_space=pltpu.SMEM)] + [spec] * 3,
-        out_specs=pl.BlockSpec((ctx // blocks, size, 2 * cols + 128), lambda i: (i, 0, 0)),
-        out_shape=jax.ShapeDtypeStruct((ctx, size, 2 * cols + 128), BF16),
+        in_specs=[pl.BlockSpec(memory_space=pltpu.SMEM)] + [spec] * 2,
+        out_specs=pl.BlockSpec((ctx // blocks, size, cols + 128), lambda i: (i, 0, 0)),
+        out_shape=jax.ShapeDtypeStruct((ctx, size, cols + 128), BF16),
         compiler_params=pltpu.CompilerParams(vmem_limit_bytes=VMEM_LIMIT),
         cost_estimate=pl.CostEstimate(flops=2 * 14 * rows * cols, bytes_accessed=10 * rows * cols, transcendentals=0),
         name="short_filters",
-    )(taps, query, key, value)
+    )(taps, key, value)
+
+
+def tail_kernel(q_ref, out_ref):
+    tail, rows = out_ref.shape
+    row = lax.broadcasted_iota(jnp.int32, (tail, 128), 0)
+    lane = lax.broadcasted_iota(jnp.int32, (tail, 128), 1)
+    pick = jnp.where(lane == 128 - tail + row, 1.0, 0.0).astype(BF16)
+    picked = lax.dot_general(pick, q_ref[...], (((1,), (1,)), ((), ())), preferred_element_type=F32)
+    out_ref[...] = picked.astype(BF16)
+
+
+def take_tail(query, tail=16):
+    rows, cols = query.shape
+    return pl.pallas_call(
+        tail_kernel,
+        grid=(1,),
+        in_specs=[pl.BlockSpec((rows, 128), lambda i: (0, cols // 128 - 1))],
+        out_specs=pl.BlockSpec((tail, rows), lambda i: (0, 0)),
+        out_shape=jax.ShapeDtypeStruct((tail, rows), BF16),
+        compiler_params=pltpu.CompilerParams(vmem_limit_bytes=VMEM_LIMIT),
+        name="query_tail",
+    )(query)
+
+
+def query_kernel(taps_ref, q_ref, rim_ref, out_ref, left_ref):
+    rows, cols = q_ref.shape
+    taps = taps_ref.shape[1]
+    tail = rim_ref.shape[0]
+    groups = taps_ref.shape[2] // pl.num_programs(0)
+    size = rows // groups
+    first = pl.program_id(0) * groups
+    row = lax.broadcasted_iota(jnp.int32, (tail, 128), 0)
+    column = lax.broadcasted_iota(jnp.int32, (tail, 128), 1)
+    place = jnp.where(column == 128 - tail + row, 1.0, 0.0).astype(BF16)
+    left_ref[...] = lax.dot_general(rim_ref[...], place, (((0,), (0,)), ((), ())), preferred_element_type=F32)
+    lane = lane_ids(size)
+    for g in range(groups):
+        at = pl.ds(g * size, size)
+        wide = q_ref[at, :].astype(F32)
+        tiles = [wide[:, i * 128 : i * 128 + 128] for i in range(cols // 128)]
+        weights = [taps_ref[0, tap, first + g] for tap in range(taps)]
+        for i, feat in enumerate(filter_tiles(weights, left_ref[at, :], tiles, lane)):
+            out_ref[at, i * 128 : i * 128 + 128] = feat.astype(BF16)
+
+
+def query_filter(taps, query, rim, blocks=4):
+    rows, cols = query.shape
+    spec = pl.BlockSpec((rows // blocks, cols), lambda i: (i, 0))
+    return pl.pallas_call(
+        query_kernel,
+        grid=(blocks,),
+        in_specs=[
+            pl.BlockSpec(memory_space=pltpu.SMEM),
+            spec,
+            pl.BlockSpec((rim.shape[0], rows // blocks), lambda i: (0, i)),
+        ],
+        out_specs=spec,
+        out_shape=jax.ShapeDtypeStruct((rows, cols), BF16),
+        scratch_shapes=[pltpu.VMEM((rows // blocks, 128), F32)],
+        compiler_params=pltpu.CompilerParams(vmem_limit_bytes=VMEM_LIMIT),
+        name="query_filter",
+    )(taps, query, rim)
 
 
 def second_dft(hi, lo, second_hi, second_lo):
@@ -154,14 +215,14 @@
             pltpu.VMEM((rows, 2 * inner), BF16),
         ],
         compiler_params=pltpu.CompilerParams(vmem_limit_bytes=VMEM_LIMIT),
-        cost_estimate=pl.CostEstimate(flops=3 * 2 * rows * 4 * inner * inner, bytes_accessed=5 * 2**20, transcendentals=0),
+        cost_estimate=pl.CostEstimate(flops=2**20, bytes_accessed=2**20, transcendentals=0),
         name="filter_spectrum",
     )(*operands)
 
 
 def conv_kernel(
-    skip_ref, taps_ref, in_ref, f_hi, f_lo, l_hi, l_lo, cos_ref, sin_ref, spec_hbm, s_hi_hbm, s_lo_hbm,
-    out_ref, rows_ref, z_ref, q_ref, edge_ref, g_hi, g_lo, spec_ref, s_hi, s_lo, sems,
+    place_ref, skip_ref, taps_ref, in_ref, f_hi, f_lo, l_hi, l_lo, cos_ref, sin_ref, spec_hbm, s_hi_hbm, s_lo_hbm,
+    out_ref, rows_ref, z_ref, edge_ref, g_hi, g_lo, spec_ref, s_hi, s_lo, sems,
 ):
     fetches = [
         pltpu.make_async_copy(source, target, sems.at[index])
@@ -170,25 +231,19 @@
     for fetch in fetches:
         fetch.start()
     outer, chans, width = in_ref.shape
-    inner = (width - 128) // 2
+    inner = width - 128
     halves = inner // 128
     rows = outer * chans
     taps = taps_ref.shape[1]
+    group = place_ref[0]
     blocks = 8
     step = rows // blocks
     units = outer // blocks
     lane = lane_ids(step)
 
     edge_ref[:chans, :] = jnp.zeros((chans, 128), F32)
-    q_ref[(halves - 1) * (rows + chans) : (halves - 1) * (rows + chans) + chans, :] = jnp.zeros((chans, 128), F32)
-    edge_ref[chans:, :] = in_ref[:, :, 2 * inner :].reshape(rows, 128).astype(F32)
-    for half in range(halves):
-        at = half * (rows + chans) + chans
-        q_ref[at : at + rows, :] = (
-            in_ref[:, :, inner + half * 128 : inner + half * 128 + 128].reshape(rows, 128).astype(F32)
-        )
-
-    weights = [jnp.where(lane < 16, taps_ref[1, tap], taps_ref[2, tap]) for tap in range(taps)]
+    edge_ref[chans:, :] = in_ref[:, :, inner:].reshape(rows, 128).astype(F32)
+    weights = [jnp.where(lane < 16, taps_ref[1, tap, group], taps_ref[2, tap, group]) for tap in range(taps)]
 
     for i in range(blocks):
         at = i * step
@@ -238,23 +293,15 @@
             for half in range(halves):
                 z_ref[pl.ds(half * rows + c, outer, stride=chans), :] = mixed[:, half * 128 : (half + 1) * 128]
 
-    q_taps = [taps_ref[0, tap] for tap in range(taps)]
-    for i in range(blocks):
-        at = i * step
-        starts = [half * (rows + chans) + chans + at for half in range(halves)]
-        tiles = [q_ref[start : start + step, :] for start in starts]
-        start = (halves - 1) * (rows + chans) + at
-        feats = filter_tiles(q_taps, q_ref[start : start + step, :], tiles, lane)
-        for half in range(halves):
-            mixed = z_ref[half * rows + at : half * rows + at + step, :].astype(BF16).astype(F32)
-            result = (feats[half] * mixed).astype(BF16).reshape(units, chans, 128)
-            for copy in range(out_ref.shape[1]):
-                out_ref[i * units : (i + 1) * units, copy, :, half * 128 : (half + 1) * 128] = result
-
-
-def long_mix(arrived, spectrum, skip_bias, taps, tables, copies):
+    for half in range(halves):
+        result = z_ref[half * rows : (half + 1) * rows, :].astype(BF16).reshape(outer, chans, 128)
+        for copy in range(out_ref.shape[1]):
+            out_ref[:, copy, :, half * 128 : (half + 1) * 128] = result
+
+
+def long_mix(place, arrived, spectrum, skip_bias, taps, tables, copies):
     outer, chans, width = arrived.shape
-    inner = (width - 128) // 2
+    inner = width - 128
     rows = outer * chans
     whole = lambda shape: pl.BlockSpec(shape, lambda i: (0,) * len(shape))
     scalars = pl.BlockSpec(memory_space=pltpu.SMEM)
@@ -263,7 +310,7 @@
     return pl.pallas_call(
         conv_kernel,
         grid=(1,),
-        in_specs=[scalars] * 2
+        in_specs=[scalars] * 3
         + [whole(operand.shape) for operand in operands]
         + [pl.BlockSpec(memory_space=pl.ANY)] * len(fetched),
         out_specs=whole((outer, copies, chans, inner)),
@@ -271,7 +318,6 @@
         scratch_shapes=[
             pltpu.VMEM((rows * inner // 128, 128), F32),
             pltpu.VMEM((rows * inner // 128, 128), F32),
-            pltpu.VMEM(((rows + chans) * inner // 128, 128), F32),
             pltpu.VMEM((rows + chans, 128), F32),
             pltpu.VMEM((rows, 2 * inner), BF16),
             pltpu.VMEM((rows, 2 * inner), BF16),
@@ -281,65 +327,83 @@
             pltpu.SemaphoreType.DMA((3,)),
         ],
         compiler_params=pltpu.CompilerParams(vmem_limit_bytes=VMEM_LIMIT),
-        cost_estimate=pl.CostEstimate(flops=6 * 2 * rows * 4 * inner * inner, bytes_accessed=6 * 2**20, transcendentals=0),
+        cost_estimate=pl.CostEstimate(flops=2**20, bytes_accessed=2**20, transcendentals=0),
         name="long_conv",
-    )(skip_bias, taps, *operands, *fetched)
+    )(place, skip_bias, taps, *operands, *fetched)
+
+
+def gate_kernel(place_ref, z_ref, q_own, q_far, out_ref):
+    _, halves, chans, cols = z_ref.shape
+    unit = 4 * chans
+    zl, zh = place_ref[1], place_ref[2]
+    for half in range(halves):
+        for x in range(4):
+            parts = []
+            for turn in range(4):
+                start = x * 4 + jnp.bitwise_and(zl - turn, 3)
+                at = pl.ds(pl.multiple_of(start * unit, unit), unit)
+                feat = jnp.where(zh == half, q_own[at, :].astype(F32), q_far[at, :].astype(F32))
+                mixed = z_ref[pl.ds(start * 4, 4), half].reshape(unit, cols).astype(F32)
+                parts.append((feat * mixed).astype(BF16))
+            to = (half * 4 + x) * 4 * unit
+            out_ref[:, to : to + 4 * unit] = jnp.concatenate(parts, axis=0).T
+
+
+def gate(place, mixed, q_own, q_far):
+    ctx, halves, chans, cols = mixed.shape
+    depth = ctx * halves * chans
+    whole = lambda shape: pl.BlockSpec(shape, lambda i: (0,) * len(shape))
+    return pl.pallas_call(
+        gate_kernel,
+        grid=(1,),
+        in_specs=[pl.BlockSpec(memory_space=pltpu.SMEM), whole(mixed.shape), whole(q_own.shape), whole(q_far.shape)],
+        out_specs=whole((cols, depth)),
+        out_shape=jax.ShapeDtypeStruct((cols, depth), BF16),
+        compiler_params=pltpu.CompilerParams(vmem_limit_bytes=VMEM_LIMIT),
+        name="gate",
+    )(place, mixed, q_own, q_far)
 
 
 def project_kernel(last, place_ref, *refs):
-    (z_ref, w_ref, sum_ref, out_ref, acc_ref) = refs if last else (refs[0], refs[1], None, refs[2], None)
-    total_ref = acc_ref if last else out_ref
-    _, _, chans, cols = z_ref.shape
-    unit = 4 * chans
-    step = pl.program_id(0)
-    zl = place_ref[0]
-    half = step // 2
-    parts = []
-    for x in range(2):
-        for turn in range(4):
-            start = (2 * (step % 2) + x) * 16 + 4 * jnp.bitwise_and(zl - turn, 3)
-            parts.append(z_ref[pl.ds(start, 4), half].reshape(unit, cols))
-    gated = jnp.concatenate(parts, axis=0)
-    part = dot(gated.T, w_ref[...])
-
-    @pl.when(step == 0)
-    def _():
-        total_ref[...] = part + sum_ref[...] if last else part
-
-    @pl.when(step > 0)
-    def _():
-        total_ref[...] += part
-
     if last:
-        @pl.when(step == pl.num_programs(0) - 1)
-        def _():
-            out_ref[...] = total_ref[...].T.astype(BF16)
+        g_ref, w_ref, sum_ref, out_ref = refs
+    else:
+        g_ref, w_ref, out_ref = refs
+    halves, rows, block = w_ref.shape
+    total = dot(g_ref[...], w_ref[...].reshape(halves * rows, block))
+    if last:
+        out_ref[...] = (total + sum_ref[...]).T.astype(BF16)
+    else:
+        out_ref[...] = total
 
 
 def project(place, gated, weight, partial=None):
     depth, width = weight.shape
-    cols = gated.shape[3]
-    last = partial is not None
-    block = depth // 8
-    whole = lambda shape: pl.BlockSpec(shape, lambda i, place: (0,) * len(shape))
-    in_specs = [whole(gated.shape), pl.BlockSpec((block, width), lambda i, place: (4 * (i // 2) + 2 * place[1] + i % 2, 0))]
-    operands = [gated, weight]
-    if last:
-        in_specs.append(whole(partial.shape))
+    cols = gated.shape[0]
+    other = 0 if partial is None else 1
+    block = 256
+    in_specs = [
+        pl.BlockSpec(gated.shape, lambda i, place: (0, 0)),
+        pl.BlockSpec((2, None, depth // 4, block), lambda i, place: (0, jnp.bitwise_xor(place[3], other), 0, i)),
+    ]
+    operands = [gated, weight.reshape(2, 2, depth // 4, width)]
+    if other:
+        in_specs.append(pl.BlockSpec((cols, block), lambda i, place: (0, i)))
         operands.append(partial)
-    return pl.pallas_call(
-        lambda *refs: project_kernel(last, *refs),
+        out_spec = pl.BlockSpec((block, cols), lambda i, place: (i, 0))
+        out_shape = jax.ShapeDtypeStruct((width, cols), BF16)
+    else:
+        out_spec = pl.BlockSpec((cols, block), lambda i, place: (0, i))
+        out_shape = jax.ShapeDtypeStruct((cols, width), F32)
+    return pl.pallas_call(
+        lambda *refs: project_kernel(bool(other), *refs),
         grid_spec=pltpu.PrefetchScalarGridSpec(
-            num_scalar_prefetch=1,
-            grid=(4,),
-            in_specs=in_specs,
-            out_specs=whole((width, cols) if last else (cols, width)),
-            scratch_shapes=[pltpu.VMEM((cols, width), F32)] if last else [],
+            num_scalar_prefetch=1, grid=(width // block,), in_specs=in_specs, out_specs=out_spec
         ),
-        out_shape=jax.ShapeDtypeStruct((width, cols), BF16) if last else jax.ShapeDtypeStruct((cols, width), F32),
-        compiler_params=pltpu.CompilerParams(vmem_limit_bytes=VMEM_LIMIT),
+        out_shape=out_shape,
+        compiler_params=pltpu.CompilerParams(vmem_limit_bytes=VMEM_LIMIT - 3 * 1024 * 1024),
         cost_estimate=pl.CostEstimate(flops=depth * width * cols, bytes_accessed=depth * width, transcendentals=0),
-        name="project_last" if last else "project_first",
+        name="project_last" if other else "project_first",
     )(place, *operands)
 
 
@@ -354,25 +418,31 @@
     chans = long_filter.shape[0]
     tables = dft_tables(ctx, cols)
 
+    taps = jnp.swapaxes(short_taps, 1, 2)
+    place = jnp.stack([lax.axis_index(name) for name in (CTX, "zl", "zh", "core")]).astype(jnp.int32)
+
     pieces = [turned(out_weight, "zl", step) for step in (1, 2, 3)]
-    ready = short_filters(short_taps, query_proj, key_proj, value_proj, ctx)
-    ready, *pieces = lax.optimization_barrier((ready, *pieces))
+    ready = short_filters(taps, key_proj, value_proj, ctx)
+    tail = take_tail(query_proj)
+    rim = lax.ppermute(tail, CTX, [(source, source + 1) for source in range(ctx - 1)])
+    ready, rim, *pieces = lax.optimization_barrier((ready, rim, *pieces))
     weight_run = jnp.concatenate([out_weight, *pieces], axis=0)
     weight = lax.all_gather(weight_run, ("y", "x"), axis=0, tiled=True)
 
+    arrived = lax.all_to_all(ready, CTX, split_axis=0, concat_axis=0, tiled=True)
+    q_feat = query_filter(taps, query_proj, rim)
+    q_far = turned(q_feat, "zh", 1)
+    long_filter, q_feat = lax.optimization_barrier((long_filter, q_feat))
     spectrum = filter_spectrum(long_filter, tables, ctx, cols)
-    arrived = lax.all_to_all(ready, CTX, split_axis=0, concat_axis=0, tiled=True)
-    own_taps = lax.dynamic_index_in_dim(short_taps, lax.axis_index(CTX), 1, keepdims=False)
-
-    gated = long_mix(arrived, spectrum, skip_bias, own_taps, tables, 2)
+
+    mixed = long_mix(place, arrived, spectrum, skip_bias, taps, tables, 2)
+    mixed, q_far = lax.optimization_barrier((mixed, q_far))
     own = lax.all_to_all(
-        gated.reshape(2 * ctx, chans, cols), CTX + ("zh",), split_axis=0, concat_axis=0, tiled=True
+        mixed.reshape(2 * ctx, chans, cols), CTX + ("zh",), split_axis=0, concat_axis=0, tiled=True
     ).reshape(ctx, 2, chans, cols)
-    other = turned(own, "core", 1)
-
-    zl, core = lax.axis_index("zl"), lax.axis_index("core")
-    partial = project(jnp.stack([zl, core]).astype(jnp.int32), own, weight)
-    return project(jnp.stack([zl, 1 - core]).astype(jnp.int32), other, weight, partial)
+    gated = gate(place, own, q_feat, q_far)
+    other = turned(gated, "core", 1)
+    return project(place, other, weight, project(place, gated, weight))
 
 
 def solution(mesh):

time: 141 us -> 156 us (1.11)
  starting transfers between devices: 14.9 us -> 23.4 us
  Pallas kernels: 35.2 us -> 41.7 us
  local copies, waits for them, and re-layouts: 4.65 us -> 1.97 us
    pallas_call x3 -> x6, Pallas kernels: 23.2 us -> 31.2 us  [the longest x2 12 us: project(): pl.pallas_call(lambda *refs: project_kernel(bool(other), *refs), grid_spe...]
    ppermute x4 -> x5, starting transfers between devices: 5.3 us -> 10.7 us  [turned(): lax.ppermute(value, axis, [(source, (source + steps) % count) for source...]
    ppermute x0 -> x1, starting transfers between devices: none -> 2.83 us  [shards(): lax.ppermute(tail, CTX, [(source, source + 1) for source in range(ctx - 1)])]
    unnamed x11 -> x8, local copies, waits for them, and re-layouts: 3.9 us -> 1.97 us
  transfers between devices with their start and end apart: 6 -> 8, of which waited for: 3 -> 2; matrix products, arithmetic and copies ran while one was open for 2% -> 0% of each run, Pallas kernels for 21% -> 23%
where the time goes in v3:
time: 156 us; the launch traced here: 153 us
  Pallas kernels  41.7 us (27%)
  blocking collectives  40.2 us (26%)
  waiting for transfers between devices  30.1 us (19%)
  starting transfers between devices  23.4 us (15%)
  between operations  13.5 us (9%)
  other arithmetic  2.41 us (2%)
  local copies, waits for them, and re-layouts  1.97 us (1%)
    all_to_all x1, blocking collectives, shards(): lax.all_to_all(mixed.reshape(2 * ctx, chans, cols), CTX + ('zh',), split_...  40.2 us
    all_to_all x1, waiting for transfers between devices, shards(): lax.all_to_all(ready, CTX, split_axis=0, concat_axis=0, tiled=True)  28.4 us
    pallas_call x2, Pallas kernels, project(): pl.pallas_call(lambda *refs: project_kernel(bool(other), *refs), grid_spe...  12 us
    ppermute x5, starting transfers between devices, turned(): lax.ppermute(value, axis, [(source, (source + steps) % count) for source...  10.7 us
    pallas_call x1, Pallas kernels, long_mix(): pl.pallas_call(conv_kernel, grid=(1,), in_specs=[scalars] * 3 + [whole(op...  9.93 us
    all_to_all x1, starting transfers between devices, shards(): lax.all_to_all(ready, CTX, split_axis=0, concat_axis=0, tiled=True)  9.87 us
    pallas_call x1, Pallas kernels, filter_spectrum(): pl.pallas_call(lambda *refs: filter_kernel(1.0 / (outer * inner), *refs),...  5.86 us
    pallas_call x1, Pallas kernels, short_filters(): pl.pallas_call(short_kernel, grid=(blocks,), in_specs=[pl.BlockSpec(memor...  4.63 us
  transfers between devices with their start and end apart: 8, of which 2 were waited for; matrix products, arithmetic and copies ran while one was open for 0% of the time, Pallas kernels for 23%

profile of v3, /device:TPU:32, one launch (start us, length us, event | category | flops | bytes accessed | tf_op | source)
XLA Modules:
  0.0 153.1 jit_solution(10136726489819544170)
XLA Ops:
  6.5 0.0 all-gather.2.cloned.1.call-start
  6.5 1.9 %collective-permute-start.1 = (bf16[64,1024]{1,0:T(8,128)(2,1)}, bf16[64,1024]{1,0:T(8,128)(2,1)S(1)}, u32[]{:S(2)}, u32[]{:S(2)}) collective-permute-start(bf16[64,1024]{1,0:T(8,128)(2,1)} %param.21), channel_id=1, source_target_pairs={{0,4},{4,8},{8,12},{12,0},{1,5},{5,9},{9,13},{13,1},{2,6},{6,10},{... | collective-permute-start | bytes 393224 | tf_op jit(solution)/shard_map/ppermute | solution.py:412
  8.5 2.3 %collective-permute-start.2 = (bf16[64,1024]{1,0:T(8,128)(2,1)}, bf16[64,1024]{1,0:T(8,128)(2,1)S(1)}, u32[]{:S(2)}, u32[]{:S(2)}) collective-permute-start(bf16[64,1024]{1,0:T(8,128)(2,1)} %param.21), channel_id=1, source_target_pairs={{0,8},{4,12},{8,0},{12,4},{1,9},{5,13},{9,1},{13,5},{2,10},{6,14},... | collective-permute-start | bytes 393224 | tf_op jit(solution)/shard_map/ppermute | solution.py:412
  10.7 1.1 collective-permute-start.3
  11.8 1.7 %query_tail.1 = bf16[16,1024]{1,0:T(8,128)(2,1)} custom-call(bf16[1024,256]{1,0:T(8,128)(2,1)} %q_ref.3), custom_call_target="tpu_custom_call" | custom-call | tf_op jit(solution)/shard_map/query_tail/pallas_call | solution.py:118
  13.6 2.8 %collective-permute-start = (bf16[16,1024]{1,0:T(8,128)(2,1)}, bf16[16,1024]{1,0:T(8,128)(2,1)S(1)}, u32[]{:S(2)}, u32[]{:S(2)}) collective-permute-start(bf16[16,1024]{1,0:T(8,128)(2,1)} %query_tail.1), channel_id=1, source_target_pairs={{0,4},{4,8},{8,12},{12,16},{16,20},{20,24},{24,28},{28,32},{32,36}... | collective-permute-start | bytes 98312 | tf_op jit(solution)/shard_map/ppermute | solution.py:427
  16.4 4.6 %short_filters.1 = bf16[64,16,384]{2,1,0:T(8,128)(2,1)} custom-call(f32[3,7,64]{2,1,0:T(8,128)} %bitcast.12, bf16[1024,256]{1,0:T(8,128)(2,1)} %k_ref.1, bf16[1024,256]{1,0:T(8,128)(2,1)} %v_ref.1), custom_call_target="tpu_custom_call" | custom-call | flops 7340032 | bytes 2621440 | tf_op jit(solution)/shard_map/short_filters/pallas_call | solution.py:95
  21.1 0.0 collective-permute-done.rim_ref
  21.1 0.0 copy-start.3
  21.1 0.0 collective-permute-done.1
  21.1 0.0 collective-permute-done.2
  21.1 1.6 %collective-permute-done.3 = bf16[64,1024]{1,0:T(8,128)(2,1)S(1)} collective-permute-done((bf16[64,1024]{1,0:T(8,128)(2,1)}, bf16[64,1024]{1,0:T(8,128)(2,1)S(1)}, u32[]{:S(2)}, u32[]{:S(2)}) %collective-permute-start.3) | collective-permute-done | bytes 131104 | tf_op jit(solution)/shard_map/ppermute | solution.py:412
  22.7 1.8 %pad_maximum_fusion = bf16[256,1024]{1,0:T(8,128)(2,1)} fusion(bf16[64,1024]{1,0:T(8,128)(2,1)S(1)} %collective-permute-done.3, bf16[64,1024]{1,0:T(8,128)(2,1)S(1)} %collective-permute-done.2, bf16[64,1024]{1,0:T(8,128)(2,1)S(1)} %collective-permute-done.1, bf16[64,1024]{1,0:T(8,128)(2,1)} %param.21), kind=kLoop, calls=%fused_computation | loop fusion | flops 2097152 | bytes 1048576 | tf_op jit(solution)/shard_map/concatenate | solution.py:429
  24.5 0.0 all-gather.2.cloned.1.call-update
  24.5 9.9 %all-to-all-start = ((bf16[64,16,384]{2,1,0:T(8,128)(2,1)}), bf16[64,16,384]{2,1,0:T(8,128)(2,1)S(1)}, u32[]{:S(2)}, u32[]{:S(2)}) async-start(bf16[64,16,384]{2,1,0:T(8,128)(2,1)} %short_filters.1), calls=%async_computation | async-start | bytes 1572864 | tf_op jit(solution)/shard_map/all_to_all | solution.py:432
  34.4 0.0 copy-done.3
  34.4 4.5 %query_filter.1.q_own = bf16[1024,256]{1,0:T(8,128)(2,1)} custom-call(f32[3,7,64]{2,1,0:T(8,128)} %bitcast.13, bf16[1024,256]{1,0:T(8,128)(2,1)} %q_ref.3, bf16[16,1024]{1,0:T(8,128)(2,1)} %copy-done.3), custom_call_target="tpu_custom_call" | custom-call | tf_op jit(solution)/shard_map/query_filter/pallas_call | solution.py:153
  38.8 5.4 %collective-permute-start.4 = (bf16[1024,256]{1,0:T(8,128)(2,1)}, bf16[1024,256]{1,0:T(8,128)(2,1)S(1)}, u32[]{:S(2)}, u32[]{:S(2)}) collective-permute-start(bf16[1024,256]{1,0:T(8,128)(2,1)} %query_filter.1.q_own), channel_id=1, source_target_pairs={{0,2},{2,0},{1,3},{3,1},{4,6},{6,4},{5,7},{7,5},{8,10},{10,8},{9,1... | collective-permute-start | bytes 1572872 | tf_op jit(solution)/shard_map/ppermute | solution.py:412
  44.2 0.6 pad_add_fusion.place_ref.refs_0_
  44.9 5.9 %filter_spectrum.1.spec_hbm = f32[1024,512]{1,0:T(8,128)} custom-call(f32[16,16384]{1,0:T(8,128)} %refs_0_, bf16[128,64]{1,0:T(8,128)(2,1)} %constant.39.clone.refs_1_.f_hi, bf16[128,64]{1,0:T(8,128)(2,1)} %constant.40.clone.refs_2_.f_lo, f32[64,256]{1,0:T(8,128)} %constant.41.clone.refs_3_.cos_ref, f32[64,256]{1,0:T(8,128)} %constant.42.clone.refs_4_.sin_ref, ...), custom_call_target="tpu_custom_call" | custom-call | flops 1048576 | bytes 1048576 | tf_op jit(solution)/shard_map/filter_spectrum/pallas_call | solution.py:206
  50.7 28.4 %all-to-all-done.in_ref = bf16[64,16,384]{2,1,0:T(8,128)(2,1)S(1)} async-done(((bf16[64,16,384]{2,1,0:T(8,128)(2,1)}), bf16[64,16,384]{2,1,0:T(8,128)(2,1)S(1)}, u32[]{:S(2)}, u32[]{:S(2)}) %all-to-all-start) | async-done | bytes 786464 | tf_op jit(solution)/shard_map/all_to_all | solution.py:432
  79.2 0.0 copy-start
  79.2 0.9 copy-done
  80.0 9.9 %long_conv.1 = bf16[64,2,16,256]{3,2,1,0:T(8,128)(2,1)} custom-call(s32[4]{0:T(128)} %pad_add_fusion.place_ref.refs_0_, f32[16]{0:T(128)} %skip_ref.1, f32[3,7,64]{2,1,0:T(8,128)} %bitcast.14, bf16[64,16,384]{2,1,0:T(8,128)(2,1)} %copy-done, bf16[128,64]{1,0:T(8,128)(2,1)} %constant.39.clone.refs_1_.f_hi, bf16[128,64]{1,0:T(8,128)(2,1)} %constant.40.clone.refs_2_.f_lo, ...), custom_call_target="tpu_custom_call" | custom-call | flops 1048576 | bytes 1048576 | tf_op jit(solution)/shard_map/long_conv/pallas_call | solution.py:310
  90.0 0.0 collective-permute-done.4.q_far
  90.0 0.0 copy-start.2
  90.0 40.2 %all_to_all.10 = bf16[128,16,256]{2,1,0:T(8,128)(2,1)} all-to-all(bf16[128,16,256]{2,1,0:T(8,128)(2,1)} %bitcast.10), channel_id=1, replica_groups=mesh['y'=4,'x'=4,'zl'=4,'zh'=2,'core'=2] {'y','x','zl','zh'}, dimensions={0} | all-to-all | bytes 2097152 | tf_op jit(solution)/shard_map/all_to_all | solution.py:440
  130.2 0.0 copy-done.2
  130.2 3.1 %gate.1.refs_1_ = bf16[256,2048]{1,0:T(8,128)(2,1)} custom-call(s32[4]{0:T(128)} %pad_add_fusion.place_ref.refs_0_, bf16[64,2,16,256]{3,2,1,0:T(8,128)(2,1)} %bitcast.11, bf16[1024,256]{1,0:T(8,128)(2,1)} %query_filter.1.q_own, bf16[1024,256]{1,0:T(8,128)(2,1)} %copy-done.2), custom_call_target="tpu_custom_call" | custom-call | tf_op jit(solution)/shard_map/gate/pallas_call | solution.py:356
  133.2 0.0 collective-permute-start.5
  133.2 0.0 all-gather.2.cloned.1.call-done
  133.2 5.9 %project_first.1.refs_3_ = f32[256,1024]{1,0:T(8,128)} custom-call(s32[4]{0:T(128)} %pad_add_fusion.place_ref.refs_0_, bf16[256,2048]{1,0:T(8,128)(2,1)} %gate.1.refs_1_, bf16[2,2,1024,1024]{3,2,1,0:T(8,128)(2,1)} %bitcast.8), custom_call_target="tpu_custom_call" | custom-call | flops 1073741824 | bytes 4194304 | tf_op jit(solution)/shard_map/project_first/pallas_call | solution.py:398
  139.2 0.0 collective-permute-done.5.refs_1_
  139.2 0.0 copy-start.1
  139.2 1.1 copy-done.1
  140.2 6.0 %project_last.1 = bf16[1024,256]{1,0:T(8,128)(2,1)} custom-call(s32[4]{0:T(128)} %pad_add_fusion.place_ref.refs_0_, bf16[256,2048]{1,0:T(8,128)(2,1)} %copy-done.1, bf16[2,2,1024,1024]{3,2,1,0:T(8,128)(2,1)} %bitcast.9, f32[256,1024]{1,0:T(8,128)} %project_first.1.refs_3_), custom_call_target="tpu_custom_call" | custom-call | flops 1073741824 | bytes 4194304 | tf_op jit(solution)/shard_map/project_last/pallas_call | solution.py:398
Async XLA Ops:
  6.5 126.7 %all-gather.2.cloned.1.call-start = ((), (), s32[]{:S(2)}) async-start(), calls=%async_computation.2 | async-start | bytes 8912896 | tf_op jit(solution)/shard_map/all_gather | solution.py:430
  6.5 14.5 %collective-permute-start.1 = (bf16[64,1024]{1,0:T(8,128)(2,1)}, bf16[64,1024]{1,0:T(8,128)(2,1)S(1)}, u32[]{:S(2)}, u32[]{:S(2)}) collective-permute-start(bf16[64,1024]{1,0:T(8,128)(2,1)} %param.21), channel_id=1, source_target_pairs={{0,4},{4,8},{8,12},{12,0},{1,5},{5,9},{9,13},{13,1},{2,6},{6,10},{... | collective-permute-start | bytes 393224 | tf_op jit(solution)/shard_map/ppermute | solution.py:412
  8.5 12.6 %collective-permute-start.2 = (bf16[64,1024]{1,0:T(8,128)(2,1)}, bf16[64,1024]{1,0:T(8,128)(2,1)S(1)}, u32[]{:S(2)}, u32[]{:S(2)}) collective-permute-start(bf16[64,1024]{1,0:T(8,128)(2,1)} %param.21), channel_id=1, source_target_pairs={{0,8},{4,12},{8,0},{12,4},{1,9},{5,13},{9,1},{13,5},{2,10},{6,14},... | collective-permute-start | bytes 393224 | tf_op jit(solution)/shard_map/ppermute | solution.py:412
  10.7 11.9 %collective-permute-start.3 = (bf16[64,1024]{1,0:T(8,128)(2,1)}, bf16[64,1024]{1,0:T(8,128)(2,1)S(1)}, u32[]{:S(2)}, u32[]{:S(2)}) collective-permute-start(bf16[64,1024]{1,0:T(8,128)(2,1)} %param.21), channel_id=1, source_target_pairs={{0,12},{4,0},{8,4},{12,8},{1,13},{5,1},{9,5},{13,9},{2,14},{6,2},{... | collective-permute-start | bytes 393224 | tf_op jit(solution)/shard_map/ppermute | solution.py:412
  13.6 7.5 %collective-permute-start = (bf16[16,1024]{1,0:T(8,128)(2,1)}, bf16[16,1024]{1,0:T(8,128)(2,1)S(1)}, u32[]{:S(2)}, u32[]{:S(2)}) collective-permute-start(bf16[16,1024]{1,0:T(8,128)(2,1)} %query_tail.1), channel_id=1, source_target_pairs={{0,4},{4,8},{8,12},{12,16},{16,20},{20,24},{24,28},{28,32},{32,36}... | collective-permute-start | bytes 98312 | tf_op jit(solution)/shard_map/ppermute | solution.py:427
  21.1 13.3 %copy-start.3 = (bf16[16,1024]{1,0:T(8,128)(2,1)}, bf16[16,1024]{1,0:T(8,128)(2,1)S(1)}, u32[]{:S(2)}) copy-start(bf16[16,1024]{1,0:T(8,128)(2,1)S(1)} %collective-permute-done.rim_ref) | copy-start | bytes 98308
  24.5 54.7 %all-to-all-start = ((bf16[64,16,384]{2,1,0:T(8,128)(2,1)}), bf16[64,16,384]{2,1,0:T(8,128)(2,1)S(1)}, u32[]{:S(2)}, u32[]{:S(2)}) async-start(bf16[64,16,384]{2,1,0:T(8,128)(2,1)} %short_filters.1), calls=%async_computation | async-start | bytes 1572864 | tf_op jit(solution)/shard_map/all_to_all | solution.py:432
  38.8 51.2 %collective-permute-start.4 = (bf16[1024,256]{1,0:T(8,128)(2,1)}, bf16[1024,256]{1,0:T(8,128)(2,1)S(1)}, u32[]{:S(2)}, u32[]{:S(2)}) collective-permute-start(bf16[1024,256]{1,0:T(8,128)(2,1)} %query_filter.1.q_own), channel_id=1, source_target_pairs={{0,2},{2,0},{1,3},{3,1},{4,6},{6,4},{5,7},{7,5},{8,10},{10,8},{9,1... | collective-permute-start | bytes 1572872 | tf_op jit(solution)/shard_map/ppermute | solution.py:412
  79.2 0.9 copy-start
  90.0 40.2 %copy-start.2 = (bf16[1024,256]{1,0:T(8,128)(2,1)}, bf16[1024,256]{1,0:T(8,128)(2,1)S(1)}, u32[]{:S(2)}) copy-start(bf16[1024,256]{1,0:T(8,128)(2,1)S(1)} %collective-permute-done.4.q_far) | copy-start | bytes 1572868
  133.2 5.9 %collective-permute-start.5 = (bf16[256,2048]{1,0:T(8,128)(2,1)}, bf16[256,2048]{1,0:T(8,128)(2,1)S(1)}, u32[]{:S(2)}, u32[]{:S(2)}) collective-permute-start(bf16[256,2048]{1,0:T(8,128)(2,1)} %gate.1.refs_1_), channel_id=1, source_target_pairs={{0,1},{1,0},{2,3},{3,2},{4,5},{5,4},{6,7},{7,6},{8,9},{9,8},{10,11... | collective-permute-start | bytes 3145736 | tf_op jit(solution)/shard_map/ppermute | solution.py:412
  139.2 1.1 copy-start.1
Sparse Core Ops, SparseCore 0:
  24.6 85.2 all-gather.1

commit v4 on v2

--- a/solution.py
+++ b/solution.py
@@ -11,7 +11,8 @@
 BF16 = jnp.bfloat16
 F32 = jnp.float32
 CTX = ("y", "x", "zl")
-VMEM_LIMIT = 60 * 1024 * 1024
+MIB = 1024 * 1024
+VMEM_LIMIT = 60 * MIB
 
 
 def hi_lo(table):
@@ -68,7 +69,7 @@
 
 def short_kernel(taps_ref, q_ref, k_ref, v_ref, out_ref):
     rows, cols = q_ref.shape
-    taps = taps_ref.shape[2]
+    taps = taps_ref.shape[1]
     size = out_ref.shape[1]
     first = pl.program_id(0) * (rows // size)
     lane = lane_ids(size)
@@ -78,7 +79,7 @@
         for index, ref in ((1, k_ref), (2, v_ref)):
             wide = ref[at, :].astype(F32)
             tiles = [wide[:, i * 128 : i * 128 + 128] for i in range(cols // 128)]
-            weights = [taps_ref[index, first + g, tap] for tap in range(taps)]
+            weights = [taps_ref[index, tap, first + g] for tap in range(taps)]
             feats.append(filter_tiles(weights, None, tiles, lane))
             shift = 8 if index == 1 else 24
             edges += [pltpu.roll(tiles[-1], shift, 1), pltpu.roll(tiles[0], shift, 1)]
@@ -160,7 +161,7 @@
 
 
 def conv_kernel(
-    skip_ref, taps_ref, in_ref, f_hi, f_lo, l_hi, l_lo, cos_ref, sin_ref, spec_hbm, s_hi_hbm, s_lo_hbm,
+    place_ref, skip_ref, taps_ref, in_ref, f_hi, f_lo, l_hi, l_lo, cos_ref, sin_ref, spec_hbm, s_hi_hbm, s_lo_hbm,
     out_ref, rows_ref, z_ref, q_ref, edge_ref, g_hi, g_lo, spec_ref, s_hi, s_lo, sems,
 ):
     fetches = [
@@ -174,6 +175,7 @@
     halves = inner // 128
     rows = outer * chans
     taps = taps_ref.shape[1]
+    group = place_ref[0]
     blocks = 8
     step = rows // blocks
     units = outer // blocks
@@ -188,7 +190,7 @@
             in_ref[:, :, inner + half * 128 : inner + half * 128 + 128].reshape(rows, 128).astype(F32)
         )
 
-    weights = [jnp.where(lane < 16, taps_ref[1, tap], taps_ref[2, tap]) for tap in range(taps)]
+    weights = [jnp.where(lane < 16, taps_ref[1, tap, group], taps_ref[2, tap, group]) for tap in range(taps)]
 
     for i in range(blocks):
         at = i * step
@@ -213,8 +215,9 @@
     for fetch in fetches:
         fetch.wait()
 
-    for i in range(chans * outer // 256):
-        at = pl.ds(i * 256, 256)
+    block = min(chans * outer, 512)
+    for i in range(chans * outer // block):
+        at = pl.ds(i * block, block)
         sig = second_dft(g_hi[at, :], g_lo[at, :], s_hi, s_lo)
         sr, si = sig[:, :inner], sig[:, inner:]
         hr, hm = spec_ref[at, :inner], spec_ref[at, inner:]
@@ -223,13 +226,13 @@
         back = second_dft(
             jnp.concatenate([r_hi, i_hi], axis=1), jnp.concatenate([r_lo, i_lo], axis=1), s_hi, s_lo
         )
-        back = back.reshape(256 // outer, outer, 2 * inner)
+        back = back.reshape(block // outer, outer, 2 * inner)
         re, im = back[:, :, :inner], back[:, :, inner:]
         cos, sin = cos_ref[...], sin_ref[...]
-        r_hi, r_lo = split_bf16((re * cos + im * sin).reshape(256, inner))
-        i_hi, i_lo = split_bf16((re * sin - im * cos).reshape(256, inner))
-        for j in range(256 // outer):
-            c = i * (256 // outer) + j
+        r_hi, r_lo = split_bf16((re * cos + im * sin).reshape(block, inner))
+        i_hi, i_lo = split_bf16((re * sin - im * cos).reshape(block, inner))
+        for j in range(block // outer):
+            c = i * (block // outer) + j
             part = slice(j * outer, (j + 1) * outer)
             hi = jnp.concatenate([r_hi[part], i_hi[part]], axis=0)
             lo = jnp.concatenate([r_lo[part], i_lo[part]], axis=0)
@@ -238,7 +241,7 @@
             for half in range(halves):
                 z_ref[pl.ds(half * rows + c, outer, stride=chans), :] = mixed[:, half * 128 : (half + 1) * 128]
 
-    q_taps = [taps_ref[0, tap] for tap in range(taps)]
+    q_taps = [taps_ref[0, tap, group] for tap in range(taps)]
     for i in range(blocks):
         at = i * step
         starts = [half * (rows + chans) + chans + at for half in range(halves)]
@@ -252,7 +255,7 @@
                 out_ref[i * units : (i + 1) * units, copy, :, half * 128 : (half + 1) * 128] = result
 
 
-def long_mix(arrived, spectrum, skip_bias, taps, tables, copies):
+def long_mix(place, arrived, spectrum, skip_bias, taps, tables, copies):
     outer, chans, width = arrived.shape
     inner = (width - 128) // 2
     rows = outer * chans
@@ -263,7 +266,7 @@
     return pl.pallas_call(
         conv_kernel,
         grid=(1,),
-        in_specs=[scalars] * 2
+        in_specs=[scalars] * 3
         + [whole(operand.shape) for operand in operands]
         + [pl.BlockSpec(memory_space=pl.ANY)] * len(fetched),
         out_specs=whole((outer, copies, chans, inner)),
@@ -281,65 +284,101 @@
             pltpu.SemaphoreType.DMA((3,)),
         ],
         compiler_params=pltpu.CompilerParams(vmem_limit_bytes=VMEM_LIMIT),
-        cost_estimate=pl.CostEstimate(flops=6 * 2 * rows * 4 * inner * inner, bytes_accessed=6 * 2**20, transcendentals=0),
+        cost_estimate=pl.CostEstimate(flops=2**20, bytes_accessed=2**20, transcendentals=0),
         name="long_conv",
-    )(skip_bias, taps, *operands, *fetched)
-
-
-def project_kernel(last, place_ref, *refs):
-    (z_ref, w_ref, sum_ref, out_ref, acc_ref) = refs if last else (refs[0], refs[1], None, refs[2], None)
-    total_ref = acc_ref if last else out_ref
-    _, _, chans, cols = z_ref.shape
+    )(place, skip_bias, taps, *operands, *fetched)
+
+
+def project_kernel(other, place_ref, z_hbm, *refs):
+    extras, refs = refs[:4], refs[4:]
+    if other:
+        w_hbm, sum_hbm, out_hbm, z_ref, w_ref, g_ref, out_ref, sum_ref, sems = refs
+    else:
+        w_hbm, out_hbm, z_ref, w_ref, g_ref, out_ref, sems = refs
+    _, halves, chans, cols = z_ref.shape
+    depth, width = w_ref.shape
     unit = 4 * chans
-    step = pl.program_id(0)
-    zl = place_ref[0]
-    half = step // 2
-    parts = []
-    for x in range(2):
-        for turn in range(4):
-            start = (2 * (step % 2) + x) * 16 + 4 * jnp.bitwise_and(zl - turn, 3)
-            parts.append(z_ref[pl.ds(start, 4), half].reshape(unit, cols))
-    gated = jnp.concatenate(parts, axis=0)
-    part = dot(gated.T, w_ref[...])
-
-    @pl.when(step == 0)
-    def _():
-        total_ref[...] = part + sum_ref[...] if last else part
-
-    @pl.when(step > 0)
-    def _():
-        total_ref[...] += part
-
-    if last:
-        @pl.when(step == pl.num_programs(0) - 1)
-        def _():
-            out_ref[...] = total_ref[...].T.astype(BF16)
-
-
-def project(place, gated, weight, partial=None):
-    depth, width = weight.shape
+    size = 4 * unit
+    run = size - unit
+    block = 256
+    y, x_here, zl = place_ref[4], place_ref[5], place_ref[1]
+    core = jnp.bitwise_xor(place_ref[3], other)
+
+    def copy(source, target, index):
+        fetch = pltpu.make_async_copy(source, target, sems.at[index])
+        fetch.start()
+        return fetch
+
+    arriving = copy(z_hbm, z_ref, 0)
+    fetches = []
+    for half in range(halves):
+        for x in range(4):
+            index = half * 4 + x
+            at = index * size
+            panel = half * 2 + core
+            start = pl.multiple_of((panel * 4 + x) * run, unit)
+            fetches.append(copy(w_hbm.at[pl.ds(start, run)], w_ref.at[pl.ds(at, run)], 1 + index))
+            start = pl.multiple_of(jnp.bitwise_and(x_here - x, 3) * unit, unit)
+            for turn, extra in enumerate(extras):
+
+                @pl.when(jnp.bitwise_and(y - panel, 3) == turn)
+                def _():
+                    copy(extra.at[pl.ds(start, unit)], w_ref.at[pl.ds(at + run, unit)], 9 + index)
+
+            fetches.append(
+                pltpu.make_async_copy(extras[0].at[pl.ds(start, unit)], w_ref.at[pl.ds(at + run, unit)], sems.at[9 + index])
+            )
+    if other:
+        fetches.append(copy(sum_hbm, sum_ref, 17))
+    arriving.wait()
+    for half in range(halves):
+        for x in range(4):
+            parts = []
+            for turn in range(4):
+                start = x * 16 + 4 * jnp.bitwise_and(zl - turn, 3)
+                parts.append(z_ref[pl.ds(start, 4), half].reshape(unit, cols))
+            to = (half * 4 + x) * size
+            g_ref[:, to : to + size] = jnp.concatenate(parts, axis=0).T
+    for fetch in fetches:
+        fetch.wait()
+    leaving = []
+    for index in range(width // block):
+        at = slice(index * block, (index + 1) * block)
+        part = dot(g_ref[...], w_ref[:, at])
+        if other:
+            out_ref[at, :] = (part + sum_ref[:, at]).T.astype(BF16)
+            leaving.append(copy(out_ref.at[at], out_hbm.at[at], 18 + index))
+        else:
+            out_ref[index] = part
+            leaving.append(copy(out_ref.at[index], out_hbm.at[:, at], 18 + index))
+    for leave in leaving:
+        leave.wait()
+
+
+def project(place, gated, weight, extras, partial=None):
+    width = weight.shape[1]
+    depth = (weight.shape[0] + 4 * extras[0].shape[0]) // 2
     cols = gated.shape[3]
-    last = partial is not None
-    block = depth // 8
-    whole = lambda shape: pl.BlockSpec(shape, lambda i, place: (0,) * len(shape))
-    in_specs = [whole(gated.shape), pl.BlockSpec((block, width), lambda i, place: (4 * (i // 2) + 2 * place[1] + i % 2, 0))]
-    operands = [gated, weight]
-    if last:
-        in_specs.append(whole(partial.shape))
-        operands.append(partial)
+    other = 0 if partial is None else 1
+    anywhere = pl.BlockSpec(memory_space=pl.ANY)
+    operands = [gated, *extras, weight] + ([partial] if other else [])
+    shape = (width, cols) if other else (cols, width)
     return pl.pallas_call(
-        lambda *refs: project_kernel(last, *refs),
-        grid_spec=pltpu.PrefetchScalarGridSpec(
-            num_scalar_prefetch=1,
-            grid=(4,),
-            in_specs=in_specs,
-            out_specs=whole((width, cols) if last else (cols, width)),
-            scratch_shapes=[pltpu.VMEM((cols, width), F32)] if last else [],
-        ),
-        out_shape=jax.ShapeDtypeStruct((width, cols), BF16) if last else jax.ShapeDtypeStruct((cols, width), F32),
+        lambda *refs: project_kernel(other, *refs),
+        in_specs=[pl.BlockSpec(memory_space=pltpu.SMEM)] + [anywhere] * len(operands),
+        out_specs=anywhere,
+        out_shape=jax.ShapeDtypeStruct(shape, BF16 if other else F32),
+        scratch_shapes=[
+            pltpu.VMEM(gated.shape, BF16),
+            pltpu.VMEM((depth, width), BF16),
+            pltpu.VMEM((cols, depth), BF16),
+            pltpu.VMEM(shape, BF16) if other else pltpu.VMEM((width // 256, cols, 256), F32),
+        ]
+        + ([pltpu.VMEM((cols, width), F32)] if other else [])
+        + [pltpu.SemaphoreType.DMA((18 + width // 256,))],
         compiler_params=pltpu.CompilerParams(vmem_limit_bytes=VMEM_LIMIT),
-        cost_estimate=pl.CostEstimate(flops=depth * width * cols, bytes_accessed=depth * width, transcendentals=0),
-        name="project_last" if last else "project_first",
+        cost_estimate=pl.CostEstimate(flops=2 * depth * width * cols, bytes_accessed=2 * depth * width, transcendentals=0),
+        name="project_last" if other else "project_first",
     )(place, *operands)
 
 
@@ -354,25 +393,29 @@
     chans = long_filter.shape[0]
     tables = dft_tables(ctx, cols)
 
+    taps = jnp.swapaxes(short_taps, 1, 2)
+    place = jnp.stack([lax.axis_index(name) for name in (CTX, "zl", "zh", "core", "y", "x")]).astype(jnp.int32)
+
     pieces = [turned(out_weight, "zl", step) for step in (1, 2, 3)]
-    ready = short_filters(short_taps, query_proj, key_proj, value_proj, ctx)
+    ready = short_filters(taps, query_proj, key_proj, value_proj, ctx)
     ready, *pieces = lax.optimization_barrier((ready, *pieces))
-    weight_run = jnp.concatenate([out_weight, *pieces], axis=0)
-    weight = lax.all_gather(weight_run, ("y", "x"), axis=0, tiled=True)
+    weight = lax.all_gather(jnp.concatenate([out_weight, *pieces[:2]], axis=0), ("y", "x"), axis=0, tiled=True)
 
     spectrum = filter_spectrum(long_filter, tables, ctx, cols)
     arrived = lax.all_to_all(ready, CTX, split_axis=0, concat_axis=0, tiled=True)
-    own_taps = lax.dynamic_index_in_dim(short_taps, lax.axis_index(CTX), 1, keepdims=False)
-
-    gated = long_mix(arrived, spectrum, skip_bias, own_taps, tables, 2)
+
+    spectrum, last_piece = lax.optimization_barrier((spectrum, pieces[2]))
+    along_x = jnp.concatenate([last_piece] + [turned(last_piece, "x", step) for step in (1, 2, 3)], axis=0)
+    along_y = [turned(along_x, "y", step) for step in (1, 2, 3)]
+
+    gated = long_mix(place, arrived, spectrum, skip_bias, taps, tables, 2)
+    gated, *along_y = lax.optimization_barrier((gated, *along_y))
+    extras = [along_x, *along_y]
     own = lax.all_to_all(
         gated.reshape(2 * ctx, chans, cols), CTX + ("zh",), split_axis=0, concat_axis=0, tiled=True
     ).reshape(ctx, 2, chans, cols)
     other = turned(own, "core", 1)
-
-    zl, core = lax.axis_index("zl"), lax.axis_index("core")
-    partial = project(jnp.stack([zl, core]).astype(jnp.int32), own, weight)
-    return project(jnp.stack([zl, 1 - core]).astype(jnp.int32), other, weight, partial)
+    return project(place, other, weight, extras, project(place, own, weight, extras))
 
 
 def solution(mesh):

time: 141 us -> 163 us (1.16)
  waiting for transfers between devices: 29.8 us -> 47.6 us
  starting transfers between devices: 14.9 us -> 26.3 us
  Pallas kernels: 35.2 us -> 31.5 us
  local copies, waits for them, and re-layouts: 4.65 us -> 2.68 us
    ppermute x4 -> x10, waiting for transfers between devices: 2.58 us -> 47.6 us  [turned(): lax.ppermute(value, axis, [(source, (source + steps) % count) for source...]
    all_to_all x1, waiting for transfers between devices: 27.2 us -> 0.01 us  [shards(): lax.all_to_all(ready, CTX, split_axis=0, concat_axis=0, tiled=True)]
    ppermute x4 -> x10, starting transfers between devices: 5.3 us -> 16.7 us  [turned(): lax.ppermute(value, axis, [(source, (source + steps) % count) for source...]
    pallas_call x3, Pallas kernels: 23.2 us -> 20.9 us  [the longest x2 11.1 us: project(): pl.pallas_call(lambda *refs: project_kernel(other, *refs), in_specs=[pl.B...]
    unnamed x11 -> x17, local copies, waits for them, and re-layouts: 3.9 us -> 2.04 us
  transfers between devices with their start and end apart: 6 -> 12, of which waited for: 3 -> 8; matrix products, arithmetic and copies ran while one was open for 2% -> 0% of each run, Pallas kernels for 21% -> 16%
where the time goes in v4:
time: 163 us; the launch traced here: 162 us
  waiting for transfers between devices  47.6 us (29%)
  blocking collectives  39.2 us (24%)
  Pallas kernels  31.5 us (19%)
  starting transfers between devices  26.3 us (16%)
  between operations  13.5 us (8%)
  local copies, waits for them, and re-layouts  2.68 us (2%)
    ppermute x10, waiting for transfers between devices, turned(): lax.ppermute(value, axis, [(source, (source + steps) % count) for source...  47.6 us
    all_to_all x1, blocking collectives, shards(): lax.all_to_all(gated.reshape(2 * ctx, chans, cols), CTX + ('zh',), split_...  39.2 us
    ppermute x10, starting transfers between devices, turned(): lax.ppermute(value, axis, [(source, (source + steps) % count) for source...  16.7 us
    pallas_call x2, Pallas kernels, project(): pl.pallas_call(lambda *refs: project_kernel(other, *refs), in_specs=[pl.B...  11.1 us
    pallas_call x1, Pallas kernels, long_mix(): pl.pallas_call(conv_kernel, grid=(1,), in_specs=[scalars] * 3 + [whole(op...  9.85 us
    all_to_all x1, starting transfers between devices, shards(): lax.all_to_all(ready, CTX, split_axis=0, concat_axis=0, tiled=True)  9.62 us
    pallas_call x1, Pallas kernels, filter_spectrum(): pl.pallas_call(lambda *refs: filter_kernel(1.0 / (outer * inner), *refs),...  5.84 us
    pallas_call x1, Pallas kernels, short_filters(): pl.pallas_call(short_kernel, grid=(blocks,), in_specs=[pl.BlockSpec(memor...  4.77 us
  transfers between devices with their start and end apart: 12, of which 8 were waited for; matrix products, arithmetic and copies ran while one was open for 0% of the time, Pallas kernels for 16%

profile of v4, /device:TPU:32, one launch (start us, length us, event | category | flops | bytes accessed | tf_op | source)
XLA Modules:
  0.0 161.6 jit_solution(8360454385637407513)
XLA Ops:
  6.5 0.0 copy-start.6
  6.5 0.0 all-gather.2.cloned.1.call-start
  6.5 1.9 %collective-permute-start = (bf16[64,1024]{1,0:T(8,128)(2,1)}, bf16[64,1024]{1,0:T(8,128)(2,1)S(1)}, u32[]{:S(2)}, u32[]{:S(2)}) collective-permute-start(bf16[64,1024]{1,0:T(8,128)(2,1)} %param.21), channel_id=1, source_target_pairs={{0,4},{4,8},{8,12},{12,0},{1,5},{5,9},{9,13},{13,1},{2,6},{6,10},{... | collective-permute-start | bytes 393224 | tf_op jit(solution)/shard_map/ppermute | solution.py:387
  8.5 2.3 %collective-permute-start.1 = (bf16[64,1024]{1,0:T(8,128)(2,1)}, bf16[64,1024]{1,0:T(8,128)(2,1)S(1)}, u32[]{:S(2)}, u32[]{:S(2)}) collective-permute-start(bf16[64,1024]{1,0:T(8,128)(2,1)} %param.21), channel_id=1, source_target_pairs={{0,8},{4,12},{8,0},{12,4},{1,9},{5,13},{9,1},{13,5},{2,10},{6,14},... | collective-permute-start | bytes 393224 | tf_op jit(solution)/shard_map/ppermute | solution.py:387
  10.7 1.1 collective-permute-start.2
  11.8 4.8 %short_filters.1 = bf16[64,16,640]{2,1,0:T(8,128)(2,1)} custom-call(f32[3,7,64]{2,1,0:T(8,128)} %bitcast.12, bf16[1024,256]{1,0:T(8,128)(2,1)} %q_ref.1, bf16[1024,256]{1,0:T(8,128)(2,1)} %k_ref.1, bf16[1024,256]{1,0:T(8,128)(2,1)} %v_ref.1), custom_call_target="tpu_custom_call" | custom-call | flops 7340032 | bytes 2621440 | tf_op jit(solution)/shard_map/short_filters/pallas_call | solution.py:97
  16.6 1.7 %collective-permute-done = bf16[64,1024]{1,0:T(8,128)(2,1)S(1)} collective-permute-done((bf16[64,1024]{1,0:T(8,128)(2,1)}, bf16[64,1024]{1,0:T(8,128)(2,1)S(1)}, u32[]{:S(2)}, u32[]{:S(2)}) %collective-permute-start) | collective-permute-done | bytes 131104 | tf_op jit(solution)/shard_map/ppermute | solution.py:387
  18.3 1.7 %collective-permute-done.1 = bf16[64,1024]{1,0:T(8,128)(2,1)S(1)} collective-permute-done((bf16[64,1024]{1,0:T(8,128)(2,1)}, bf16[64,1024]{1,0:T(8,128)(2,1)S(1)}, u32[]{:S(2)}, u32[]{:S(2)}) %collective-permute-start.1) | collective-permute-done | bytes 131104 | tf_op jit(solution)/shard_map/ppermute | solution.py:387
  20.0 2.1 %collective-permute-done.2 = bf16[64,1024]{1,0:T(8,128)(2,1)S(1)} collective-permute-done((bf16[64,1024]{1,0:T(8,128)(2,1)}, bf16[64,1024]{1,0:T(8,128)(2,1)S(1)}, u32[]{:S(2)}, u32[]{:S(2)}) %collective-permute-start.2) | collective-permute-done | bytes 131104 | tf_op jit(solution)/shard_map/ppermute | solution.py:387
  22.0 0.0 copy-done.6
  22.0 0.8 pad_maximum_fusion
  22.8 0.0 all-gather.2.cloned.1.call-update
  22.8 9.6 %all-to-all-start = ((bf16[64,16,640]{2,1,0:T(8,128)(2,1)}), bf16[64,16,640]{2,1,0:T(8,128)(2,1)S(1)}, u32[]{:S(2)}, u32[]{:S(2)}) async-start(bf16[64,16,640]{2,1,0:T(8,128)(2,1)} %short_filters.1), calls=%async_computation | async-start | bytes 2621440 | tf_op jit(solution)/shard_map/all_to_all | solution.py:405
  32.4 5.8 %filter_spectrum.1.spec_hbm = f32[1024,512]{1,0:T(8,128)} custom-call(f32[16,16384]{1,0:T(8,128)} %refs_0_.1, bf16[128,64]{1,0:T(8,128)(2,1)} %constant.39.clone.refs_1_.f_hi, bf16[128,64]{1,0:T(8,128)(2,1)} %constant.40.clone.refs_2_.f_lo, f32[64,256]{1,0:T(8,128)} %constant.41.clone.refs_3_.cos_ref, f32[64,256]{1,0:T(8,128)} %constant.42.clone.refs_4_.sin_ref, ...), custom_call_target="tpu_custom_call" | custom-call | flops 1610612736 | bytes 5242880 | tf_op jit(solution)/shard_map/filter_spectrum/pallas_call | solution.py:146
  38.3 1.4 collective-permute-start.3
  39.7 2.7 %collective-permute-start.4 = (bf16[64,1024]{1,0:T(8,128)(2,1)S(1)}, bf16[64,1024]{1,0:T(8,128)(2,1)S(1)}, u32[]{:S(2)}, u32[]{:S(2)}) collective-permute-start(bf16[64,1024]{1,0:T(8,128)(2,1)S(1)} %collective-permute-done.2), channel_id=1, source_target_pairs={{0,32},{16,48},{32,0},{48,16},{1,33},{17,49},{33,1},{49,17},{2,34}... | collective-permute-start | bytes 393224 | tf_op jit(solution)/shard_map/ppermute | solution.py:387
  42.4 1.6 collective-permute-start.5
  44.0 7.7 %collective-permute-done.3 = bf16[64,1024]{1,0:T(8,128)(2,1)S(1)} collective-permute-done((bf16[64,1024]{1,0:T(8,128)(2,1)S(1)}, bf16[64,1024]{1,0:T(8,128)(2,1)S(1)}, u32[]{:S(2)}, u32[]{:S(2)}) %collective-permute-start.3) | collective-permute-done | bytes 131104 | tf_op jit(solution)/shard_map/ppermute | solution.py:387
  51.7 9.3 %collective-permute-done.4 = bf16[64,1024]{1,0:T(8,128)(2,1)S(1)} collective-permute-done((bf16[64,1024]{1,0:T(8,128)(2,1)S(1)}, bf16[64,1024]{1,0:T(8,128)(2,1)S(1)}, u32[]{:S(2)}, u32[]{:S(2)}) %collective-permute-start.4) | collective-permute-done | bytes 131104 | tf_op jit(solution)/shard_map/ppermute | solution.py:387
  60.9 0.0 collective-permute-done.5
  61.0 0.0 copy-start.2
  61.0 1.6 collective-permute-start.6
  62.6 2.7 %collective-permute-start.7 = (bf16[256,1024]{1,0:T(8,128)(2,1)S(1)}, bf16[256,1024]{1,0:T(8,128)(2,1)S(1)}, u32[]{:S(2)}, u32[]{:S(2)}) collective-permute-start(bf16[256,1024]{1,0:T(8,128)(2,1)S(1)} %constant_dynamic-update-slice_fusion.refs_2_), channel_id=1, source_target_pairs={{0,128},{64,192},{128,0},{192,64},{1,129},{65,193},{129,1},{193,65... | collective-permute-start | bytes 1572872 | tf_op jit(solution)/shard_map/ppermute | solution.py:387
  65.3 1.4 collective-permute-start.8
  66.7 0.6 stack.27.place_ref.refs_0_
  67.3 0.0 all-to-all-done.in_ref
  67.3 0.0 copy-start
  67.3 1.1 copy-done
  68.4 9.8 %long_conv.1 = bf16[64,2,16,256]{3,2,1,0:T(8,128)(2,1)} custom-call(s32[6]{0:T(128)} %stack.27.place_ref.refs_0_, f32[16]{0:T(128)} %skip_ref.1, f32[3,7,64]{2,1,0:T(8,128)} %bitcast.13, bf16[64,16,640]{2,1,0:T(8,128)(2,1)} %copy-done, bf16[128,64]{1,0:T(8,128)(2,1)} %constant.39.clone.refs_1_.f_hi, bf16[128,64]{1,0:T(8,128)(2,1)} %constant.40.clone.refs_2_.f_lo, ...), custom_call_target="tpu_custom_call" | custom-call | flops 1048576 | bytes 1048576 | tf_op jit(solution)/shard_map/long_conv/pallas_call | solution.py:266
  78.2 1.9 %collective-permute-done.6.refs_3_ = bf16[256,1024]{1,0:T(8,128)(2,1)S(1)} collective-permute-done((bf16[256,1024]{1,0:T(8,128)(2,1)S(1)}, bf16[256,1024]{1,0:T(8,128)(2,1)S(1)}, u32[]{:S(2)}, u32[]{:S(2)}) %collective-permute-start.6) | collective-permute-done | bytes 524320 | tf_op jit(solution)/shard_map/ppermute | solution.py:387
  80.2 0.0 copy-start.3
  80.2 22.4 %collective-permute-done.7.refs_4_ = bf16[256,1024]{1,0:T(8,128)(2,1)S(1)} collective-permute-done((bf16[256,1024]{1,0:T(8,128)(2,1)S(1)}, bf16[256,1024]{1,0:T(8,128)(2,1)S(1)}, u32[]{:S(2)}, u32[]{:S(2)}) %collective-permute-start.7) | collective-permute-done | bytes 524320 | tf_op jit(solution)/shard_map/ppermute | solution.py:387
  102.6 0.0 copy-start.4
  102.6 0.9 collective-permute-done.8.refs_5_
  103.5 0.0 copy-start.5
  103.5 39.2 %all_to_all.10 = bf16[128,16,256]{2,1,0:T(8,128)(2,1)S(1)} all-to-all(bf16[128,16,256]{2,1,0:T(8,128)(2,1)} %bitcast.9), channel_id=1, replica_groups=mesh['y'=4,'x'=4,'zl'=4,'zh'=2,'core'=2] {'y','x','zl','zh'}, dimensions={0} | all-to-all | bytes 2097152 | tf_op jit(solution)/shard_map/all_to_all | solution.py:414
  142.7 0.0 copy-start.1
  142.7 0.0 collective-permute-start.9
  142.7 0.0 all-gather.2.cloned.1.call-done.refs_6_
  142.7 0.0 copy-done.2
  142.7 0.0 copy-done.3
  142.7 0.0 copy-done.4
  142.7 0.0 copy-done.5
  142.7 0.9 copy-done.1
  143.6 5.4 %project_first.1.refs_7_ = f32[256,1024]{1,0:T(8,128)} custom-call(s32[6]{0:T(128)} %stack.27.place_ref.refs_0_, bf16[64,2,16,256]{3,2,1,0:T(8,128)(2,1)} %bitcast.11, bf16[256,1024]{1,0:T(8,128)(2,1)} %copy-done.2, bf16[256,1024]{1,0:T(8,128)(2,1)} %copy-done.3, bf16[256,1024]{1,0:T(8,128)(2,1)} %copy-done.4, bf16[256,1024]{1,0:T(8,128)(2,1)} %copy-done.5, ...), custom_call_target="tpu_custom_call" | custom-call | flops 1073741824 | bytes 4194304 | tf_op jit(solution)/shard_map/project_first/pallas_call | solution.py:366
  149.0 0.0 collective-permute-done.9.refs_1_
  149.1 5.7 %project_last.1 = bf16[1024,256]{1,0:T(8,128)(2,1)} custom-call(s32[6]{0:T(128)} %stack.27.place_ref.refs_0_, bf16[64,2,16,256]{3,2,1,0:T(8,128)(2,1)} %collective-permute-done.9.refs_1_, bf16[256,1024]{1,0:T(8,128)(2,1)} %copy-done.2, bf16[256,1024]{1,0:T(8,128)(2,1)} %copy-done.3, bf16[256,1024]{1,0:T(8,128)(2,1)} %copy-done.4, ...), custom_call_target="tpu_custom_call" | custom-call | flops 1073741824 | bytes 4194304 | tf_op jit(solution)/shard_map/project_last/pallas_call | solution.py:366
  (4 shorter events, 0.0 us)
Async XLA Ops:
  6.5 15.5 %copy-start.6 = (bf16[64,1024]{1,0:T(8,128)(2,1)S(1)}, bf16[64,1024]{1,0:T(8,128)(2,1)}, u32[]{:S(2)}) copy-start(bf16[64,1024]{1,0:T(8,128)(2,1)} %param.21) | copy-start | bytes 393220
  6.5 136.1 %all-gather.2.cloned.1.call-start = ((), (), s32[]{:S(2)}) async-start(), calls=%async_computation.2 | async-start | bytes 6684672 | tf_op jit(solution)/shard_map/all_gather | solution.py:402
  6.5 11.8 %collective-permute-start = (bf16[64,1024]{1,0:T(8,128)(2,1)}, bf16[64,1024]{1,0:T(8,128)(2,1)S(1)}, u32[]{:S(2)}, u32[]{:S(2)}) collective-permute-start(bf16[64,1024]{1,0:T(8,128)(2,1)} %param.21), channel_id=1, source_target_pairs={{0,4},{4,8},{8,12},{12,0},{1,5},{5,9},{9,13},{13,1},{2,6},{6,10},{... | collective-permute-start | bytes 393224 | tf_op jit(solution)/shard_map/ppermute | solution.py:387
  8.5 11.5 %collective-permute-start.1 = (bf16[64,1024]{1,0:T(8,128)(2,1)}, bf16[64,1024]{1,0:T(8,128)(2,1)S(1)}, u32[]{:S(2)}, u32[]{:S(2)}) collective-permute-start(bf16[64,1024]{1,0:T(8,128)(2,1)} %param.21), channel_id=1, source_target_pairs={{0,8},{4,12},{8,0},{12,4},{1,9},{5,13},{9,1},{13,5},{2,10},{6,14},... | collective-permute-start | bytes 393224 | tf_op jit(solution)/shard_map/ppermute | solution.py:387
  10.7 11.3 %collective-permute-start.2 = (bf16[64,1024]{1,0:T(8,128)(2,1)}, bf16[64,1024]{1,0:T(8,128)(2,1)S(1)}, u32[]{:S(2)}, u32[]{:S(2)}) collective-permute-start(bf16[64,1024]{1,0:T(8,128)(2,1)} %param.21), channel_id=1, source_target_pairs={{0,12},{4,0},{8,4},{12,8},{1,13},{5,1},{9,5},{13,9},{2,14},{6,2},{... | collective-permute-start | bytes 393224 | tf_op jit(solution)/shard_map/ppermute | solution.py:387
  22.8 44.5 %all-to-all-start = ((bf16[64,16,640]{2,1,0:T(8,128)(2,1)}), bf16[64,16,640]{2,1,0:T(8,128)(2,1)S(1)}, u32[]{:S(2)}, u32[]{:S(2)}) async-start(bf16[64,16,640]{2,1,0:T(8,128)(2,1)} %short_filters.1), calls=%async_computation | async-start | bytes 2621440 | tf_op jit(solution)/shard_map/all_to_all | solution.py:405
  38.3 13.4 %collective-permute-start.3 = (bf16[64,1024]{1,0:T(8,128)(2,1)S(1)}, bf16[64,1024]{1,0:T(8,128)(2,1)S(1)}, u32[]{:S(2)}, u32[]{:S(2)}) collective-permute-start(bf16[64,1024]{1,0:T(8,128)(2,1)S(1)} %collective-permute-done.2), channel_id=1, source_target_pairs={{0,16},{16,32},{32,48},{48,0},{1,17},{17,33},{33,49},{49,1},{2,18}... | collective-permute-start | bytes 393224 | tf_op jit(solution)/shard_map/ppermute | solution.py:387
  39.7 21.2 %collective-permute-start.4 = (bf16[64,1024]{1,0:T(8,128)(2,1)S(1)}, bf16[64,1024]{1,0:T(8,128)(2,1)S(1)}, u32[]{:S(2)}, u32[]{:S(2)}) collective-permute-start(bf16[64,1024]{1,0:T(8,128)(2,1)S(1)} %collective-permute-done.2), channel_id=1, source_target_pairs={{0,32},{16,48},{32,0},{48,16},{1,33},{17,49},{33,1},{49,17},{2,34}... | collective-permute-start | bytes 393224 | tf_op jit(solution)/shard_map/ppermute | solution.py:387
  42.4 18.5 %collective-permute-start.5 = (bf16[64,1024]{1,0:T(8,128)(2,1)S(1)}, bf16[64,1024]{1,0:T(8,128)(2,1)S(1)}, u32[]{:S(2)}, u32[]{:S(2)}) collective-permute-start(bf16[64,1024]{1,0:T(8,128)(2,1)S(1)} %collective-permute-done.2), channel_id=1, source_target_pairs={{0,48},{16,0},{32,16},{48,32},{1,49},{17,1},{33,17},{49,33},{2,50}... | collective-permute-start | bytes 393224 | tf_op jit(solution)/shard_map/ppermute | solution.py:387
  61.0 81.7 %copy-start.2 = (bf16[256,1024]{1,0:T(8,128)(2,1)}, bf16[256,1024]{1,0:T(8,128)(2,1)S(1)}, u32[]{:S(2)}) copy-start(bf16[256,1024]{1,0:T(8,128)(2,1)S(1)} %constant_dynamic-update-slice_fusion.refs_2_) | copy-start | bytes 1572868
  61.0 19.2 %collective-permute-start.6 = (bf16[256,1024]{1,0:T(8,128)(2,1)S(1)}, bf16[256,1024]{1,0:T(8,128)(2,1)S(1)}, u32[]{:S(2)}, u32[]{:S(2)}) collective-permute-start(bf16[256,1024]{1,0:T(8,128)(2,1)S(1)} %constant_dynamic-update-slice_fusion.refs_2_), channel_id=1, source_target_pairs={{0,64},{64,128},{128,192},{192,0},{1,65},{65,129},{129,193},{193,1... | collective-permute-start | bytes 1572872 | tf_op jit(solution)/shard_map/ppermute | solution.py:387
  62.6 40.0 %collective-permute-start.7 = (bf16[256,1024]{1,0:T(8,128)(2,1)S(1)}, bf16[256,1024]{1,0:T(8,128)(2,1)S(1)}, u32[]{:S(2)}, u32[]{:S(2)}) collective-permute-start(bf16[256,1024]{1,0:T(8,128)(2,1)S(1)} %constant_dynamic-update-slice_fusion.refs_2_), channel_id=1, source_target_pairs={{0,128},{64,192},{128,0},{192,64},{1,129},{65,193},{129,1},{193,65... | collective-permute-start | bytes 1572872 | tf_op jit(solution)/shard_map/ppermute | solution.py:387
  65.3 38.2 %collective-permute-start.8 = (bf16[256,1024]{1,0:T(8,128)(2,1)S(1)}, bf16[256,1024]{1,0:T(8,128)(2,1)S(1)}, u32[]{:S(2)}, u32[]{:S(2)}) collective-permute-start(bf16[256,1024]{1,0:T(8,128)(2,1)S(1)} %constant_dynamic-update-slice_fusion.refs_2_), channel_id=1, source_target_pairs={{0,192},{64,0},{128,64},{192,128},{1,193},{65,1},{129,65},{193,129... | collective-permute-start | bytes 1572872 | tf_op jit(solution)/shard_map/ppermute | solution.py:387
  67.3 1.1 copy-start
  80.2 62.5 %copy-start.3 = (bf16[256,1024]{1,0:T(8,128)(2,1)}, bf16[256,1024]{1,0:T(8,128)(2,1)S(1)}, u32[]{:S(2)}) copy-start(bf16[256,1024]{1,0:T(8,128)(2,1)S(1)} %collective-permute-done.6.refs_3_) | copy-start | bytes 1572868
  102.6 40.1 %copy-start.4 = (bf16[256,1024]{1,0:T(8,128)(2,1)}, bf16[256,1024]{1,0:T(8,128)(2,1)S(1)}, u32[]{:S(2)}) copy-start(bf16[256,1024]{1,0:T(8,128)(2,1)S(1)} %collective-permute-done.7.refs_4_) | copy-start | bytes 1572868
  103.5 39.2 %copy-start.5 = (bf16[256,1024]{1,0:T(8,128)(2,1)}, bf16[256,1024]{1,0:T(8,128)(2,1)S(1)}, u32[]{:S(2)}) copy-start(bf16[256,1024]{1,0:T(8,128)(2,1)S(1)} %collective-permute-done.8.refs_5_) | copy-start | bytes 1572868
  142.7 1.0 copy-start.1
  142.7 6.4 %collective-permute-start.9 = (bf16[64,2,16,256]{3,2,1,0:T(8,128)(2,1)S(1)}, bf16[64,2,16,256]{3,2,1,0:T(8,128)(2,1)}, u32[]{:S(2)}, u32[]{:S(2)}) collective-permute-start(bf16[64,2,16,256]{3,2,1,0:T(8,128)(2,1)S(1)} %bitcast.10), channel_id=1, source_target_pairs={{0,1},{1,0},{2,3},{3,2},{4,5},{5,4},{6,7},{7,6},{8,9},{9,8},{10,11... | collective-permute-start | bytes 3145736 | tf_op jit(solution)/shard_map/ppermute | solution.py:387
Sparse Core Ops, SparseCore 0:
  22.9 89.9 all-gather.1

commit v5 on v4

--- a/solution.py
+++ b/solution.py
@@ -283,14 +283,13 @@
             pltpu.VMEM((2 * inner, 2 * inner), BF16),
             pltpu.SemaphoreType.DMA((3,)),
         ],
-        compiler_params=pltpu.CompilerParams(vmem_limit_bytes=VMEM_LIMIT),
+        compiler_params=pltpu.CompilerParams(vmem_limit_bytes=VMEM_LIMIT - 12 * MIB),
         cost_estimate=pl.CostEstimate(flops=2**20, bytes_accessed=2**20, transcendentals=0),
         name="long_conv",
     )(place, skip_bias, taps, *operands, *fetched)
 
 
 def project_kernel(other, place_ref, z_hbm, *refs):
-    extras, refs = refs[:4], refs[4:]
     if other:
         w_hbm, sum_hbm, out_hbm, z_ref, w_ref, g_ref, out_ref, sum_ref, sems = refs
     else:
@@ -299,9 +298,8 @@
     depth, width = w_ref.shape
     unit = 4 * chans
     size = 4 * unit
-    run = size - unit
     block = 256
-    y, x_here, zl = place_ref[4], place_ref[5], place_ref[1]
+    zl = place_ref[1]
     core = jnp.bitwise_xor(place_ref[3], other)
 
     def copy(source, target, index):
@@ -314,22 +312,10 @@
     for half in range(halves):
         for x in range(4):
             index = half * 4 + x
-            at = index * size
-            panel = half * 2 + core
-            start = pl.multiple_of((panel * 4 + x) * run, unit)
-            fetches.append(copy(w_hbm.at[pl.ds(start, run)], w_ref.at[pl.ds(at, run)], 1 + index))
-            start = pl.multiple_of(jnp.bitwise_and(x_here - x, 3) * unit, unit)
-            for turn, extra in enumerate(extras):
-
-                @pl.when(jnp.bitwise_and(y - panel, 3) == turn)
-                def _():
-                    copy(extra.at[pl.ds(start, unit)], w_ref.at[pl.ds(at + run, unit)], 9 + index)
-
-            fetches.append(
-                pltpu.make_async_copy(extras[0].at[pl.ds(start, unit)], w_ref.at[pl.ds(at + run, unit)], sems.at[9 + index])
-            )
+            start = pl.multiple_of(((half * 2 + core) * 4 + x) * size, size)
+            fetches.append(copy(w_hbm.at[pl.ds(start, size)], w_ref.at[pl.ds(index * size, size)], 1 + index))
     if other:
-        fetches.append(copy(sum_hbm, sum_ref, 17))
+        fetches.append(copy(sum_hbm, sum_ref, 9))
     arriving.wait()
     for half in range(halves):
         for x in range(4):
@@ -347,21 +333,21 @@
         part = dot(g_ref[...], w_ref[:, at])
         if other:
             out_ref[at, :] = (part + sum_ref[:, at]).T.astype(BF16)
-            leaving.append(copy(out_ref.at[at], out_hbm.at[at], 18 + index))
+            leaving.append(copy(out_ref.at[at], out_hbm.at[at], 10 + index))
         else:
             out_ref[index] = part
-            leaving.append(copy(out_ref.at[index], out_hbm.at[:, at], 18 + index))
+            leaving.append(copy(out_ref.at[index], out_hbm.at[:, at], 10 + index))
     for leave in leaving:
         leave.wait()
 
 
-def project(place, gated, weight, extras, partial=None):
+def project(place, gated, weight, partial=None):
     width = weight.shape[1]
-    depth = (weight.shape[0] + 4 * extras[0].shape[0]) // 2
+    depth = weight.shape[0] // 2
     cols = gated.shape[3]
     other = 0 if partial is None else 1
     anywhere = pl.BlockSpec(memory_space=pl.ANY)
-    operands = [gated, *extras, weight] + ([partial] if other else [])
+    operands = [gated, weight] + ([partial] if other else [])
     shape = (width, cols) if other else (cols, width)
     return pl.pallas_call(
         lambda *refs: project_kernel(other, *refs),
@@ -375,8 +361,8 @@
             pltpu.VMEM(shape, BF16) if other else pltpu.VMEM((width // 256, cols, 256), F32),
         ]
         + ([pltpu.VMEM((cols, width), F32)] if other else [])
-        + [pltpu.SemaphoreType.DMA((18 + width // 256,))],
-        compiler_params=pltpu.CompilerParams(vmem_limit_bytes=VMEM_LIMIT),
+        + [pltpu.SemaphoreType.DMA((10 + width // 256,))],
+        compiler_params=pltpu.CompilerParams(vmem_limit_bytes=VMEM_LIMIT - 12 * MIB),
         cost_estimate=pl.CostEstimate(flops=2 * depth * width * cols, bytes_accessed=2 * depth * width, transcendentals=0),
         name="project_last" if other else "project_first",
     )(place, *operands)
@@ -394,28 +380,21 @@
     tables = dft_tables(ctx, cols)
 
     taps = jnp.swapaxes(short_taps, 1, 2)
-    place = jnp.stack([lax.axis_index(name) for name in (CTX, "zl", "zh", "core", "y", "x")]).astype(jnp.int32)
+    place = jnp.stack([lax.axis_index(name) for name in (CTX, "zl", "zh", "core")]).astype(jnp.int32)
 
     pieces = [turned(out_weight, "zl", step) for step in (1, 2, 3)]
     ready = short_filters(taps, query_proj, key_proj, value_proj, ctx)
     ready, *pieces = lax.optimization_barrier((ready, *pieces))
-    weight = lax.all_gather(jnp.concatenate([out_weight, *pieces[:2]], axis=0), ("y", "x"), axis=0, tiled=True)
+    weight = lax.all_gather(jnp.concatenate([out_weight, *pieces], axis=0), ("y", "x"), axis=0, tiled=True)
 
     spectrum = filter_spectrum(long_filter, tables, ctx, cols)
     arrived = lax.all_to_all(ready, CTX, split_axis=0, concat_axis=0, tiled=True)
-
-    spectrum, last_piece = lax.optimization_barrier((spectrum, pieces[2]))
-    along_x = jnp.concatenate([last_piece] + [turned(last_piece, "x", step) for step in (1, 2, 3)], axis=0)
-    along_y = [turned(along_x, "y", step) for step in (1, 2, 3)]
-
     gated = long_mix(place, arrived, spectrum, skip_bias, taps, tables, 2)
-    gated, *along_y = lax.optimization_barrier((gated, *along_y))
-    extras = [along_x, *along_y]
     own = lax.all_to_all(
         gated.reshape(2 * ctx, chans, cols), CTX + ("zh",), split_axis=0, concat_axis=0, tiled=True
     ).reshape(ctx, 2, chans, cols)
     other = turned(own, "core", 1)
-    return project(place, other, weight, extras, project(place, own, weight, extras))
+    return project(place, other, weight, project(place, own, weight))
 
 
 def solution(mesh):

time: 163 us -> 136 us (0.83)
  waiting for transfers between devices: 47.6 us -> 33.5 us
  starting transfers between devices: 26.3 us -> 14.9 us
  Pallas kernels: 31.5 us -> 29.2 us
    ppermute x10 -> x4, waiting for transfers between devices: 47.6 us -> 5.41 us  [turned(): lax.ppermute(value, axis, [(source, (source + steps) % count) for source...]
    all_to_all x1, waiting for transfers between devices: 0.01 us -> 27.7 us  [shards(): lax.all_to_all(ready, CTX, split_axis=0, concat_axis=0, tiled=True)]
    ppermute x10 -> x4, starting transfers between devices: 16.7 us -> 5.3 us  [turned(): lax.ppermute(value, axis, [(source, (source + steps) % count) for source...]
    pallas_call x1, Pallas kernels: 9.85 us -> 7.93 us  [long_mix(): pl.pallas_call(conv_kernel, grid=(1,), in_specs=[scalars] * 3 + [whole(op...]
  transfers between devices with their start and end apart: 12 -> 6, of which waited for: 8 -> 5; matrix products, arithmetic and copies ran while one was open for 0% -> 0% of each run, Pallas kernels for 16% -> 18%
where the time goes in v5:
time: 136 us; the launch traced here: 134 us
  blocking collectives  39.7 us (29%)
  waiting for transfers between devices  33.5 us (25%)
  Pallas kernels  29.2 us (21%)
  starting transfers between devices  14.9 us (11%)
  between operations  13.6 us (10%)
  local copies, waits for them, and re-layouts  1.72 us (1%)
    all_to_all x1, blocking collectives, shards(): lax.all_to_all(gated.reshape(2 * ctx, chans, cols), CTX + ('zh',), split_...  39.7 us
    all_to_all x1, waiting for transfers between devices, shards(): lax.all_to_all(ready, CTX, split_axis=0, concat_axis=0, tiled=True)  27.7 us
    pallas_call x2, Pallas kernels, project(): pl.pallas_call(lambda *refs: project_kernel(other, *refs), in_specs=[pl.B...  10.6 us
    all_to_all x1, starting transfers between devices, shards(): lax.all_to_all(ready, CTX, split_axis=0, concat_axis=0, tiled=True)  9.63 us
    pallas_call x1, Pallas kernels, long_mix(): pl.pallas_call(conv_kernel, grid=(1,), in_specs=[scalars] * 3 + [whole(op...  7.93 us
    pallas_call x1, Pallas kernels, filter_spectrum(): pl.pallas_call(lambda *refs: filter_kernel(1.0 / (outer * inner), *refs),...  5.9 us
    ppermute x4, waiting for transfers between devices, turned(): lax.ppermute(value, axis, [(source, (source + steps) % count) for source...  5.41 us
    ppermute x4, starting transfers between devices, turned(): lax.ppermute(value, axis, [(source, (source + steps) % count) for source...  5.3 us
  transfers between devices with their start and end apart: 6, of which 5 were waited for; matrix products, arithmetic and copies ran while one was open for 0% of the time, Pallas kernels for 18%

profile of v5, /device:TPU:32, one launch (start us, length us, event | category | flops | bytes accessed | tf_op | source)
XLA Modules:
  0.0 133.5 jit_solution(1557204815075624098)
XLA Ops:
  6.5 0.0 copy-start.11
  6.5 0.0 all-gather.2.cloned.1.call-start
  6.5 1.9 %collective-permute-start = (bf16[64,1024]{1,0:T(8,128)(2,1)}, bf16[64,1024]{1,0:T(8,128)(2,1)S(1)}, u32[]{:S(2)}, u32[]{:S(2)}) collective-permute-start(bf16[64,1024]{1,0:T(8,128)(2,1)} %param.21), channel_id=1, source_target_pairs={{0,4},{4,8},{8,12},{12,0},{1,5},{5,9},{9,13},{13,1},{2,6},{6,10},{... | collective-permute-start | bytes 393224 | tf_op jit(solution)/shard_map/ppermute | solution.py:373
  8.5 2.3 %collective-permute-start.1 = (bf16[64,1024]{1,0:T(8,128)(2,1)}, bf16[64,1024]{1,0:T(8,128)(2,1)S(1)}, u32[]{:S(2)}, u32[]{:S(2)}) collective-permute-start(bf16[64,1024]{1,0:T(8,128)(2,1)} %param.21), channel_id=1, source_target_pairs={{0,8},{4,12},{8,0},{12,4},{1,9},{5,13},{9,1},{13,5},{2,10},{6,14},... | collective-permute-start | bytes 393224 | tf_op jit(solution)/shard_map/ppermute | solution.py:373
  10.7 1.1 collective-permute-start.2
  11.8 4.8 %short_filters.1 = bf16[64,16,640]{2,1,0:T(8,128)(2,1)} custom-call(f32[3,7,64]{2,1,0:T(8,128)} %bitcast.10, bf16[1024,256]{1,0:T(8,128)(2,1)} %q_ref.1, bf16[1024,256]{1,0:T(8,128)(2,1)} %k_ref.1, bf16[1024,256]{1,0:T(8,128)(2,1)} %v_ref.1), custom_call_target="tpu_custom_call" | custom-call | flops 7340032 | bytes 2621440 | tf_op jit(solution)/shard_map/short_filters/pallas_call | solution.py:97
  16.6 1.7 %collective-permute-done = bf16[64,1024]{1,0:T(8,128)(2,1)S(1)} collective-permute-done((bf16[64,1024]{1,0:T(8,128)(2,1)}, bf16[64,1024]{1,0:T(8,128)(2,1)S(1)}, u32[]{:S(2)}, u32[]{:S(2)}) %collective-permute-start) | collective-permute-done | bytes 131104 | tf_op jit(solution)/shard_map/ppermute | solution.py:373
  18.3 1.7 %collective-permute-done.1 = bf16[64,1024]{1,0:T(8,128)(2,1)S(1)} collective-permute-done((bf16[64,1024]{1,0:T(8,128)(2,1)}, bf16[64,1024]{1,0:T(8,128)(2,1)S(1)}, u32[]{:S(2)}, u32[]{:S(2)}) %collective-permute-start.1) | collective-permute-done | bytes 131104 | tf_op jit(solution)/shard_map/ppermute | solution.py:373
  20.0 2.1 %collective-permute-done.2 = bf16[64,1024]{1,0:T(8,128)(2,1)S(1)} collective-permute-done((bf16[64,1024]{1,0:T(8,128)(2,1)}, bf16[64,1024]{1,0:T(8,128)(2,1)S(1)}, u32[]{:S(2)}, u32[]{:S(2)}) %collective-permute-start.2) | collective-permute-done | bytes 131104 | tf_op jit(solution)/shard_map/ppermute | solution.py:373
  22.0 0.0 copy-done.11
  22.0 0.8 pad_maximum_fusion
  22.8 0.0 all-gather.2.cloned.1.call-update
  22.9 9.6 %all-to-all-start = ((bf16[64,16,640]{2,1,0:T(8,128)(2,1)}), bf16[64,16,640]{2,1,0:T(8,128)(2,1)S(1)}, u32[]{:S(2)}, u32[]{:S(2)}) async-start(bf16[64,16,640]{2,1,0:T(8,128)(2,1)} %short_filters.1), calls=%async_computation | async-start | bytes 2621440 | tf_op jit(solution)/shard_map/all_to_all | solution.py:391
  32.5 0.1 pad_add_fusion.place_ref.refs_0_
  32.6 0.0 copy-start.1
  32.6 0.0 copy-start.2
  32.6 0.0 copy-start.3
  32.6 0.0 copy-start.4
  32.6 0.0 copy-start.5
  32.6 0.0 copy-start.6
  32.6 0.0 copy-start.7
  32.6 0.0 copy-start.8
  32.7 0.0 copy-start.9
  32.7 0.0 copy-start.10
  32.7 5.9 %filter_spectrum.1.spec_hbm = f32[1024,512]{1,0:T(8,128)} custom-call(f32[16,16384]{1,0:T(8,128)} %refs_0_.1, bf16[128,64]{1,0:T(8,128)(2,1)} %constant.39.clone.refs_1_.f_hi, bf16[128,64]{1,0:T(8,128)(2,1)} %constant.40.clone.refs_2_.f_lo, f32[64,256]{1,0:T(8,128)} %constant.41.clone.refs_3_.cos_ref, f32[64,256]{1,0:T(8,128)} %constant.42.clone.refs_4_.sin_ref, ...), custom_call_target="tpu_custom_call" | custom-call | flops 1610612736 | bytes 5242880 | tf_op jit(solution)/shard_map/filter_spectrum/pallas_call | solution.py:146
  38.6 27.7 %all-to-all-done.in_ref = bf16[64,16,640]{2,1,0:T(8,128)(2,1)S(1)} async-done(((bf16[64,16,640]{2,1,0:T(8,128)(2,1)}), bf16[64,16,640]{2,1,0:T(8,128)(2,1)S(1)}, u32[]{:S(2)}, u32[]{:S(2)}) %all-to-all-start) | async-done | bytes 1310752 | tf_op jit(solution)/shard_map/all_to_all | solution.py:391
  66.2 0.0 copy-done.1
  66.2 0.0 copy-done.2
  66.2 0.0 copy-done.3
  66.3 0.0 copy-done.4
  66.3 0.0 copy-done.5
  66.3 0.0 copy-done.6
  66.3 0.0 copy-done.7
  66.3 0.0 copy-done.8
  66.3 0.0 copy-done.9
  66.3 0.0 copy-done.10
  66.3 0.0 copy-start
  66.3 1.7 %copy-done = f32[1024,512]{1,0:T(8,128)S(1)} copy-done((f32[1024,512]{1,0:T(8,128)S(1)}, f32[1024,512]{1,0:T(8,128)}, u32[]{:S(2)}) %copy-start) | copy-done | bytes 2097176
  68.0 7.9 %long_conv.1 = bf16[64,2,16,256]{3,2,1,0:T(8,128)(2,1)S(1)} custom-call(s32[4]{0:T(128)S(1)} %pad_add_fusion.place_ref.refs_0_, f32[16]{0:T(128)S(1)} %copy-done.10, f32[3,7,64]{2,1,0:T(8,128)S(1)} %bitcast.11, bf16[64,16,640]{2,1,0:T(8,128)(2,1)S(1)} %all-to-all-done.in_ref, bf16[128,64]{1,0:T(8,128)(2,1)S(1)} %copy-done.6, bf16[128,64]{1,0:T(8,128)(2,1)S(1)} %copy-done.7, ...), custom_call_target="tpu_custom_call" | custom-call | flops 1048576 | bytes 1048576 | tf_op jit(solution)/shard_map/long_conv/pallas_call | solution.py:266
  75.9 39.7 %all_to_all.10 = bf16[128,16,256]{2,1,0:T(8,128)(2,1)S(1)} all-to-all(bf16[128,16,256]{2,1,0:T(8,128)(2,1)S(1)} %bitcast.7), channel_id=1, replica_groups=mesh['y'=4,'x'=4,'zl'=4,'zh'=2,'core'=2] {'y','x','zl','zh'}, dimensions={0} | all-to-all | bytes 2097152 | tf_op jit(solution)/shard_map/all_to_all | solution.py:393
  115.6 0.0 collective-permute-start.3
  115.6 0.4 all-gather.2.cloned.1.call-done.refs_2_
  116.0 5.7 %project_first.1.refs_3_ = f32[256,1024]{1,0:T(8,128)S(1)} custom-call(s32[4]{0:T(128)S(1)} %pad_add_fusion.place_ref.refs_0_, bf16[64,2,16,256]{3,2,1,0:T(8,128)(2,1)S(1)} %bitcast.9, bf16[4096,1024]{1,0:T(8,128)(2,1)} %all-gather.2.cloned.1.call-done.refs_2_), custom_call_target="tpu_custom_call" | custom-call | flops 1073741824 | bytes 4194304 | tf_op jit(solution)/shard_map/project_first/pallas_call | solution.py:352
  121.7 0.0 collective-permute-done.3.refs_1_
  121.7 4.9 %project_last.1 = bf16[1024,256]{1,0:T(8,128)(2,1)} custom-call(s32[4]{0:T(128)S(1)} %pad_add_fusion.place_ref.refs_0_, bf16[64,2,16,256]{3,2,1,0:T(8,128)(2,1)S(1)} %collective-permute-done.3.refs_1_, bf16[4096,1024]{1,0:T(8,128)(2,1)} %all-gather.2.cloned.1.call-done.refs_2_, f32[256,1024]{1,0:T(8,128)S(1)} %project_first.1.refs_3_), custom_call_target="tpu_custom_call" | custom-call | flops 1073741824 | bytes 4194304 | tf_op jit(solution)/shard_map/project_last/pallas_call | solution.py:352
Async XLA Ops:
  6.5 15.5 %copy-start.11 = (bf16[64,1024]{1,0:T(8,128)(2,1)S(1)}, bf16[64,1024]{1,0:T(8,128)(2,1)}, u32[]{:S(2)}) copy-start(bf16[64,1024]{1,0:T(8,128)(2,1)} %param.21) | copy-start | bytes 393220
  6.5 109.5 %all-gather.2.cloned.1.call-start = ((), (), s32[]{:S(2)}) async-start(), calls=%async_computation.2 | async-start | bytes 8912896 | tf_op jit(solution)/shard_map/all_gather | solution.py:388
  6.5 11.8 %collective-permute-start = (bf16[64,1024]{1,0:T(8,128)(2,1)}, bf16[64,1024]{1,0:T(8,128)(2,1)S(1)}, u32[]{:S(2)}, u32[]{:S(2)}) collective-permute-start(bf16[64,1024]{1,0:T(8,128)(2,1)} %param.21), channel_id=1, source_target_pairs={{0,4},{4,8},{8,12},{12,0},{1,5},{5,9},{9,13},{13,1},{2,6},{6,10},{... | collective-permute-start | bytes 393224 | tf_op jit(solution)/shard_map/ppermute | solution.py:373
  8.5 11.5 %collective-permute-start.1 = (bf16[64,1024]{1,0:T(8,128)(2,1)}, bf16[64,1024]{1,0:T(8,128)(2,1)S(1)}, u32[]{:S(2)}, u32[]{:S(2)}) collective-permute-start(bf16[64,1024]{1,0:T(8,128)(2,1)} %param.21), channel_id=1, source_target_pairs={{0,8},{4,12},{8,0},{12,4},{1,9},{5,13},{9,1},{13,5},{2,10},{6,14},... | collective-permute-start | bytes 393224 | tf_op jit(solution)/shard_map/ppermute | solution.py:373
  10.7 11.3 %collective-permute-start.2 = (bf16[64,1024]{1,0:T(8,128)(2,1)}, bf16[64,1024]{1,0:T(8,128)(2,1)S(1)}, u32[]{:S(2)}, u32[]{:S(2)}) collective-permute-start(bf16[64,1024]{1,0:T(8,128)(2,1)} %param.21), channel_id=1, source_target_pairs={{0,12},{4,0},{8,4},{12,8},{1,13},{5,1},{9,5},{13,9},{2,14},{6,2},{... | collective-permute-start | bytes 393224 | tf_op jit(solution)/shard_map/ppermute | solution.py:373
  22.9 43.4 %all-to-all-start = ((bf16[64,16,640]{2,1,0:T(8,128)(2,1)}), bf16[64,16,640]{2,1,0:T(8,128)(2,1)S(1)}, u32[]{:S(2)}, u32[]{:S(2)}) async-start(bf16[64,16,640]{2,1,0:T(8,128)(2,1)} %short_filters.1), calls=%async_computation | async-start | bytes 2621440 | tf_op jit(solution)/shard_map/all_to_all | solution.py:391
  32.6 33.7 %copy-start.1 = (bf16[512,512]{1,0:T(8,128)(2,1)S(1)}, bf16[512,512]{1,0:T(8,128)(2,1)}, u32[]{:S(2)}) copy-start(bf16[512,512]{1,0:T(8,128)(2,1)} %constant.43.clone.refs_5_.s_hi_hbm) | copy-start | bytes 1572868
  32.6 33.7 %copy-start.2 = (bf16[512,512]{1,0:T(8,128)(2,1)S(1)}, bf16[512,512]{1,0:T(8,128)(2,1)}, u32[]{:S(2)}) copy-start(bf16[512,512]{1,0:T(8,128)(2,1)} %constant.44.clone.refs_6_.s_lo_hbm) | copy-start | bytes 1572868
  32.6 33.7 %copy-start.3 = (f32[64,256]{1,0:T(8,128)S(1)}, f32[64,256]{1,0:T(8,128)}, u32[]{:S(2)}) copy-start(f32[64,256]{1,0:T(8,128)} %constant.41.clone.refs_3_.cos_ref) | copy-start | bytes 196612
  32.6 33.7 %copy-start.4 = (f32[64,256]{1,0:T(8,128)S(1)}, f32[64,256]{1,0:T(8,128)}, u32[]{:S(2)}) copy-start(f32[64,256]{1,0:T(8,128)} %constant.42.clone.refs_4_.sin_ref) | copy-start | bytes 196612
  32.6 33.7 %copy-start.5 = (f32[3,64,7]{1,2,0:T(8,128)S(1)}, f32[3,64,7]{1,2,0:T(8,128)}, u32[]{:S(2)}) copy-start(f32[3,64,7]{1,2,0:T(8,128)} %param.18) | copy-start | bytes 16132
  32.6 33.7 %copy-start.6 = (bf16[128,64]{1,0:T(8,128)(2,1)S(1)}, bf16[128,64]{1,0:T(8,128)(2,1)}, u32[]{:S(2)}) copy-start(bf16[128,64]{1,0:T(8,128)(2,1)} %constant.39.clone.refs_1_.f_hi) | copy-start | bytes 49156
  32.6 33.7 %copy-start.7 = (bf16[128,64]{1,0:T(8,128)(2,1)S(1)}, bf16[128,64]{1,0:T(8,128)(2,1)}, u32[]{:S(2)}) copy-start(bf16[128,64]{1,0:T(8,128)(2,1)} %constant.40.clone.refs_2_.f_lo) | copy-start | bytes 49156
  32.6 33.7 %copy-start.8 = (bf16[64,128]{1,0:T(8,128)(2,1)S(1)}, bf16[64,128]{1,0:T(8,128)(2,1)}, u32[]{:S(2)}) copy-start(bf16[64,128]{1,0:T(8,128)(2,1)} %constant.45.clone.l_hi) | copy-start | bytes 49156
  32.7 33.6 %copy-start.9 = (bf16[64,128]{1,0:T(8,128)(2,1)S(1)}, bf16[64,128]{1,0:T(8,128)(2,1)}, u32[]{:S(2)}) copy-start(bf16[64,128]{1,0:T(8,128)(2,1)} %constant.46.clone.l_lo) | copy-start | bytes 49156
  32.7 33.6 %copy-start.10 = (f32[16]{0:T(128)S(1)}, f32[16]{0:T(128)}, u32[]{:S(2)}) copy-start(f32[16]{0:T(128)} %skip_ref.1) | copy-start | bytes 196
  66.3 1.7 %copy-start = (f32[1024,512]{1,0:T(8,128)S(1)}, f32[1024,512]{1,0:T(8,128)}, u32[]{:S(2)}) copy-start(f32[1024,512]{1,0:T(8,128)} %filter_spectrum.1.spec_hbm) | copy-start | bytes 6291460
  115.6 6.1 %collective-permute-start.3 = (bf16[64,2,16,256]{3,2,1,0:T(8,128)(2,1)S(1)}, bf16[64,2,16,256]{3,2,1,0:T(8,128)(2,1)S(1)}, u32[]{:S(2)}, u32[]{:S(2)}) collective-permute-start(bf16[64,2,16,256]{3,2,1,0:T(8,128)(2,1)S(1)} %bitcast.8), channel_id=1, source_target_pairs={{0,1},{1,0},{2,3},{3,2},{4,5},{5,4},{6,7},{7,6},{8,9},{9,8},{10,11... | collective-permute-start | bytes 3145736 | tf_op jit(solution)/shard_map/ppermute | solution.py:373
Sparse Core Ops, SparseCore 0:
  23.0 92.9 all-gather.1

commit v6 on v5

--- a/solution.py
+++ b/solution.py
@@ -283,23 +283,25 @@
             pltpu.VMEM((2 * inner, 2 * inner), BF16),
             pltpu.SemaphoreType.DMA((3,)),
         ],
-        compiler_params=pltpu.CompilerParams(vmem_limit_bytes=VMEM_LIMIT - 12 * MIB),
+        compiler_params=pltpu.CompilerParams(vmem_limit_bytes=VMEM_LIMIT),
         cost_estimate=pl.CostEstimate(flops=2**20, bytes_accessed=2**20, transcendentals=0),
         name="long_conv",
     )(place, skip_bias, taps, *operands, *fetched)
 
 
 def project_kernel(other, place_ref, z_hbm, *refs):
+    by_y, by_x, refs = refs[:4], refs[4:8], refs[8:]
     if other:
-        w_hbm, sum_hbm, out_hbm, z_ref, w_ref, g_ref, out_ref, sum_ref, sems = refs
+        sum_hbm, out_hbm, z_ref, w_ref, g_ref, out_ref, sum_ref, sems = refs
     else:
-        w_hbm, out_hbm, z_ref, w_ref, g_ref, out_ref, sems = refs
+        out_hbm, z_ref, w_ref, g_ref, out_ref, sems = refs
     _, halves, chans, cols = z_ref.shape
     depth, width = w_ref.shape
     unit = 4 * chans
     size = 4 * unit
+    run = size // 2
     block = 256
-    zl = place_ref[1]
+    zl, y, x_here = place_ref[1], place_ref[4], place_ref[5]
     core = jnp.bitwise_xor(place_ref[3], other)
 
     def copy(source, target, index):
@@ -312,10 +314,21 @@
     for half in range(halves):
         for x in range(4):
             index = half * 4 + x
-            start = pl.multiple_of(((half * 2 + core) * 4 + x) * size, size)
-            fetches.append(copy(w_hbm.at[pl.ds(start, size)], w_ref.at[pl.ds(index * size, size)], 1 + index))
+            along_y = jnp.bitwise_and(y - (half * 2 + core), 3)
+            along_x = jnp.bitwise_and(x_here - x, 3)
+            for part, (held, pick, row) in enumerate(((by_y, along_y, along_x), (by_x, along_x, along_y))):
+                source = pl.ds(pl.multiple_of(row * run, run), run)
+                target = w_ref.at[pl.ds(index * size + part * run, run)]
+                sem = 1 + 2 * index + part
+                for turn in range(4):
+
+                    @pl.when(pick == turn)
+                    def _():
+                        copy(held[turn].at[source], target, sem)
+
+                fetches.append(pltpu.make_async_copy(held[0].at[source], target, sems.at[sem]))
     if other:
-        fetches.append(copy(sum_hbm, sum_ref, 9))
+        fetches.append(copy(sum_hbm, sum_ref, 17))
     arriving.wait()
     for half in range(halves):
         for x in range(4):
@@ -333,21 +346,21 @@
         part = dot(g_ref[...], w_ref[:, at])
         if other:
             out_ref[at, :] = (part + sum_ref[:, at]).T.astype(BF16)
-            leaving.append(copy(out_ref.at[at], out_hbm.at[at], 10 + index))
+            leaving.append(copy(out_ref.at[at], out_hbm.at[at], 18 + index))
         else:
             out_ref[index] = part
-            leaving.append(copy(out_ref.at[index], out_hbm.at[:, at], 10 + index))
+            leaving.append(copy(out_ref.at[index], out_hbm.at[:, at], 18 + index))
     for leave in leaving:
         leave.wait()
 
 
 def project(place, gated, weight, partial=None):
-    width = weight.shape[1]
-    depth = weight.shape[0] // 2
+    width = weight[0].shape[1]
+    depth = 4 * weight[0].shape[0]
     cols = gated.shape[3]
     other = 0 if partial is None else 1
     anywhere = pl.BlockSpec(memory_space=pl.ANY)
-    operands = [gated, weight] + ([partial] if other else [])
+    operands = [gated, *weight] + ([partial] if other else [])
     shape = (width, cols) if other else (cols, width)
     return pl.pallas_call(
         lambda *refs: project_kernel(other, *refs),
@@ -361,7 +374,7 @@
             pltpu.VMEM(shape, BF16) if other else pltpu.VMEM((width // 256, cols, 256), F32),
         ]
         + ([pltpu.VMEM((cols, width), F32)] if other else [])
-        + [pltpu.SemaphoreType.DMA((10 + width // 256,))],
+        + [pltpu.SemaphoreType.DMA((18 + width // 256,))],
         compiler_params=pltpu.CompilerParams(vmem_limit_bytes=VMEM_LIMIT - 12 * MIB),
         cost_estimate=pl.CostEstimate(flops=2 * depth * width * cols, bytes_accessed=2 * depth * width, transcendentals=0),
         name="project_last" if other else "project_first",
@@ -380,16 +393,26 @@
     tables = dft_tables(ctx, cols)
 
     taps = jnp.swapaxes(short_taps, 1, 2)
-    place = jnp.stack([lax.axis_index(name) for name in (CTX, "zl", "zh", "core")]).astype(jnp.int32)
+    place = jnp.stack([lax.axis_index(name) for name in (CTX, "zl", "zh", "core", "y", "x")]).astype(jnp.int32)
 
     pieces = [turned(out_weight, "zl", step) for step in (1, 2, 3)]
     ready = short_filters(taps, query_proj, key_proj, value_proj, ctx)
-    ready, *pieces = lax.optimization_barrier((ready, *pieces))
-    weight = lax.all_gather(jnp.concatenate([out_weight, *pieces], axis=0), ("y", "x"), axis=0, tiled=True)
-
+    arrived = lax.all_to_all(ready, CTX, split_axis=0, concat_axis=0, tiled=True)
+
+    first_half = jnp.concatenate([out_weight, pieces[0]], axis=0)
+    second_half = jnp.concatenate(pieces[1:], axis=0)
+    run_x = jnp.concatenate([first_half] + [turned(first_half, "x", step) for step in (1, 2, 3)], axis=0)
+    run_y = jnp.concatenate([second_half] + [turned(second_half, "y", step) for step in (1, 2, 3)], axis=0)
+    near = [turned(run_x, "y", 1), turned(run_x, "y", 3), turned(run_y, "x", 1), turned(run_y, "x", 3)]
+
+    long_filter, run_x, run_y = lax.optimization_barrier((long_filter, run_x, run_y))
     spectrum = filter_spectrum(long_filter, tables, ctx, cols)
-    arrived = lax.all_to_all(ready, CTX, split_axis=0, concat_axis=0, tiled=True)
     gated = long_mix(place, arrived, spectrum, skip_bias, taps, tables, 2)
+    gated, run_x, run_y, *near = lax.optimization_barrier((gated, run_x, run_y, *near))
+    by_y = [run_x, near[0], turned(run_x, "y", 2), near[1]]
+    by_x = [run_y, near[2], turned(run_y, "x", 2), near[3]]
+    weight = by_y + by_x
+
     own = lax.all_to_all(
         gated.reshape(2 * ctx, chans, cols), CTX + ("zh",), split_axis=0, concat_axis=0, tiled=True
     ).reshape(ctx, 2, chans, cols)

time: 136 us -> 166 us (1.22)
  waiting for transfers between devices: 33.5 us -> 78.5 us
  blocking collectives: 39.7 us -> 0 us
  starting transfers between devices: 14.9 us -> 46.6 us
  between operations: 13.6 us -> 0.31 us
  local copies, waits for them, and re-layouts: 1.72 us -> 8.67 us
    ppermute x4 -> x16, waiting for transfers between devices: 5.41 us -> 56 us  [turned(): lax.ppermute(value, axis, [(source, (source + steps) % count) for source...]
    all_to_all x1 -> x0, blocking collectives: 39.7 us -> none  [shards(): lax.all_to_all(gated.reshape(2 * ctx, chans, cols), CTX + ('zh',), split_...]
    all_to_all x1, waiting for transfers between devices: 27.7 us -> 0.01 us  [shards(): lax.all_to_all(ready, CTX, split_axis=0, concat_axis=0, tiled=True)]
    all_to_all x0 -> x1, waiting for transfers between devices: none -> 22.4 us  [shards(): lax.all_to_all(gated.reshape(2 * ctx, chans, cols), CTX + ('zh',), split_...]
    ppermute x4 -> x16, starting transfers between devices: 5.3 us -> 24.8 us  [turned(): lax.ppermute(value, axis, [(source, (source + steps) % count) for source...]
    all_to_all x0 -> x1, starting transfers between devices: none -> 9.89 us  [shards(): lax.all_to_all(gated.reshape(2 * ctx, chans, cols), CTX + ('zh',), split_...]
    unnamed x24 -> x22, local copies, waits for them, and re-layouts: 1.72 us -> 6.58 us
    all_to_all x1, starting transfers between devices: 9.63 us -> 12 us  [shards(): lax.all_to_all(ready, CTX, split_axis=0, concat_axis=0, tiled=True)]
  transfers between devices with their start and end apart: 6 -> 18, of which waited for: 5 -> 11; matrix products, arithmetic and copies ran while one was open for 0% -> 3% of each run, Pallas kernels for 18% -> 13%
where the time goes in v6:
time: 166 us; the launch traced here: 165 us
  waiting for transfers between devices  78.5 us (47%)
  starting transfers between devices  46.6 us (28%)
  Pallas kernels  30.5 us (18%)
  local copies, waits for them, and re-layouts  8.67 us (5%)
    ppermute x16, waiting for transfers between devices, turned(): lax.ppermute(value, axis, [(source, (source + steps) % count) for source...  56 us
    ppermute x16, starting transfers between devices, turned(): lax.ppermute(value, axis, [(source, (source + steps) % count) for source...  24.8 us
    all_to_all x1, waiting for transfers between devices, shards(): lax.all_to_all(gated.reshape(2 * ctx, chans, cols), CTX + ('zh',), split_...  22.4 us
    all_to_all x1, starting transfers between devices, shards(): lax.all_to_all(ready, CTX, split_axis=0, concat_axis=0, tiled=True)  12 us
    pallas_call x2, Pallas kernels, project(): pl.pallas_call(lambda *refs: project_kernel(other, *refs), in_specs=[pl.B...  10.5 us
    all_to_all x1, starting transfers between devices, shards(): lax.all_to_all(gated.reshape(2 * ctx, chans, cols), CTX + ('zh',), split_...  9.89 us
    pallas_call x1, Pallas kernels, long_mix(): pl.pallas_call(conv_kernel, grid=(1,), in_specs=[scalars] * 3 + [whole(op...  9.43 us
    unnamed x22, local copies, waits for them, and re-layouts  6.58 us
  transfers between devices with their start and end apart: 18, of which 11 were waited for; matrix products, arithmetic and copies ran while one was open for 3% of the time, Pallas kernels for 13%

profile of v6, /device:TPU:32, one launch (start us, length us, event | category | flops | bytes accessed | tf_op | source)
XLA Modules:
  0.0 164.6 jit_solution(8882228112412750634)
XLA Ops:
  0.0 4.8 %short_filters.1 = bf16[64,16,640]{2,1,0:T(8,128)(2,1)} custom-call(f32[3,7,64]{2,1,0:T(8,128)} %bitcast.12, bf16[1024,256]{1,0:T(8,128)(2,1)} %q_ref.1, bf16[1024,256]{1,0:T(8,128)(2,1)} %k_ref.1, bf16[1024,256]{1,0:T(8,128)(2,1)} %v_ref.1), custom_call_target="tpu_custom_call" | custom-call | flops 7340032 | bytes 2621440 | tf_op jit(solution)/shard_map/short_filters/pallas_call | solution.py:97
  4.8 12.0 %all-to-all-start = ((bf16[64,16,640]{2,1,0:T(8,128)(2,1)}), bf16[64,16,640]{2,1,0:T(8,128)(2,1)}, u32[]{:S(2)}, u32[]{:S(2)}) async-start(bf16[64,16,640]{2,1,0:T(8,128)(2,1)} %short_filters.1), calls=%async_computation | async-start | bytes 2621440 | tf_op jit(solution)/shard_map/all_to_all | solution.py:400
  16.8 2.4 %collective-permute-start.4 = (bf16[64,1024]{1,0:T(8,128)(2,1)S(1)}, bf16[64,1024]{1,0:T(8,128)(2,1)S(1)}, u32[]{:S(2)}, u32[]{:S(2)}) collective-permute-start(bf16[64,1024]{1,0:T(8,128)(2,1)S(1)} %copy-done.7), channel_id=1, source_target_pairs={{0,8},{4,12},{8,0},{12,4},{1,9},{5,13},{9,1},{13,5},{2,10},{6,14},... | collective-permute-start | bytes 393224 | tf_op jit(solution)/shard_map/ppermute | solution.py:386
  19.2 0.6 collective-permute-start.5
  19.8 32.8 %collective-permute-done.4 = bf16[64,1024]{1,0:T(8,128)(2,1)S(1)} collective-permute-done((bf16[64,1024]{1,0:T(8,128)(2,1)S(1)}, bf16[64,1024]{1,0:T(8,128)(2,1)S(1)}, u32[]{:S(2)}, u32[]{:S(2)}) %collective-permute-start.4) | collective-permute-done | bytes 131104 | tf_op jit(solution)/shard_map/ppermute | solution.py:386
  52.6 0.7 constant_dynamic-update-slice_fusion.8
  53.3 1.2 collective-permute-done.5
  54.5 0.7 constant_dynamic-update-slice_fusion.7
  55.2 1.5 collective-permute-start.6
  56.7 0.0 collective-permute-start
  56.7 2.9 %collective-permute-start.7 = (bf16[128,1024]{1,0:T(8,128)(2,1)S(1)}, bf16[128,1024]{1,0:T(8,128)(2,1)S(1)}, u32[]{:S(2)}, u32[]{:S(2)}) collective-permute-start(bf16[128,1024]{1,0:T(8,128)(2,1)S(1)} %get-tuple-element.25), channel_id=1, source_target_pairs={{0,128},{64,192},{128,0},{192,64},{1,129},{65,193},{129,1},{193,65... | collective-permute-start | bytes 786440 | tf_op jit(solution)/shard_map/ppermute | solution.py:386
  59.6 1.4 collective-permute-start.8
  61.0 0.6 collective-permute-done
  61.6 2.8 %collective-permute-start.3 = (bf16[128,1024]{1,0:T(8,128)(2,1)S(1)}, bf16[128,1024]{1,0:T(8,128)(2,1)S(1)}, u32[]{:S(2)}, u32[]{:S(2)}) collective-permute-start(bf16[128,1024]{1,0:T(8,128)(2,1)S(1)} %get-tuple-element.29), channel_id=1, source_target_pairs={{0,48},{16,0},{32,16},{48,32},{1,49},{17,1},{33,17},{49,33},{2,50}... | collective-permute-start | bytes 786440 | tf_op jit(solution)/shard_map/ppermute | solution.py:386
  64.5 0.8 collective-permute-start.2
  65.3 0.0 collective-permute-done.6
  65.3 0.9 collective-permute-start.1
  66.2 0.7 constant_dynamic-update-slice_fusion.11
  66.9 3.3 %collective-permute-done.7 = bf16[128,1024]{1,0:T(8,128)(2,1)S(1)} collective-permute-done((bf16[128,1024]{1,0:T(8,128)(2,1)S(1)}, bf16[128,1024]{1,0:T(8,128)(2,1)S(1)}, u32[]{:S(2)}, u32[]{:S(2)}) %collective-permute-start.7) | collective-permute-done | bytes 262176 | tf_op jit(solution)/shard_map/ppermute | solution.py:386
  70.2 0.7 constant_dynamic-update-slice_fusion.10
  70.9 0.0 collective-permute-done.8
  70.9 0.7 constant_dynamic-update-slice_fusion.9.refs_6_
  71.7 2.8 %collective-permute-start.12 = (bf16[512,1024]{1,0:T(8,128)(2,1)}, bf16[512,1024]{1,0:T(8,128)(2,1)}, u32[]{:S(2)}, u32[]{:S(2)}) collective-permute-start(bf16[512,1024]{1,0:T(8,128)(2,1)} %constant_dynamic-update-slice_fusion.9.refs_6_), channel_id=1, source_target_pairs={{0,48},{16,0},{32,16},{48,32},{1,49},{17,1},{33,17},{49,33},{2,50}... | collective-permute-start | bytes 3145736 | tf_op jit(solution)/shard_map/ppermute | solution.py:386
  74.4 0.0 collective-permute-start.11
  74.4 3.3 %collective-permute-done.1 = bf16[128,1024]{1,0:T(8,128)(2,1)S(1)} collective-permute-done((bf16[128,1024]{1,0:T(8,128)(2,1)S(1)}, bf16[128,1024]{1,0:T(8,128)(2,1)S(1)}, u32[]{:S(2)}, u32[]{:S(2)}) %collective-permute-start.1) | collective-permute-done | bytes 262176 | tf_op jit(solution)/shard_map/ppermute | solution.py:386
  77.8 0.0 collective-permute-done.3
  77.8 1.0 collective-permute-start.10
  78.8 1.2 collective-permute-start.9
  80.1 0.7 stack.27.place_ref.refs_0_
  80.7 5.8 %filter_spectrum.1.spec_hbm = f32[1024,512]{1,0:T(8,128)} custom-call(f32[16,16384]{1,0:T(8,128)} %refs_0_, bf16[128,64]{1,0:T(8,128)(2,1)} %constant.39.clone.refs_1_.f_hi, bf16[128,64]{1,0:T(8,128)(2,1)} %constant.40.clone.refs_2_.f_lo, f32[64,256]{1,0:T(8,128)} %constant.41.clone.refs_3_.cos_ref, f32[64,256]{1,0:T(8,128)} %constant.42.clone.refs_4_.sin_ref, ...), custom_call_target="tpu_custom_call" | custom-call | flops 1610612736 | bytes 5242880 | tf_op jit(solution)/shard_map/filter_spectrum/pallas_call | solution.py:146
  86.5 0.0 all-to-all-done.in_ref
  86.5 9.4 %long_conv.1 = bf16[64,2,16,256]{3,2,1,0:T(8,128)(2,1)} custom-call(s32[6]{0:T(128)} %stack.27.place_ref.refs_0_, f32[16]{0:T(128)} %skip_ref.1, f32[3,7,64]{2,1,0:T(8,128)} %bitcast.13, bf16[64,16,640]{2,1,0:T(8,128)(2,1)} %all-to-all-done.in_ref, bf16[128,64]{1,0:T(8,128)(2,1)} %constant.39.clone.refs_1_.f_hi, ...), custom_call_target="tpu_custom_call" | custom-call | flops 1048576 | bytes 1048576 | tf_op jit(solution)/shard_map/long_conv/pallas_call | solution.py:266
  95.9 0.0 collective-permute-done.12.refs_9_
  95.9 3.6 %collective-permute-done.11.refs_7_ = bf16[512,1024]{1,0:T(8,128)(2,1)} collective-permute-done((bf16[512,1024]{1,0:T(8,128)(2,1)}, bf16[512,1024]{1,0:T(8,128)(2,1)}, u32[]{:S(2)}, u32[]{:S(2)}) %collective-permute-start.11) | collective-permute-done | bytes 1048608 | tf_op jit(solution)/shard_map/ppermute | solution.py:386
  99.5 1.8 %collective-permute-done.10.refs_5_ = bf16[512,1024]{1,0:T(8,128)(2,1)S(1)} collective-permute-done((bf16[512,1024]{1,0:T(8,128)(2,1)S(1)}, bf16[512,1024]{1,0:T(8,128)(2,1)S(1)}, u32[]{:S(2)}, u32[]{:S(2)}) %collective-permute-start.10) | collective-permute-done | bytes 1048608 | tf_op jit(solution)/shard_map/ppermute | solution.py:386
  101.3 2.1 %collective-permute-done.9.refs_3_ = bf16[512,1024]{1,0:T(8,128)(2,1)S(1)} collective-permute-done((bf16[512,1024]{1,0:T(8,128)(2,1)S(1)}, bf16[512,1024]{1,0:T(8,128)(2,1)S(1)}, u32[]{:S(2)}, u32[]{:S(2)}) %collective-permute-start.9) | collective-permute-done | bytes 1048608 | tf_op jit(solution)/shard_map/ppermute | solution.py:386
  103.4 1.0 copy-done.2
  104.4 9.9 %all-to-all-start.1 = ((bf16[128,16,256]{2,1,0:T(8,128)(2,1)}), bf16[128,16,256]{2,1,0:T(8,128)(2,1)S(1)}, u32[]{:S(2)}, u32[]{:S(2)}) async-start(bf16[128,16,256]{2,1,0:T(8,128)(2,1)} %bitcast.11), calls=%async_computation.1 | async-start | bytes 2097152 | tf_op jit(solution)/shard_map/all_to_all | solution.py:416
  114.3 3.4 %collective-permute-start.14 = (bf16[512,1024]{1,0:T(8,128)(2,1)S(1)}, bf16[512,1024]{1,0:T(8,128)(2,1)}, u32[]{:S(2)}, u32[]{:S(2)}) collective-permute-start(bf16[512,1024]{1,0:T(8,128)(2,1)S(1)} %constant_dynamic-update-slice_fusion.2.refs_2_), channel_id=1, source_target_pairs={{0,128},{64,192},{128,0},{192,64},{1,129},{65,193},{129,1},{193,65... | collective-permute-start | bytes 3145736 | tf_op jit(solution)/shard_map/ppermute | solution.py:386
  117.6 3.1 %collective-permute-start.15 = (bf16[512,1024]{1,0:T(8,128)(2,1)}, bf16[512,1024]{1,0:T(8,128)(2,1)}, u32[]{:S(2)}, u32[]{:S(2)}) collective-permute-start(bf16[512,1024]{1,0:T(8,128)(2,1)} %constant_dynamic-update-slice_fusion.9.refs_6_), channel_id=1, source_target_pairs={{0,32},{16,48},{32,0},{48,16},{1,33},{17,49},{33,1},{49,17},{2,34}... | collective-permute-start | bytes 3145736 | tf_op jit(solution)/shard_map/ppermute | solution.py:386
  120.7 22.4 %all-to-all-done.1 = bf16[128,16,256]{2,1,0:T(8,128)(2,1)S(1)} async-done(((bf16[128,16,256]{2,1,0:T(8,128)(2,1)}), bf16[128,16,256]{2,1,0:T(8,128)(2,1)S(1)}, u32[]{:S(2)}, u32[]{:S(2)}) %all-to-all-start.1) | async-done | bytes 1048608 | tf_op jit(solution)/shard_map/all_to_all | solution.py:416
  143.2 6.4 %collective-permute-done.14.refs_4_ = bf16[512,1024]{1,0:T(8,128)(2,1)} collective-permute-done((bf16[512,1024]{1,0:T(8,128)(2,1)S(1)}, bf16[512,1024]{1,0:T(8,128)(2,1)}, u32[]{:S(2)}, u32[]{:S(2)}) %collective-permute-start.14) | collective-permute-done | bytes 1048608 | tf_op jit(solution)/shard_map/ppermute | solution.py:386
  149.5 0.9 collective-permute-done.15.refs_8_
  150.4 1.2 copy-done.3
  151.7 5.7 %project_first.1.refs_10_ = f32[256,1024]{1,0:T(8,128)S(1)} custom-call(s32[6]{0:T(128)S(1)} %copy-done.6, bf16[64,2,16,256]{3,2,1,0:T(8,128)(2,1)S(1)} %bitcast.10, bf16[512,1024]{1,0:T(8,128)(2,1)S(1)} %constant_dynamic-update-slice_fusion.2.refs_2_, bf16[512,1024]{1,0:T(8,128)(2,1)S(1)} %copy-done.3, bf16[512,1024]{1,0:T(8,128)(2,1)} %collective-permute-done.14.refs_4_, ...), custom_call_target="tpu_custom_call" | custom-call | flops 1073741824 | bytes 4194304 | tf_op jit(solution)/shard_map/project_first/pallas_call | solution.py:365
  157.4 1.0 copy-done.5
  158.4 1.2 copy-done.1
  159.6 4.8 %project_last.1 = bf16[1024,256]{1,0:T(8,128)(2,1)} custom-call(s32[6]{0:T(128)S(1)} %copy-done.6, bf16[64,2,16,256]{3,2,1,0:T(8,128)(2,1)S(1)} %collective-permute-done.13.refs_1_, bf16[512,1024]{1,0:T(8,128)(2,1)S(1)} %constant_dynamic-update-slice_fusion.2.refs_2_, bf16[512,1024]{1,0:T(8,128)(2,1)S(1)} %copy-done.4, ...), custom_call_target="tpu_custom_call" | custom-call | flops 1073741824 | bytes 4194304 | tf_op jit(solution)/shard_map/project_last/pallas_call | solution.py:365
  (20 shorter events, 0.1 us)
Async XLA Ops:
  4.8 12.0 %copy-start.7 = (bf16[64,1024]{1,0:T(8,128)(2,1)S(1)}, bf16[64,1024]{1,0:T(8,128)(2,1)}, u32[]{:S(2)}) copy-start(bf16[64,1024]{1,0:T(8,128)(2,1)} %param.21) | copy-start | bytes 393220
  4.8 81.7 %all-to-all-start = ((bf16[64,16,640]{2,1,0:T(8,128)(2,1)}), bf16[64,16,640]{2,1,0:T(8,128)(2,1)}, u32[]{:S(2)}, u32[]{:S(2)}) async-start(bf16[64,16,640]{2,1,0:T(8,128)(2,1)} %short_filters.1), calls=%async_computation | async-start | bytes 2621440 | tf_op jit(solution)/shard_map/all_to_all | solution.py:400
  16.8 35.8 %collective-permute-start.4 = (bf16[64,1024]{1,0:T(8,128)(2,1)S(1)}, bf16[64,1024]{1,0:T(8,128)(2,1)S(1)}, u32[]{:S(2)}, u32[]{:S(2)}) collective-permute-start(bf16[64,1024]{1,0:T(8,128)(2,1)S(1)} %copy-done.7), channel_id=1, source_target_pairs={{0,8},{4,12},{8,0},{12,4},{1,9},{5,13},{9,1},{13,5},{2,10},{6,14},... | collective-permute-start | bytes 393224 | tf_op jit(solution)/shard_map/ppermute | solution.py:386
  19.2 35.3 %collective-permute-start.5 = (bf16[64,1024]{1,0:T(8,128)(2,1)S(1)}, bf16[64,1024]{1,0:T(8,128)(2,1)S(1)}, u32[]{:S(2)}, u32[]{:S(2)}) collective-permute-start(bf16[64,1024]{1,0:T(8,128)(2,1)S(1)} %copy-done.7), channel_id=1, source_target_pairs={{0,12},{4,0},{8,4},{12,8},{1,13},{5,1},{9,5},{13,9},{2,14},{6,2},{... | collective-permute-start | bytes 393224 | tf_op jit(solution)/shard_map/ppermute | solution.py:386
  55.2 10.1 %collective-permute-start.6 = (bf16[128,1024]{1,0:T(8,128)(2,1)S(1)}, bf16[128,1024]{1,0:T(8,128)(2,1)S(1)}, u32[]{:S(2)}, u32[]{:S(2)}) collective-permute-start(bf16[128,1024]{1,0:T(8,128)(2,1)S(1)} %get-tuple-element.25), channel_id=1, source_target_pairs={{0,64},{64,128},{128,192},{192,0},{1,65},{65,129},{129,193},{193,1... | collective-permute-start | bytes 786440 | tf_op jit(solution)/shard_map/ppermute | solution.py:386
  56.7 5.0 %collective-permute-start = (bf16[64,1024]{1,0:T(8,128)(2,1)S(1)}, bf16[64,1024]{1,0:T(8,128)(2,1)S(1)}, u32[]{:S(2)}, u32[]{:S(2)}) collective-permute-start(bf16[64,1024]{1,0:T(8,128)(2,1)S(1)} %copy-done.7), channel_id=1, source_target_pairs={{0,4},{4,8},{8,12},{12,0},{1,5},{5,9},{9,13},{13,1},{2,6},{6,10},{... | collective-permute-start | bytes 393224 | tf_op jit(solution)/shard_map/ppermute | solution.py:386
  56.7 13.5 %collective-permute-start.7 = (bf16[128,1024]{1,0:T(8,128)(2,1)S(1)}, bf16[128,1024]{1,0:T(8,128)(2,1)S(1)}, u32[]{:S(2)}, u32[]{:S(2)}) collective-permute-start(bf16[128,1024]{1,0:T(8,128)(2,1)S(1)} %get-tuple-element.25), channel_id=1, source_target_pairs={{0,128},{64,192},{128,0},{192,64},{1,129},{65,193},{129,1},{193,65... | collective-permute-start | bytes 786440 | tf_op jit(solution)/shard_map/ppermute | solution.py:386
  59.6 11.4 %collective-permute-start.8 = (bf16[128,1024]{1,0:T(8,128)(2,1)S(1)}, bf16[128,1024]{1,0:T(8,128)(2,1)S(1)}, u32[]{:S(2)}, u32[]{:S(2)}) collective-permute-start(bf16[128,1024]{1,0:T(8,128)(2,1)S(1)} %get-tuple-element.25), channel_id=1, source_target_pairs={{0,192},{64,0},{128,64},{192,128},{1,193},{65,1},{129,65},{193,129... | collective-permute-start | bytes 786440 | tf_op jit(solution)/shard_map/ppermute | solution.py:386
  61.6 16.1 %collective-permute-start.3 = (bf16[128,1024]{1,0:T(8,128)(2,1)S(1)}, bf16[128,1024]{1,0:T(8,128)(2,1)S(1)}, u32[]{:S(2)}, u32[]{:S(2)}) collective-permute-start(bf16[128,1024]{1,0:T(8,128)(2,1)S(1)} %get-tuple-element.29), channel_id=1, source_target_pairs={{0,48},{16,0},{32,16},{48,32},{1,49},{17,1},{33,17},{49,33},{2,50}... | collective-permute-start | bytes 786440 | tf_op jit(solution)/shard_map/ppermute | solution.py:386
  64.5 13.3 %collective-permute-start.2 = (bf16[128,1024]{1,0:T(8,128)(2,1)S(1)}, bf16[128,1024]{1,0:T(8,128)(2,1)S(1)}, u32[]{:S(2)}, u32[]{:S(2)}) collective-permute-start(bf16[128,1024]{1,0:T(8,128)(2,1)S(1)} %get-tuple-element.29), channel_id=1, source_target_pairs={{0,32},{16,48},{32,0},{48,16},{1,33},{17,49},{33,1},{49,17},{2,34}... | collective-permute-start | bytes 786440 | tf_op jit(solution)/shard_map/ppermute | solution.py:386
  65.3 12.4 %collective-permute-start.1 = (bf16[128,1024]{1,0:T(8,128)(2,1)S(1)}, bf16[128,1024]{1,0:T(8,128)(2,1)S(1)}, u32[]{:S(2)}, u32[]{:S(2)}) collective-permute-start(bf16[128,1024]{1,0:T(8,128)(2,1)S(1)} %get-tuple-element.29), channel_id=1, source_target_pairs={{0,16},{16,32},{32,48},{48,0},{1,17},{17,33},{33,49},{49,1},{2,18}... | collective-permute-start | bytes 786440 | tf_op jit(solution)/shard_map/ppermute | solution.py:386
  71.7 24.3 %collective-permute-start.12 = (bf16[512,1024]{1,0:T(8,128)(2,1)}, bf16[512,1024]{1,0:T(8,128)(2,1)}, u32[]{:S(2)}, u32[]{:S(2)}) collective-permute-start(bf16[512,1024]{1,0:T(8,128)(2,1)} %constant_dynamic-update-slice_fusion.9.refs_6_), channel_id=1, source_target_pairs={{0,48},{16,0},{32,16},{48,32},{1,49},{17,1},{33,17},{49,33},{2,50}... | collective-permute-start | bytes 3145736 | tf_op jit(solution)/shard_map/ppermute | solution.py:386
  74.4 25.1 %collective-permute-start.11 = (bf16[512,1024]{1,0:T(8,128)(2,1)}, bf16[512,1024]{1,0:T(8,128)(2,1)}, u32[]{:S(2)}, u32[]{:S(2)}) collective-permute-start(bf16[512,1024]{1,0:T(8,128)(2,1)} %constant_dynamic-update-slice_fusion.9.refs_6_), channel_id=1, source_target_pairs={{0,16},{16,32},{32,48},{48,0},{1,17},{17,33},{33,49},{49,1},{2,18}... | collective-permute-start | bytes 3145736 | tf_op jit(solution)/shard_map/ppermute | solution.py:386
  77.8 23.5 %collective-permute-start.10 = (bf16[512,1024]{1,0:T(8,128)(2,1)S(1)}, bf16[512,1024]{1,0:T(8,128)(2,1)S(1)}, u32[]{:S(2)}, u32[]{:S(2)}) collective-permute-start(bf16[512,1024]{1,0:T(8,128)(2,1)S(1)} %constant_dynamic-update-slice_fusion.2.refs_2_), channel_id=1, source_target_pairs={{0,192},{64,0},{128,64},{192,128},{1,193},{65,1},{129,65},{193,129... | collective-permute-start | bytes 3145736 | tf_op jit(solution)/shard_map/ppermute | solution.py:386
  78.8 24.6 %collective-permute-start.9 = (bf16[512,1024]{1,0:T(8,128)(2,1)S(1)}, bf16[512,1024]{1,0:T(8,128)(2,1)S(1)}, u32[]{:S(2)}, u32[]{:S(2)}) collective-permute-start(bf16[512,1024]{1,0:T(8,128)(2,1)S(1)} %constant_dynamic-update-slice_fusion.2.refs_2_), channel_id=1, source_target_pairs={{0,64},{64,128},{128,192},{192,0},{1,65},{65,129},{129,193},{193,1... | collective-permute-start | bytes 3145736 | tf_op jit(solution)/shard_map/ppermute | solution.py:386
  95.9 54.5 %copy-start.6 = (s32[6]{0:T(128)S(1)}, s32[6]{0:T(128)}, u32[]{:S(2)}) copy-start(s32[6]{0:T(128)} %stack.27.place_ref.refs_0_) | copy-start | bytes 76
  101.3 49.1 %copy-start = (bf16[512,1024]{1,0:T(8,128)(2,1)}, bf16[512,1024]{1,0:T(8,128)(2,1)S(1)}, u32[]{:S(2)}) copy-start(bf16[512,1024]{1,0:T(8,128)(2,1)S(1)} %collective-permute-done.10.refs_5_) | copy-start | bytes 3145732
  103.4 1.0 copy-start.2
  104.4 38.8 %all-to-all-start.1 = ((bf16[128,16,256]{2,1,0:T(8,128)(2,1)}), bf16[128,16,256]{2,1,0:T(8,128)(2,1)S(1)}, u32[]{:S(2)}, u32[]{:S(2)}) async-start(bf16[128,16,256]{2,1,0:T(8,128)(2,1)} %bitcast.11), calls=%async_computation.1 | async-start | bytes 2097152 | tf_op jit(solution)/shard_map/all_to_all | solution.py:416
  114.3 35.3 %collective-permute-start.14 = (bf16[512,1024]{1,0:T(8,128)(2,1)S(1)}, bf16[512,1024]{1,0:T(8,128)(2,1)}, u32[]{:S(2)}, u32[]{:S(2)}) collective-permute-start(bf16[512,1024]{1,0:T(8,128)(2,1)S(1)} %constant_dynamic-update-slice_fusion.2.refs_2_), channel_id=1, source_target_pairs={{0,128},{64,192},{128,0},{192,64},{1,129},{65,193},{129,1},{193,65... | collective-permute-start | bytes 3145736 | tf_op jit(solution)/shard_map/ppermute | solution.py:386
  117.6 32.8 %collective-permute-start.15 = (bf16[512,1024]{1,0:T(8,128)(2,1)}, bf16[512,1024]{1,0:T(8,128)(2,1)}, u32[]{:S(2)}, u32[]{:S(2)}) collective-permute-start(bf16[512,1024]{1,0:T(8,128)(2,1)} %constant_dynamic-update-slice_fusion.9.refs_6_), channel_id=1, source_target_pairs={{0,32},{16,48},{32,0},{48,16},{1,33},{17,49},{33,1},{49,17},{2,34}... | collective-permute-start | bytes 3145736 | tf_op jit(solution)/shard_map/ppermute | solution.py:386
  143.2 15.2 %collective-permute-start.13 = (bf16[64,2,16,256]{3,2,1,0:T(8,128)(2,1)S(1)}, bf16[64,2,16,256]{3,2,1,0:T(8,128)(2,1)S(1)}, u32[]{:S(2)}, u32[]{:S(2)}) collective-permute-start(bf16[64,2,16,256]{3,2,1,0:T(8,128)(2,1)S(1)} %bitcast.9), channel_id=1, source_target_pairs={{0,1},{1,0},{2,3},{3,2},{4,5},{5,4},{6,7},{7,6},{8,9},{9,8},{10,11... | collective-permute-start | bytes 3145736 | tf_op jit(solution)/shard_map/ppermute | solution.py:386
  150.4 1.2 copy-start.3
  151.7 6.7 %copy-start.4 = (bf16[512,1024]{1,0:T(8,128)(2,1)S(1)}, bf16[512,1024]{1,0:T(8,128)(2,1)}, u32[]{:S(2)}) copy-start(bf16[512,1024]{1,0:T(8,128)(2,1)} %copy-done.2) | copy-start | bytes 3145732
  157.4 1.0 copy-start.5
  158.4 1.2 copy-start.1

commit v7 on v6

--- a/solution.py
+++ b/solution.py
@@ -375,7 +375,7 @@
         ]
         + ([pltpu.VMEM((cols, width), F32)] if other else [])
         + [pltpu.SemaphoreType.DMA((18 + width // 256,))],
-        compiler_params=pltpu.CompilerParams(vmem_limit_bytes=VMEM_LIMIT - 12 * MIB),
+        compiler_params=pltpu.CompilerParams(vmem_limit_bytes=VMEM_LIMIT - 0 * MIB),
         cost_estimate=pl.CostEstimate(flops=2 * depth * width * cols, bytes_accessed=2 * depth * width, transcendentals=0),
         name="project_last" if other else "project_first",
     )(place, *operands)
@@ -397,6 +397,7 @@
 
     pieces = [turned(out_weight, "zl", step) for step in (1, 2, 3)]
     ready = short_filters(taps, query_proj, key_proj, value_proj, ctx)
+    ready, *pieces = lax.optimization_barrier((ready, *pieces))
     arrived = lax.all_to_all(ready, CTX, split_axis=0, concat_axis=0, tiled=True)
 
     first_half = jnp.concatenate([out_weight, pieces[0]], axis=0)

time: 166 us -> 142 us (0.86)
  waiting for transfers between devices: 78.5 us -> 55.9 us
  local copies, waits for them, and re-layouts: 8.67 us -> 2.84 us
  starting transfers between devices: 46.6 us -> 50.4 us
    ppermute x16, waiting for transfers between devices: 56 us -> 33.2 us  [turned(): lax.ppermute(value, axis, [(source, (source + steps) % count) for source...]
    unnamed x22 -> x16, local copies, waits for them, and re-layouts: 6.58 us -> 1.19 us
    ppermute x16, starting transfers between devices: 24.8 us -> 28.8 us  [turned(): lax.ppermute(value, axis, [(source, (source + steps) % count) for source...]
  transfers between devices with their start and end apart: 18 -> 18, of which waited for: 11 -> 10; matrix products, arithmetic and copies ran while one was open for 3% -> 1% of each run, Pallas kernels for 13% -> 18%
where the time goes in v7:
time: 142 us; the launch traced here: 141 us
  waiting for transfers between devices  55.9 us (39%)
  starting transfers between devices  50.4 us (35%)
  Pallas kernels  31.1 us (22%)
  local copies, waits for them, and re-layouts  2.84 us (2%)
    ppermute x16, waiting for transfers between devices, turned(): lax.ppermute(value, axis, [(source, (source + steps) % count) for source...  33.2 us
    ppermute x16, starting transfers between devices, turned(): lax.ppermute(value, axis, [(source, (source + steps) % count) for source...  28.8 us
    all_to_all x1, waiting for transfers between devices, shards(): lax.all_to_all(gated.reshape(2 * ctx, chans, cols), CTX + ('zh',), split_...  22.7 us
    pallas_call x2, Pallas kernels, project(): pl.pallas_call(lambda *refs: project_kernel(other, *refs), in_specs=[pl.B...  11.1 us
    all_to_all x1, starting transfers between devices, shards(): lax.all_to_all(ready, CTX, split_axis=0, concat_axis=0, tiled=True)  10.9 us
    all_to_all x1, starting transfers between devices, shards(): lax.all_to_all(gated.reshape(2 * ctx, chans, cols), CTX + ('zh',), split_...  10.8 us
    pallas_call x1, Pallas kernels, long_mix(): pl.pallas_call(conv_kernel, grid=(1,), in_specs=[scalars] * 3 + [whole(op...  9.49 us
    pallas_call x1, Pallas kernels, filter_spectrum(): pl.pallas_call(lambda *refs: filter_kernel(1.0 / (outer * inner), *refs),...  5.75 us
  transfers between devices with their start and end apart: 18, of which 10 were waited for; matrix products, arithmetic and copies ran while one was open for 1% of the time, Pallas kernels for 18%

profile of v7, /device:TPU:32, one launch (start us, length us, event | category | flops | bytes accessed | tf_op | source)
XLA Modules:
  0.0 140.5 jit_solution(13818952833801376480)
XLA Ops:
  0.0 3.3 %collective-permute-start.1 = (bf16[64,1024]{1,0:T(8,128)(2,1)}, bf16[64,1024]{1,0:T(8,128)(2,1)S(1)}, u32[]{:S(2)}, u32[]{:S(2)}) collective-permute-start(bf16[64,1024]{1,0:T(8,128)(2,1)} %param.21), channel_id=1, source_target_pairs={{0,8},{4,12},{8,0},{12,4},{1,9},{5,13},{9,1},{13,5},{2,10},{6,14},... | collective-permute-start | bytes 393224 | tf_op jit(solution)/shard_map/ppermute | solution.py:386
  3.3 0.0 collective-permute-start
  3.3 2.0 %collective-permute-start.2 = (bf16[64,1024]{1,0:T(8,128)(2,1)}, bf16[64,1024]{1,0:T(8,128)(2,1)S(1)}, u32[]{:S(2)}, u32[]{:S(2)}) collective-permute-start(bf16[64,1024]{1,0:T(8,128)(2,1)} %param.21), channel_id=1, source_target_pairs={{0,12},{4,0},{8,4},{12,8},{1,13},{5,1},{9,5},{13,9},{2,14},{6,2},{... | collective-permute-start | bytes 393224 | tf_op jit(solution)/shard_map/ppermute | solution.py:386
  5.3 4.8 %short_filters.1 = bf16[64,16,640]{2,1,0:T(8,128)(2,1)} custom-call(f32[3,7,64]{2,1,0:T(8,128)} %bitcast.12, bf16[1024,256]{1,0:T(8,128)(2,1)} %q_ref.1, bf16[1024,256]{1,0:T(8,128)(2,1)} %k_ref.1, bf16[1024,256]{1,0:T(8,128)(2,1)} %v_ref.1), custom_call_target="tpu_custom_call" | custom-call | flops 7340032 | bytes 2621440 | tf_op jit(solution)/shard_map/short_filters/pallas_call | solution.py:97
  10.1 0.0 collective-permute-done.1
  10.1 4.2 %collective-permute-done = bf16[64,1024]{1,0:T(8,128)(2,1)} collective-permute-done((bf16[64,1024]{1,0:T(8,128)(2,1)}, bf16[64,1024]{1,0:T(8,128)(2,1)}, u32[]{:S(2)}, u32[]{:S(2)}) %collective-permute-start) | collective-permute-done | bytes 131104 | tf_op jit(solution)/shard_map/ppermute | solution.py:386
  14.3 0.0 collective-permute-done.2
  14.3 10.9 %all-to-all-start = ((bf16[64,16,640]{2,1,0:T(8,128)(2,1)}), bf16[64,16,640]{2,1,0:T(8,128)(2,1)S(1)}, u32[]{:S(2)}, u32[]{:S(2)}) async-start(bf16[64,16,640]{2,1,0:T(8,128)(2,1)} %short_filters.1), calls=%async_computation | async-start | bytes 2621440 | tf_op jit(solution)/shard_map/all_to_all | solution.py:401
  25.2 1.5 %collective-permute-start.6 = (bf16[128,1024]{1,0:T(8,128)(2,1)S(1)}, bf16[128,1024]{1,0:T(8,128)(2,1)S(1)}, u32[]{:S(2)}, u32[]{:S(2)}) collective-permute-start(bf16[128,1024]{1,0:T(8,128)(2,1)S(1)} %get-tuple-element.33), channel_id=1, source_target_pairs={{0,64},{64,128},{128,192},{192,0},{1,65},{65,129},{129,193},{193,1... | collective-permute-start | bytes 786440 | tf_op jit(solution)/shard_map/ppermute | solution.py:386
  26.8 2.9 %collective-permute-start.7 = (bf16[128,1024]{1,0:T(8,128)(2,1)S(1)}, bf16[128,1024]{1,0:T(8,128)(2,1)S(1)}, u32[]{:S(2)}, u32[]{:S(2)}) collective-permute-start(bf16[128,1024]{1,0:T(8,128)(2,1)S(1)} %get-tuple-element.33), channel_id=1, source_target_pairs={{0,128},{64,192},{128,0},{192,64},{1,129},{65,193},{129,1},{193,65... | collective-permute-start | bytes 786440 | tf_op jit(solution)/shard_map/ppermute | solution.py:386
  29.7 0.0 copy-done.4
  29.7 1.4 %collective-permute-start.8 = (bf16[128,1024]{1,0:T(8,128)(2,1)S(1)}, bf16[128,1024]{1,0:T(8,128)(2,1)S(1)}, u32[]{:S(2)}, u32[]{:S(2)}) collective-permute-start(bf16[128,1024]{1,0:T(8,128)(2,1)S(1)} %get-tuple-element.33), channel_id=1, source_target_pairs={{0,192},{64,0},{128,64},{192,128},{1,193},{65,1},{129,65},{193,129... | collective-permute-start | bytes 786440 | tf_op jit(solution)/shard_map/ppermute | solution.py:386
  31.1 0.9 constant_dynamic-update-slice_fusion
  32.1 2.8 %collective-permute-start.5 = (bf16[128,1024]{1,0:T(8,128)(2,1)S(1)}, bf16[128,1024]{1,0:T(8,128)(2,1)S(1)}, u32[]{:S(2)}, u32[]{:S(2)}) collective-permute-start(bf16[128,1024]{1,0:T(8,128)(2,1)S(1)} %get-tuple-element.37), channel_id=1, source_target_pairs={{0,48},{16,0},{32,16},{48,32},{1,49},{17,1},{33,17},{49,33},{2,50}... | collective-permute-start | bytes 786440 | tf_op jit(solution)/shard_map/ppermute | solution.py:386
  34.9 0.8 collective-permute-start.4
  35.7 6.3 %collective-permute-done.6 = bf16[128,1024]{1,0:T(8,128)(2,1)S(1)} collective-permute-done((bf16[128,1024]{1,0:T(8,128)(2,1)S(1)}, bf16[128,1024]{1,0:T(8,128)(2,1)S(1)}, u32[]{:S(2)}, u32[]{:S(2)}) %collective-permute-start.6) | collective-permute-done | bytes 262176 | tf_op jit(solution)/shard_map/ppermute | solution.py:386
  42.0 2.8 %collective-permute-start.3 = (bf16[128,1024]{1,0:T(8,128)(2,1)S(1)}, bf16[128,1024]{1,0:T(8,128)(2,1)S(1)}, u32[]{:S(2)}, u32[]{:S(2)}) collective-permute-start(bf16[128,1024]{1,0:T(8,128)(2,1)S(1)} %get-tuple-element.37), channel_id=1, source_target_pairs={{0,16},{16,32},{32,48},{48,0},{1,17},{17,33},{33,49},{49,1},{2,18}... | collective-permute-start | bytes 786440 | tf_op jit(solution)/shard_map/ppermute | solution.py:386
  44.8 7.4 %collective-permute-done.7 = bf16[128,1024]{1,0:T(8,128)(2,1)S(1)} collective-permute-done((bf16[128,1024]{1,0:T(8,128)(2,1)S(1)}, bf16[128,1024]{1,0:T(8,128)(2,1)S(1)}, u32[]{:S(2)}, u32[]{:S(2)}) %collective-permute-start.7) | collective-permute-done | bytes 262176 | tf_op jit(solution)/shard_map/ppermute | solution.py:386
  52.2 0.0 collective-permute-done.8
  52.2 0.0 copy-start.2
  52.2 2.6 %collective-permute-start.12 = (bf16[512,1024]{1,0:T(8,128)(2,1)S(1)}, bf16[512,1024]{1,0:T(8,128)(2,1)}, u32[]{:S(2)}, u32[]{:S(2)}) collective-permute-start(bf16[512,1024]{1,0:T(8,128)(2,1)S(1)} %constant_dynamic-update-slice_fusion.9.refs_6_), channel_id=1, source_target_pairs={{0,48},{16,0},{32,16},{48,32},{1,49},{17,1},{33,17},{49,33},{2,50}... | collective-permute-start | bytes 3145736 | tf_op jit(solution)/shard_map/ppermute | solution.py:386
  54.8 0.0 collective-permute-start.11
  54.8 0.5 collective-permute-done.3
  55.4 0.0 collective-permute-done.4
  55.4 0.0 collective-permute-done.5
  55.4 0.0 copy-start.1
  55.5 1.2 collective-permute-start.10
  56.6 0.9 collective-permute-start.9
  57.6 0.7 stack.27.place_ref.refs_0_
  58.2 5.7 %filter_spectrum.1.spec_hbm = f32[1024,512]{1,0:T(8,128)} custom-call(f32[16,16384]{1,0:T(8,128)} %refs_0_, bf16[128,64]{1,0:T(8,128)(2,1)} %constant.39.clone.refs_1_.f_hi, bf16[128,64]{1,0:T(8,128)(2,1)} %constant.40.clone.refs_2_.f_lo, f32[64,256]{1,0:T(8,128)} %constant.41.clone.refs_3_.cos_ref, f32[64,256]{1,0:T(8,128)} %constant.42.clone.refs_4_.sin_ref, ...), custom_call_target="tpu_custom_call" | custom-call | flops 1610612736 | bytes 5242880 | tf_op jit(solution)/shard_map/filter_spectrum/pallas_call | solution.py:146
  64.0 0.0 all-to-all-done.in_ref
  64.0 1.1 copy-done
  65.0 9.5 %long_conv.1 = bf16[64,2,16,256]{3,2,1,0:T(8,128)(2,1)} custom-call(s32[6]{0:T(128)} %stack.27.place_ref.refs_0_, f32[16]{0:T(128)} %skip_ref.1, f32[3,7,64]{2,1,0:T(8,128)} %bitcast.13, bf16[64,16,640]{2,1,0:T(8,128)(2,1)} %copy-done, bf16[128,64]{1,0:T(8,128)(2,1)} %constant.39.clone.refs_1_.f_hi, bf16[128,64]{1,0:T(8,128)(2,1)} %constant.40.clone.refs_2_.f_lo, ...), custom_call_target="tpu_custom_call" | custom-call | flops 1048576 | bytes 1048576 | tf_op jit(solution)/shard_map/long_conv/pallas_call | solution.py:266
  74.5 2.9 %collective-permute-done.12.refs_9_ = bf16[512,1024]{1,0:T(8,128)(2,1)} collective-permute-done((bf16[512,1024]{1,0:T(8,128)(2,1)S(1)}, bf16[512,1024]{1,0:T(8,128)(2,1)}, u32[]{:S(2)}, u32[]{:S(2)}) %collective-permute-start.12) | collective-permute-done | bytes 1048608 | tf_op jit(solution)/shard_map/ppermute | solution.py:386
  77.4 3.5 %collective-permute-done.11.refs_7_ = bf16[512,1024]{1,0:T(8,128)(2,1)} collective-permute-done((bf16[512,1024]{1,0:T(8,128)(2,1)S(1)}, bf16[512,1024]{1,0:T(8,128)(2,1)}, u32[]{:S(2)}, u32[]{:S(2)}) %collective-permute-start.11) | collective-permute-done | bytes 1048608 | tf_op jit(solution)/shard_map/ppermute | solution.py:386
  80.9 0.0 collective-permute-done.10.refs_5_
  80.9 1.3 collective-permute-done.9.refs_3_
  82.3 10.8 %all-to-all-start.1 = ((bf16[128,16,256]{2,1,0:T(8,128)(2,1)}), bf16[128,16,256]{2,1,0:T(8,128)(2,1)S(1)}, u32[]{:S(2)}, u32[]{:S(2)}) async-start(bf16[128,16,256]{2,1,0:T(8,128)(2,1)} %bitcast.9), calls=%async_computation.1 | async-start | bytes 2097152 | tf_op jit(solution)/shard_map/all_to_all | solution.py:417
  93.1 3.4 %collective-permute-start.14 = (bf16[512,1024]{1,0:T(8,128)(2,1)S(1)}, bf16[512,1024]{1,0:T(8,128)(2,1)}, u32[]{:S(2)}, u32[]{:S(2)}) collective-permute-start(bf16[512,1024]{1,0:T(8,128)(2,1)S(1)} %constant_dynamic-update-slice_fusion.2.refs_2_), channel_id=1, source_target_pairs={{0,128},{64,192},{128,0},{192,64},{1,129},{65,193},{129,1},{193,65... | collective-permute-start | bytes 3145736 | tf_op jit(solution)/shard_map/ppermute | solution.py:386
  96.4 0.0 copy-done.2
  96.4 3.1 %collective-permute-start.15 = (bf16[512,1024]{1,0:T(8,128)(2,1)S(1)}, bf16[512,1024]{1,0:T(8,128)(2,1)}, u32[]{:S(2)}, u32[]{:S(2)}) collective-permute-start(bf16[512,1024]{1,0:T(8,128)(2,1)S(1)} %constant_dynamic-update-slice_fusion.9.refs_6_), channel_id=1, source_target_pairs={{0,32},{16,48},{32,0},{48,16},{1,33},{17,49},{33,1},{49,17},{2,34}... | collective-permute-start | bytes 3145736 | tf_op jit(solution)/shard_map/ppermute | solution.py:386
  99.5 22.7 %all-to-all-done.1 = bf16[128,16,256]{2,1,0:T(8,128)(2,1)S(1)} async-done(((bf16[128,16,256]{2,1,0:T(8,128)(2,1)}), bf16[128,16,256]{2,1,0:T(8,128)(2,1)S(1)}, u32[]{:S(2)}, u32[]{:S(2)}) %all-to-all-start.1) | async-done | bytes 1048608 | tf_op jit(solution)/shard_map/all_to_all | solution.py:417
  122.2 0.0 collective-permute-start.13
  122.2 6.4 %collective-permute-done.14.refs_4_ = bf16[512,1024]{1,0:T(8,128)(2,1)} collective-permute-done((bf16[512,1024]{1,0:T(8,128)(2,1)S(1)}, bf16[512,1024]{1,0:T(8,128)(2,1)}, u32[]{:S(2)}, u32[]{:S(2)}) %collective-permute-start.14) | collective-permute-done | bytes 1048608 | tf_op jit(solution)/shard_map/ppermute | solution.py:386
  128.6 0.7 collective-permute-done.15.refs_8_
  129.2 5.4 %project_first.1.refs_10_ = f32[256,1024]{1,0:T(8,128)} custom-call(s32[6]{0:T(128)} %stack.27.place_ref.refs_0_, bf16[64,2,16,256]{3,2,1,0:T(8,128)(2,1)} %bitcast.11, bf16[512,1024]{1,0:T(8,128)(2,1)} %copy-done.1, bf16[512,1024]{1,0:T(8,128)(2,1)} %collective-permute-done.9.refs_3_, bf16[512,1024]{1,0:T(8,128)(2,1)} %collective-permute-done.14.refs_4_, ...), custom_call_target="tpu_custom_call" | custom-call | flops 1073741824 | bytes 4194304 | tf_op jit(solution)/shard_map/project_first/pallas_call | solution.py:365
  134.6 0.0 collective-permute-done.13.refs_1_
  134.6 5.7 %project_last.1 = bf16[1024,256]{1,0:T(8,128)(2,1)} custom-call(s32[6]{0:T(128)} %stack.27.place_ref.refs_0_, bf16[64,2,16,256]{3,2,1,0:T(8,128)(2,1)} %collective-permute-done.13.refs_1_, bf16[512,1024]{1,0:T(8,128)(2,1)} %copy-done.1, bf16[512,1024]{1,0:T(8,128)(2,1)} %collective-permute-done.9.refs_3_, bf16[512,1024]{1,0:T(8,128)(2,1)} %collective-permute-done.14.refs_4_, ...), custom_call_target="tpu_custom_call" | custom-call | flops 1073741824 | bytes 4194304 | tf_op jit(solution)/shard_map/project_last/pallas_call | solution.py:365
  (14 shorter events, 0.2 us)
Async XLA Ops:
  0.0 10.1 %collective-permute-start.1 = (bf16[64,1024]{1,0:T(8,128)(2,1)}, bf16[64,1024]{1,0:T(8,128)(2,1)S(1)}, u32[]{:S(2)}, u32[]{:S(2)}) collective-permute-start(bf16[64,1024]{1,0:T(8,128)(2,1)} %param.21), channel_id=1, source_target_pairs={{0,8},{4,12},{8,0},{12,4},{1,9},{5,13},{9,1},{13,5},{2,10},{6,14},... | collective-permute-start | bytes 393224 | tf_op jit(solution)/shard_map/ppermute | solution.py:386
  3.3 11.0 %collective-permute-start = (bf16[64,1024]{1,0:T(8,128)(2,1)}, bf16[64,1024]{1,0:T(8,128)(2,1)}, u32[]{:S(2)}, u32[]{:S(2)}) collective-permute-start(bf16[64,1024]{1,0:T(8,128)(2,1)} %param.21), channel_id=1, source_target_pairs={{0,4},{4,8},{8,12},{12,0},{1,5},{5,9},{9,13},{13,1},{2,6},{6,10},{... | collective-permute-start | bytes 393224 | tf_op jit(solution)/shard_map/ppermute | solution.py:386
  3.3 11.0 %collective-permute-start.2 = (bf16[64,1024]{1,0:T(8,128)(2,1)}, bf16[64,1024]{1,0:T(8,128)(2,1)S(1)}, u32[]{:S(2)}, u32[]{:S(2)}) collective-permute-start(bf16[64,1024]{1,0:T(8,128)(2,1)} %param.21), channel_id=1, source_target_pairs={{0,12},{4,0},{8,4},{12,8},{1,13},{5,1},{9,5},{13,9},{2,14},{6,2},{... | collective-permute-start | bytes 393224 | tf_op jit(solution)/shard_map/ppermute | solution.py:386
  10.1 19.6 %copy-start.4 = (bf16[64,1024]{1,0:T(8,128)(2,1)S(1)}, bf16[64,1024]{1,0:T(8,128)(2,1)}, u32[]{:S(2)}) copy-start(bf16[64,1024]{1,0:T(8,128)(2,1)} %param.21) | copy-start | bytes 393220
  14.3 49.7 %all-to-all-start = ((bf16[64,16,640]{2,1,0:T(8,128)(2,1)}), bf16[64,16,640]{2,1,0:T(8,128)(2,1)S(1)}, u32[]{:S(2)}, u32[]{:S(2)}) async-start(bf16[64,16,640]{2,1,0:T(8,128)(2,1)} %short_filters.1), calls=%async_computation | async-start | bytes 2621440 | tf_op jit(solution)/shard_map/all_to_all | solution.py:401
  25.2 16.7 %collective-permute-start.6 = (bf16[128,1024]{1,0:T(8,128)(2,1)S(1)}, bf16[128,1024]{1,0:T(8,128)(2,1)S(1)}, u32[]{:S(2)}, u32[]{:S(2)}) collective-permute-start(bf16[128,1024]{1,0:T(8,128)(2,1)S(1)} %get-tuple-element.33), channel_id=1, source_target_pairs={{0,64},{64,128},{128,192},{192,0},{1,65},{65,129},{129,193},{193,1... | collective-permute-start | bytes 786440 | tf_op jit(solution)/shard_map/ppermute | solution.py:386
  26.8 25.3 %collective-permute-start.7 = (bf16[128,1024]{1,0:T(8,128)(2,1)S(1)}, bf16[128,1024]{1,0:T(8,128)(2,1)S(1)}, u32[]{:S(2)}, u32[]{:S(2)}) collective-permute-start(bf16[128,1024]{1,0:T(8,128)(2,1)S(1)} %get-tuple-element.33), channel_id=1, source_target_pairs={{0,128},{64,192},{128,0},{192,64},{1,129},{65,193},{129,1},{193,65... | collective-permute-start | bytes 786440 | tf_op jit(solution)/shard_map/ppermute | solution.py:386
  29.7 22.5 %collective-permute-start.8 = (bf16[128,1024]{1,0:T(8,128)(2,1)S(1)}, bf16[128,1024]{1,0:T(8,128)(2,1)S(1)}, u32[]{:S(2)}, u32[]{:S(2)}) collective-permute-start(bf16[128,1024]{1,0:T(8,128)(2,1)S(1)} %get-tuple-element.33), channel_id=1, source_target_pairs={{0,192},{64,0},{128,64},{192,128},{1,193},{65,1},{129,65},{193,129... | collective-permute-start | bytes 786440 | tf_op jit(solution)/shard_map/ppermute | solution.py:386
  32.1 23.4 %collective-permute-start.5 = (bf16[128,1024]{1,0:T(8,128)(2,1)S(1)}, bf16[128,1024]{1,0:T(8,128)(2,1)S(1)}, u32[]{:S(2)}, u32[]{:S(2)}) collective-permute-start(bf16[128,1024]{1,0:T(8,128)(2,1)S(1)} %get-tuple-element.37), channel_id=1, source_target_pairs={{0,48},{16,0},{32,16},{48,32},{1,49},{17,1},{33,17},{49,33},{2,50}... | collective-permute-start | bytes 786440 | tf_op jit(solution)/shard_map/ppermute | solution.py:386
  34.9 20.5 %collective-permute-start.4 = (bf16[128,1024]{1,0:T(8,128)(2,1)S(1)}, bf16[128,1024]{1,0:T(8,128)(2,1)S(1)}, u32[]{:S(2)}, u32[]{:S(2)}) collective-permute-start(bf16[128,1024]{1,0:T(8,128)(2,1)S(1)} %get-tuple-element.37), channel_id=1, source_target_pairs={{0,32},{16,48},{32,0},{48,16},{1,33},{17,49},{33,1},{49,17},{2,34}... | collective-permute-start | bytes 786440 | tf_op jit(solution)/shard_map/ppermute | solution.py:386
  42.0 13.4 %collective-permute-start.3 = (bf16[128,1024]{1,0:T(8,128)(2,1)S(1)}, bf16[128,1024]{1,0:T(8,128)(2,1)S(1)}, u32[]{:S(2)}, u32[]{:S(2)}) collective-permute-start(bf16[128,1024]{1,0:T(8,128)(2,1)S(1)} %get-tuple-element.37), channel_id=1, source_target_pairs={{0,16},{16,32},{32,48},{48,0},{1,17},{17,33},{33,49},{49,1},{2,18}... | collective-permute-start | bytes 786440 | tf_op jit(solution)/shard_map/ppermute | solution.py:386
  52.2 44.3 %copy-start.2 = (bf16[512,1024]{1,0:T(8,128)(2,1)}, bf16[512,1024]{1,0:T(8,128)(2,1)S(1)}, u32[]{:S(2)}) copy-start(bf16[512,1024]{1,0:T(8,128)(2,1)S(1)} %constant_dynamic-update-slice_fusion.9.refs_6_) | copy-start | bytes 3145732
  52.2 25.2 %collective-permute-start.12 = (bf16[512,1024]{1,0:T(8,128)(2,1)S(1)}, bf16[512,1024]{1,0:T(8,128)(2,1)}, u32[]{:S(2)}, u32[]{:S(2)}) collective-permute-start(bf16[512,1024]{1,0:T(8,128)(2,1)S(1)} %constant_dynamic-update-slice_fusion.9.refs_6_), channel_id=1, source_target_pairs={{0,48},{16,0},{32,16},{48,32},{1,49},{17,1},{33,17},{49,33},{2,50}... | collective-permute-start | bytes 3145736 | tf_op jit(solution)/shard_map/ppermute | solution.py:386
  54.8 26.1 %collective-permute-start.11 = (bf16[512,1024]{1,0:T(8,128)(2,1)S(1)}, bf16[512,1024]{1,0:T(8,128)(2,1)}, u32[]{:S(2)}, u32[]{:S(2)}) collective-permute-start(bf16[512,1024]{1,0:T(8,128)(2,1)S(1)} %constant_dynamic-update-slice_fusion.9.refs_6_), channel_id=1, source_target_pairs={{0,16},{16,32},{32,48},{48,0},{1,17},{17,33},{33,49},{49,1},{2,18}... | collective-permute-start | bytes 3145736 | tf_op jit(solution)/shard_map/ppermute | solution.py:386
  55.4 37.6 %copy-start.1 = (bf16[512,1024]{1,0:T(8,128)(2,1)}, bf16[512,1024]{1,0:T(8,128)(2,1)S(1)}, u32[]{:S(2)}) copy-start(bf16[512,1024]{1,0:T(8,128)(2,1)S(1)} %constant_dynamic-update-slice_fusion.2.refs_2_) | copy-start | bytes 3145732
  55.5 25.5 %collective-permute-start.10 = (bf16[512,1024]{1,0:T(8,128)(2,1)S(1)}, bf16[512,1024]{1,0:T(8,128)(2,1)}, u32[]{:S(2)}, u32[]{:S(2)}) collective-permute-start(bf16[512,1024]{1,0:T(8,128)(2,1)S(1)} %constant_dynamic-update-slice_fusion.2.refs_2_), channel_id=1, source_target_pairs={{0,192},{64,0},{128,64},{192,128},{1,193},{65,1},{129,65},{193,129... | collective-permute-start | bytes 3145736 | tf_op jit(solution)/shard_map/ppermute | solution.py:386
  56.6 25.7 %collective-permute-start.9 = (bf16[512,1024]{1,0:T(8,128)(2,1)S(1)}, bf16[512,1024]{1,0:T(8,128)(2,1)}, u32[]{:S(2)}, u32[]{:S(2)}) collective-permute-start(bf16[512,1024]{1,0:T(8,128)(2,1)S(1)} %constant_dynamic-update-slice_fusion.2.refs_2_), channel_id=1, source_target_pairs={{0,64},{64,128},{128,192},{192,0},{1,65},{65,129},{129,193},{193,1... | collective-permute-start | bytes 3145736 | tf_op jit(solution)/shard_map/ppermute | solution.py:386
  64.0 1.1 copy-start
  82.3 39.9 %all-to-all-start.1 = ((bf16[128,16,256]{2,1,0:T(8,128)(2,1)}), bf16[128,16,256]{2,1,0:T(8,128)(2,1)S(1)}, u32[]{:S(2)}, u32[]{:S(2)}) async-start(bf16[128,16,256]{2,1,0:T(8,128)(2,1)} %bitcast.9), calls=%async_computation.1 | async-start | bytes 2097152 | tf_op jit(solution)/shard_map/all_to_all | solution.py:417
  93.1 35.5 %collective-permute-start.14 = (bf16[512,1024]{1,0:T(8,128)(2,1)S(1)}, bf16[512,1024]{1,0:T(8,128)(2,1)}, u32[]{:S(2)}, u32[]{:S(2)}) collective-permute-start(bf16[512,1024]{1,0:T(8,128)(2,1)S(1)} %constant_dynamic-update-slice_fusion.2.refs_2_), channel_id=1, source_target_pairs={{0,128},{64,192},{128,0},{192,64},{1,129},{65,193},{129,1},{193,65... | collective-permute-start | bytes 3145736 | tf_op jit(solution)/shard_map/ppermute | solution.py:386
  96.4 32.8 %collective-permute-start.15 = (bf16[512,1024]{1,0:T(8,128)(2,1)S(1)}, bf16[512,1024]{1,0:T(8,128)(2,1)}, u32[]{:S(2)}, u32[]{:S(2)}) collective-permute-start(bf16[512,1024]{1,0:T(8,128)(2,1)S(1)} %constant_dynamic-update-slice_fusion.9.refs_6_), channel_id=1, source_target_pairs={{0,32},{16,48},{32,0},{48,16},{1,33},{17,49},{33,1},{49,17},{2,34}... | collective-permute-start | bytes 3145736 | tf_op jit(solution)/shard_map/ppermute | solution.py:386
  122.2 7.0 %copy-start.3 = (bf16[128,16,256]{2,1,0:T(8,128)(2,1)}, bf16[128,16,256]{2,1,0:T(8,128)(2,1)S(1)}, u32[]{:S(2)}) copy-start(bf16[128,16,256]{2,1,0:T(8,128)(2,1)S(1)} %all-to-all-done.1) | copy-start | bytes 3145732
  122.2 12.4 %collective-permute-start.13 = (bf16[64,2,16,256]{3,2,1,0:T(8,128)(2,1)S(1)}, bf16[64,2,16,256]{3,2,1,0:T(8,128)(2,1)}, u32[]{:S(2)}, u32[]{:S(2)}) collective-permute-start(bf16[64,2,16,256]{3,2,1,0:T(8,128)(2,1)S(1)} %bitcast.10), channel_id=1, source_target_pairs={{0,1},{1,0},{2,3},{3,2},{4,5},{5,4},{6,7},{7,6},{8,9},{9,8},{10,11... | collective-permute-start | bytes 3145736 | tf_op jit(solution)/shard_map/ppermute | solution.py:386

commit v8 on v5

--- a/solution.py
+++ b/solution.py
@@ -283,7 +283,7 @@
             pltpu.VMEM((2 * inner, 2 * inner), BF16),
             pltpu.SemaphoreType.DMA((3,)),
         ],
-        compiler_params=pltpu.CompilerParams(vmem_limit_bytes=VMEM_LIMIT - 12 * MIB),
+        compiler_params=pltpu.CompilerParams(vmem_limit_bytes=VMEM_LIMIT - 10 * MIB),
         cost_estimate=pl.CostEstimate(flops=2**20, bytes_accessed=2**20, transcendentals=0),
         name="long_conv",
     )(place, skip_bias, taps, *operands, *fetched)
@@ -325,17 +325,28 @@
                 parts.append(z_ref[pl.ds(start, 4), half].reshape(unit, cols))
             to = (half * 4 + x) * size
             g_ref[:, to : to + size] = jnp.concatenate(parts, axis=0).T
-    for fetch in fetches:
+    held = sum_ref if other else out_ref
+    middle = depth // 2
+    for fetch in fetches[:4] + fetches[8:]:
+        fetch.wait()
+    for index in range(width // block):
+        at = slice(index * block, (index + 1) * block)
+        part = dot(g_ref[:, :middle], w_ref[:middle, at])
+        if other:
+            held[:, at] += part
+        else:
+            held[index] = part
+    for fetch in fetches[4:8]:
         fetch.wait()
     leaving = []
     for index in range(width // block):
         at = slice(index * block, (index + 1) * block)
-        part = dot(g_ref[...], w_ref[:, at])
+        part = dot(g_ref[:, middle:], w_ref[middle:, at])
         if other:
-            out_ref[at, :] = (part + sum_ref[:, at]).T.astype(BF16)
+            out_ref[at, :] = (part + held[:, at]).T.astype(BF16)
             leaving.append(copy(out_ref.at[at], out_hbm.at[at], 10 + index))
         else:
-            out_ref[index] = part
+            held[index] += part
             leaving.append(copy(out_ref.at[index], out_hbm.at[:, at], 10 + index))
     for leave in leaving:
         leave.wait()

time: 136 us -> 134 us (0.985)
  waiting for transfers between devices: 33.5 us -> 35.3 us
  local copies, waits for them, and re-layouts: 1.72 us -> 0.06 us
    all_gather x1, waiting for transfers between devices: 0.4 us -> 2.18 us  [shards(): lax.all_gather(jnp.concatenate([out_weight, *pieces], axis=0), ('y', 'x')...]
    unnamed x24 -> x22, local copies, waits for them, and re-layouts: 1.72 us -> 0.06 us
    pallas_call x2, Pallas kernels: 10.6 us -> 9.19 us  [project(): pl.pallas_call(lambda *refs: project_kernel(other, *refs), in_specs=[pl.B...]
where the time goes in v8:
time: 134 us; the launch traced here: 132 us
  blocking collectives  39.4 us (29%)
  waiting for transfers between devices  35.3 us (26%)
  Pallas kernels  28 us (21%)
  starting transfers between devices  14.9 us (11%)
  between operations  13.6 us (10%)
    all_to_all x1, blocking collectives, shards(): lax.all_to_all(gated.reshape(2 * ctx, chans, cols), CTX + ('zh',), split_...  39.4 us
    all_to_all x1, waiting for transfers between devices, shards(): lax.all_to_all(ready, CTX, split_axis=0, concat_axis=0, tiled=True)  27.7 us
    all_to_all x1, starting transfers between devices, shards(): lax.all_to_all(ready, CTX, split_axis=0, concat_axis=0, tiled=True)  9.63 us
    pallas_call x2, Pallas kernels, project(): pl.pallas_call(lambda *refs: project_kernel(other, *refs), in_specs=[pl.B...  9.19 us
    pallas_call x1, Pallas kernels, long_mix(): pl.pallas_call(conv_kernel, grid=(1,), in_specs=[scalars] * 3 + [whole(op...  8.13 us
    pallas_call x1, Pallas kernels, filter_spectrum(): pl.pallas_call(lambda *refs: filter_kernel(1.0 / (outer * inner), *refs),...  5.9 us
    ppermute x4, waiting for transfers between devices, turned(): lax.ppermute(value, axis, [(source, (source + steps) % count) for source...  5.4 us
    ppermute x4, starting transfers between devices, turned(): lax.ppermute(value, axis, [(source, (source + steps) % count) for source...  5.3 us
  transfers between devices with their start and end apart: 6, of which 5 were waited for; matrix products, arithmetic and copies ran while one was open for 0% of the time, Pallas kernels for 18%

profile of v8, /device:TPU:32, one launch (start us, length us, event | category | flops | bytes accessed | tf_op | source)
XLA Modules:
  0.0 132.1 jit_solution(13159627173666943624)
XLA Ops:
  6.5 0.0 copy-start.10
  6.5 0.0 all-gather.2.cloned.1.call-start
  6.5 1.9 %collective-permute-start = (bf16[64,1024]{1,0:T(8,128)(2,1)}, bf16[64,1024]{1,0:T(8,128)(2,1)S(1)}, u32[]{:S(2)}, u32[]{:S(2)}) collective-permute-start(bf16[64,1024]{1,0:T(8,128)(2,1)} %param.21), channel_id=1, source_target_pairs={{0,4},{4,8},{8,12},{12,0},{1,5},{5,9},{9,13},{13,1},{2,6},{6,10},{... | collective-permute-start | bytes 393224 | tf_op jit(solution)/shard_map/ppermute | solution.py:384
  8.5 2.3 %collective-permute-start.1 = (bf16[64,1024]{1,0:T(8,128)(2,1)}, bf16[64,1024]{1,0:T(8,128)(2,1)S(1)}, u32[]{:S(2)}, u32[]{:S(2)}) collective-permute-start(bf16[64,1024]{1,0:T(8,128)(2,1)} %param.21), channel_id=1, source_target_pairs={{0,8},{4,12},{8,0},{12,4},{1,9},{5,13},{9,1},{13,5},{2,10},{6,14},... | collective-permute-start | bytes 393224 | tf_op jit(solution)/shard_map/ppermute | solution.py:384
  10.7 1.1 collective-permute-start.2
  11.8 4.8 %short_filters.1 = bf16[64,16,640]{2,1,0:T(8,128)(2,1)} custom-call(f32[3,7,64]{2,1,0:T(8,128)} %bitcast.10, bf16[1024,256]{1,0:T(8,128)(2,1)} %q_ref.1, bf16[1024,256]{1,0:T(8,128)(2,1)} %k_ref.1, bf16[1024,256]{1,0:T(8,128)(2,1)} %v_ref.1), custom_call_target="tpu_custom_call" | custom-call | flops 7340032 | bytes 2621440 | tf_op jit(solution)/shard_map/short_filters/pallas_call | solution.py:97
  16.6 1.7 %collective-permute-done = bf16[64,1024]{1,0:T(8,128)(2,1)S(1)} collective-permute-done((bf16[64,1024]{1,0:T(8,128)(2,1)}, bf16[64,1024]{1,0:T(8,128)(2,1)S(1)}, u32[]{:S(2)}, u32[]{:S(2)}) %collective-permute-start) | collective-permute-done | bytes 131104 | tf_op jit(solution)/shard_map/ppermute | solution.py:384
  18.3 1.7 %collective-permute-done.1 = bf16[64,1024]{1,0:T(8,128)(2,1)S(1)} collective-permute-done((bf16[64,1024]{1,0:T(8,128)(2,1)}, bf16[64,1024]{1,0:T(8,128)(2,1)S(1)}, u32[]{:S(2)}, u32[]{:S(2)}) %collective-permute-start.1) | collective-permute-done | bytes 131104 | tf_op jit(solution)/shard_map/ppermute | solution.py:384
  20.0 2.1 %collective-permute-done.2 = bf16[64,1024]{1,0:T(8,128)(2,1)S(1)} collective-permute-done((bf16[64,1024]{1,0:T(8,128)(2,1)}, bf16[64,1024]{1,0:T(8,128)(2,1)S(1)}, u32[]{:S(2)}, u32[]{:S(2)}) %collective-permute-start.2) | collective-permute-done | bytes 131104 | tf_op jit(solution)/shard_map/ppermute | solution.py:384
  22.0 0.0 copy-done.10
  22.0 0.8 pad_maximum_fusion
  22.8 0.0 all-gather.2.cloned.1.call-update
  22.9 9.6 %all-to-all-start = ((bf16[64,16,640]{2,1,0:T(8,128)(2,1)}), bf16[64,16,640]{2,1,0:T(8,128)(2,1)S(1)}, u32[]{:S(2)}, u32[]{:S(2)}) async-start(bf16[64,16,640]{2,1,0:T(8,128)(2,1)} %short_filters.1), calls=%async_computation | async-start | bytes 2621440 | tf_op jit(solution)/shard_map/all_to_all | solution.py:402
  32.5 0.1 pad_add_fusion.place_ref.refs_0_
  32.6 0.0 copy-start
  32.6 0.0 copy-start.1
  32.6 0.0 copy-start.2
  32.6 0.0 copy-start.3
  32.6 0.0 copy-start.4
  32.6 0.0 copy-start.5
  32.6 0.0 copy-start.6
  32.6 0.0 copy-start.7
  32.7 0.0 copy-start.8
  32.7 0.0 copy-start.9
  32.7 5.9 %filter_spectrum.1.spec_hbm = f32[1024,512]{1,0:T(8,128)} custom-call(f32[16,16384]{1,0:T(8,128)} %refs_0_.1, bf16[128,64]{1,0:T(8,128)(2,1)} %constant.39.clone.refs_1_.f_hi, bf16[128,64]{1,0:T(8,128)(2,1)} %constant.40.clone.refs_2_.f_lo, f32[64,256]{1,0:T(8,128)} %constant.41.clone.refs_3_.cos_ref, f32[64,256]{1,0:T(8,128)} %constant.42.clone.refs_4_.sin_ref, ...), custom_call_target="tpu_custom_call" | custom-call | flops 1610612736 | bytes 5242880 | tf_op jit(solution)/shard_map/filter_spectrum/pallas_call | solution.py:146
  38.6 27.7 %all-to-all-done.in_ref = bf16[64,16,640]{2,1,0:T(8,128)(2,1)S(1)} async-done(((bf16[64,16,640]{2,1,0:T(8,128)(2,1)}), bf16[64,16,640]{2,1,0:T(8,128)(2,1)S(1)}, u32[]{:S(2)}, u32[]{:S(2)}) %all-to-all-start) | async-done | bytes 1310752 | tf_op jit(solution)/shard_map/all_to_all | solution.py:402
  66.2 0.0 copy-done
  66.2 0.0 copy-done.1
  66.2 0.0 copy-done.2
  66.3 0.0 copy-done.3
  66.3 0.0 copy-done.4
  66.3 0.0 copy-done.5
  66.3 0.0 copy-done.6
  66.3 0.0 copy-done.7
  66.3 0.0 copy-done.8
  66.3 0.0 copy-done.9
  66.3 8.1 %long_conv.1 = bf16[64,2,16,256]{3,2,1,0:T(8,128)(2,1)S(1)} custom-call(s32[4]{0:T(128)S(1)} %pad_add_fusion.place_ref.refs_0_, f32[16]{0:T(128)S(1)} %copy-done.9, f32[3,7,64]{2,1,0:T(8,128)S(1)} %bitcast.11, bf16[64,16,640]{2,1,0:T(8,128)(2,1)S(1)} %all-to-all-done.in_ref, bf16[128,64]{1,0:T(8,128)(2,1)S(1)} %copy-done.5, bf16[128,64]{1,0:T(8,128)(2,1)S(1)} %copy-done.6, ...), custom_call_target="tpu_custom_call" | custom-call | flops 1048576 | bytes 1048576 | tf_op jit(solution)/shard_map/long_conv/pallas_call | solution.py:266
  74.5 39.4 %all_to_all.10 = bf16[128,16,256]{2,1,0:T(8,128)(2,1)S(1)} all-to-all(bf16[128,16,256]{2,1,0:T(8,128)(2,1)S(1)} %bitcast.7), channel_id=1, replica_groups=mesh['y'=4,'x'=4,'zl'=4,'zh'=2,'core'=2] {'y','x','zl','zh'}, dimensions={0} | all-to-all | bytes 2097152 | tf_op jit(solution)/shard_map/all_to_all | solution.py:404
  113.9 0.0 collective-permute-start.3
  113.9 2.2 %all-gather.2.cloned.1.call-done.refs_2_ = bf16[4096,1024]{1,0:T(8,128)(2,1)} async-done(((bf16[256,1024]{1,0:T(8,128)(2,1)}), bf16[4096,1024]{1,0:T(8,128)(2,1)}) %all-gather.2.cloned.1.call-update) | async-done | bytes 8388624 | tf_op jit(solution)/shard_map/all_gather | solution.py:399
  116.0 4.7 %project_first.1.refs_3_ = f32[256,1024]{1,0:T(8,128)S(1)} custom-call(s32[4]{0:T(128)S(1)} %pad_add_fusion.place_ref.refs_0_, bf16[64,2,16,256]{3,2,1,0:T(8,128)(2,1)S(1)} %bitcast.9, bf16[4096,1024]{1,0:T(8,128)(2,1)} %all-gather.2.cloned.1.call-done.refs_2_), custom_call_target="tpu_custom_call" | custom-call | flops 1073741824 | bytes 4194304 | tf_op jit(solution)/shard_map/project_first/pallas_call | solution.py:363
  120.8 0.0 collective-permute-done.3.refs_1_
  120.8 4.5 %project_last.1 = bf16[1024,256]{1,0:T(8,128)(2,1)} custom-call(s32[4]{0:T(128)S(1)} %pad_add_fusion.place_ref.refs_0_, bf16[64,2,16,256]{3,2,1,0:T(8,128)(2,1)S(1)} %collective-permute-done.3.refs_1_, bf16[4096,1024]{1,0:T(8,128)(2,1)} %all-gather.2.cloned.1.call-done.refs_2_, f32[256,1024]{1,0:T(8,128)S(1)} %project_first.1.refs_3_), custom_call_target="tpu_custom_call" | custom-call | flops 1073741824 | bytes 4194304 | tf_op jit(solution)/shard_map/project_last/pallas_call | solution.py:363
Async XLA Ops:
  6.5 15.5 %copy-start.10 = (bf16[64,1024]{1,0:T(8,128)(2,1)S(1)}, bf16[64,1024]{1,0:T(8,128)(2,1)}, u32[]{:S(2)}) copy-start(bf16[64,1024]{1,0:T(8,128)(2,1)} %param.21) | copy-start | bytes 393220
  6.5 109.5 %all-gather.2.cloned.1.call-start = ((), (), s32[]{:S(2)}) async-start(), calls=%async_computation.2 | async-start | bytes 8912896 | tf_op jit(solution)/shard_map/all_gather | solution.py:399
  6.5 11.8 %collective-permute-start = (bf16[64,1024]{1,0:T(8,128)(2,1)}, bf16[64,1024]{1,0:T(8,128)(2,1)S(1)}, u32[]{:S(2)}, u32[]{:S(2)}) collective-permute-start(bf16[64,1024]{1,0:T(8,128)(2,1)} %param.21), channel_id=1, source_target_pairs={{0,4},{4,8},{8,12},{12,0},{1,5},{5,9},{9,13},{13,1},{2,6},{6,10},{... | collective-permute-start | bytes 393224 | tf_op jit(solution)/shard_map/ppermute | solution.py:384
  8.5 11.5 %collective-permute-start.1 = (bf16[64,1024]{1,0:T(8,128)(2,1)}, bf16[64,1024]{1,0:T(8,128)(2,1)S(1)}, u32[]{:S(2)}, u32[]{:S(2)}) collective-permute-start(bf16[64,1024]{1,0:T(8,128)(2,1)} %param.21), channel_id=1, source_target_pairs={{0,8},{4,12},{8,0},{12,4},{1,9},{5,13},{9,1},{13,5},{2,10},{6,14},... | collective-permute-start | bytes 393224 | tf_op jit(solution)/shard_map/ppermute | solution.py:384
  10.7 11.3 %collective-permute-start.2 = (bf16[64,1024]{1,0:T(8,128)(2,1)}, bf16[64,1024]{1,0:T(8,128)(2,1)S(1)}, u32[]{:S(2)}, u32[]{:S(2)}) collective-permute-start(bf16[64,1024]{1,0:T(8,128)(2,1)} %param.21), channel_id=1, source_target_pairs={{0,12},{4,0},{8,4},{12,8},{1,13},{5,1},{9,5},{13,9},{2,14},{6,2},{... | collective-permute-start | bytes 393224 | tf_op jit(solution)/shard_map/ppermute | solution.py:384
  22.9 43.4 %all-to-all-start = ((bf16[64,16,640]{2,1,0:T(8,128)(2,1)}), bf16[64,16,640]{2,1,0:T(8,128)(2,1)S(1)}, u32[]{:S(2)}, u32[]{:S(2)}) async-start(bf16[64,16,640]{2,1,0:T(8,128)(2,1)} %short_filters.1), calls=%async_computation | async-start | bytes 2621440 | tf_op jit(solution)/shard_map/all_to_all | solution.py:402
  32.6 33.7 %copy-start = (bf16[512,512]{1,0:T(8,128)(2,1)S(1)}, bf16[512,512]{1,0:T(8,128)(2,1)}, u32[]{:S(2)}) copy-start(bf16[512,512]{1,0:T(8,128)(2,1)} %constant.43.clone.refs_5_.s_hi_hbm) | copy-start | bytes 1572868
  32.6 33.7 %copy-start.1 = (bf16[512,512]{1,0:T(8,128)(2,1)S(1)}, bf16[512,512]{1,0:T(8,128)(2,1)}, u32[]{:S(2)}) copy-start(bf16[512,512]{1,0:T(8,128)(2,1)} %constant.44.clone.refs_6_.s_lo_hbm) | copy-start | bytes 1572868
  32.6 33.7 %copy-start.2 = (f32[64,256]{1,0:T(8,128)S(1)}, f32[64,256]{1,0:T(8,128)}, u32[]{:S(2)}) copy-start(f32[64,256]{1,0:T(8,128)} %constant.41.clone.refs_3_.cos_ref) | copy-start | bytes 196612
  32.6 33.7 %copy-start.3 = (f32[64,256]{1,0:T(8,128)S(1)}, f32[64,256]{1,0:T(8,128)}, u32[]{:S(2)}) copy-start(f32[64,256]{1,0:T(8,128)} %constant.42.clone.refs_4_.sin_ref) | copy-start | bytes 196612
  32.6 33.7 %copy-start.4 = (f32[3,64,7]{1,2,0:T(8,128)S(1)}, f32[3,64,7]{1,2,0:T(8,128)}, u32[]{:S(2)}) copy-start(f32[3,64,7]{1,2,0:T(8,128)} %param.18) | copy-start | bytes 16132
  32.6 33.7 %copy-start.5 = (bf16[128,64]{1,0:T(8,128)(2,1)S(1)}, bf16[128,64]{1,0:T(8,128)(2,1)}, u32[]{:S(2)}) copy-start(bf16[128,64]{1,0:T(8,128)(2,1)} %constant.39.clone.refs_1_.f_hi) | copy-start | bytes 49156
  32.6 33.7 %copy-start.6 = (bf16[128,64]{1,0:T(8,128)(2,1)S(1)}, bf16[128,64]{1,0:T(8,128)(2,1)}, u32[]{:S(2)}) copy-start(bf16[128,64]{1,0:T(8,128)(2,1)} %constant.40.clone.refs_2_.f_lo) | copy-start | bytes 49156
  32.6 33.7 %copy-start.7 = (bf16[64,128]{1,0:T(8,128)(2,1)S(1)}, bf16[64,128]{1,0:T(8,128)(2,1)}, u32[]{:S(2)}) copy-start(bf16[64,128]{1,0:T(8,128)(2,1)} %constant.45.clone.l_hi) | copy-start | bytes 49156
  32.7 33.6 %copy-start.8 = (bf16[64,128]{1,0:T(8,128)(2,1)S(1)}, bf16[64,128]{1,0:T(8,128)(2,1)}, u32[]{:S(2)}) copy-start(bf16[64,128]{1,0:T(8,128)(2,1)} %constant.46.clone.l_lo) | copy-start | bytes 49156
  32.7 33.6 %copy-start.9 = (f32[16]{0:T(128)S(1)}, f32[16]{0:T(128)}, u32[]{:S(2)}) copy-start(f32[16]{0:T(128)} %skip_ref.1) | copy-start | bytes 196
  113.9 6.9 %collective-permute-start.3 = (bf16[64,2,16,256]{3,2,1,0:T(8,128)(2,1)S(1)}, bf16[64,2,16,256]{3,2,1,0:T(8,128)(2,1)S(1)}, u32[]{:S(2)}, u32[]{:S(2)}) collective-permute-start(bf16[64,2,16,256]{3,2,1,0:T(8,128)(2,1)S(1)} %bitcast.8), channel_id=1, source_target_pairs={{0,1},{1,0},{2,3},{3,2},{4,5},{5,4},{6,7},{7,6},{8,9},{9,8},{10,11... | collective-permute-start | bytes 3145736 | tf_op jit(solution)/shard_map/ppermute | solution.py:384
Sparse Core Ops, SparseCore 0:
  23.0 93.0 all-gather.1

commit v9 on v5

--- a/solution.py
+++ b/solution.py
@@ -283,89 +283,85 @@
             pltpu.VMEM((2 * inner, 2 * inner), BF16),
             pltpu.SemaphoreType.DMA((3,)),
         ],
-        compiler_params=pltpu.CompilerParams(vmem_limit_bytes=VMEM_LIMIT - 12 * MIB),
+        compiler_params=pltpu.CompilerParams(vmem_limit_bytes=VMEM_LIMIT - 10 * MIB),
         cost_estimate=pl.CostEstimate(flops=2**20, bytes_accessed=2**20, transcendentals=0),
         name="long_conv",
     )(place, skip_bias, taps, *operands, *fetched)
 
 
-def project_kernel(other, place_ref, z_hbm, *refs):
-    if other:
-        w_hbm, sum_hbm, out_hbm, z_ref, w_ref, g_ref, out_ref, sum_ref, sems = refs
-    else:
-        w_hbm, out_hbm, z_ref, w_ref, g_ref, out_ref, sems = refs
-    _, halves, chans, cols = z_ref.shape
+def project_kernel(place_ref, own_hbm, other_hbm, w_hbm, out_hbm, z_ref, w_ref, g_ref, sum_ref, out_ref, sems):
+    cores, _, halves, chans, cols = z_ref.shape
     depth, width = w_ref.shape
     unit = 4 * chans
     size = 4 * unit
+    panel = 4 * size
     block = 256
     zl = place_ref[1]
-    core = jnp.bitwise_xor(place_ref[3], other)
 
     def copy(source, target, index):
         fetch = pltpu.make_async_copy(source, target, sems.at[index])
         fetch.start()
         return fetch
 
-    arriving = copy(z_hbm, z_ref, 0)
+    arriving = [copy(own_hbm, z_ref.at[0], 0), copy(other_hbm, z_ref.at[1], 1)]
     fetches = []
-    for half in range(halves):
-        for x in range(4):
-            index = half * 4 + x
-            start = pl.multiple_of(((half * 2 + core) * 4 + x) * size, size)
-            fetches.append(copy(w_hbm.at[pl.ds(start, size)], w_ref.at[pl.ds(index * size, size)], 1 + index))
-    if other:
-        fetches.append(copy(sum_hbm, sum_ref, 9))
-    arriving.wait()
-    for half in range(halves):
-        for x in range(4):
-            parts = []
-            for turn in range(4):
-                start = x * 16 + 4 * jnp.bitwise_and(zl - turn, 3)
-                parts.append(z_ref[pl.ds(start, 4), half].reshape(unit, cols))
-            to = (half * 4 + x) * size
-            g_ref[:, to : to + size] = jnp.concatenate(parts, axis=0).T
-    for fetch in fetches:
-        fetch.wait()
+    for other in range(cores):
+        for half in range(halves):
+            start = (half * 2 + jnp.bitwise_xor(place_ref[3], other)) * panel
+            for x in range(4):
+                index = (other * halves + half) * 4 + x
+                source = pl.ds(pl.multiple_of(start + x * size, size), size)
+                fetches.append(copy(w_hbm.at[source], w_ref.at[pl.ds(index * size, size)], 2 + index))
     leaving = []
-    for index in range(width // block):
-        at = slice(index * block, (index + 1) * block)
-        part = dot(g_ref[...], w_ref[:, at])
-        if other:
-            out_ref[at, :] = (part + sum_ref[:, at]).T.astype(BF16)
-            leaving.append(copy(out_ref.at[at], out_hbm.at[at], 10 + index))
-        else:
-            out_ref[index] = part
-            leaving.append(copy(out_ref.at[index], out_hbm.at[:, at], 10 + index))
+    for other in range(cores):
+        arriving[other].wait()
+        for half in range(halves):
+            base = (other * halves + half) * panel
+            for x in range(4):
+                parts = []
+                for turn in range(4):
+                    start = x * 16 + 4 * jnp.bitwise_and(zl - turn, 3)
+                    parts.append(z_ref[other, pl.ds(start, 4), half].reshape(unit, cols))
+                g_ref[:, base + x * size : base + (x + 1) * size] = jnp.concatenate(parts, axis=0).T
+    for part in range(cores * halves):
+        for fetch in fetches[part * 4 : part * 4 + 4]:
+            fetch.wait()
+        rows = slice(part * panel, (part + 1) * panel)
+        for index in range(width // block):
+            at = slice(index * block, (index + 1) * block)
+            total = dot(g_ref[:, rows], w_ref[rows, at])
+            if part:
+                total += sum_ref[:, at]
+            if part < cores * halves - 1:
+                sum_ref[:, at] = total
+            else:
+                out_ref[at, :] = total.T.astype(BF16)
+                leaving.append(copy(out_ref.at[at], out_hbm.at[at], 18 + index))
     for leave in leaving:
         leave.wait()
 
 
-def project(place, gated, weight, partial=None):
-    width = weight.shape[1]
-    depth = weight.shape[0] // 2
-    cols = gated.shape[3]
-    other = 0 if partial is None else 1
+def project(place, own, other, weight):
+    depth, width = weight.shape
+    cols = own.shape[3]
     anywhere = pl.BlockSpec(memory_space=pl.ANY)
-    operands = [gated, weight] + ([partial] if other else [])
-    shape = (width, cols) if other else (cols, width)
     return pl.pallas_call(
-        lambda *refs: project_kernel(other, *refs),
-        in_specs=[pl.BlockSpec(memory_space=pltpu.SMEM)] + [anywhere] * len(operands),
+        project_kernel,
+        in_specs=[pl.BlockSpec(memory_space=pltpu.SMEM)] + [anywhere] * 3,
         out_specs=anywhere,
-        out_shape=jax.ShapeDtypeStruct(shape, BF16 if other else F32),
+        out_shape=jax.ShapeDtypeStruct((width, cols), BF16),
         scratch_shapes=[
-            pltpu.VMEM(gated.shape, BF16),
+            pltpu.VMEM((2, *own.shape), BF16),
             pltpu.VMEM((depth, width), BF16),
             pltpu.VMEM((cols, depth), BF16),
-            pltpu.VMEM(shape, BF16) if other else pltpu.VMEM((width // 256, cols, 256), F32),
-        ]
-        + ([pltpu.VMEM((cols, width), F32)] if other else [])
-        + [pltpu.SemaphoreType.DMA((10 + width // 256,))],
+            pltpu.VMEM((cols, width), F32),
+            pltpu.VMEM((width, cols), BF16),
+            pltpu.SemaphoreType.DMA((18 + width // 256,)),
+        ],
         compiler_params=pltpu.CompilerParams(vmem_limit_bytes=VMEM_LIMIT - 12 * MIB),
         cost_estimate=pl.CostEstimate(flops=2 * depth * width * cols, bytes_accessed=2 * depth * width, transcendentals=0),
-        name="project_last" if other else "project_first",
-    )(place, *operands)
+        name="project",
+    )(place, own, other, weight)
 
 
 def turned(value, axis, steps):
@@ -394,7 +390,7 @@
         gated.reshape(2 * ctx, chans, cols), CTX + ("zh",), split_axis=0, concat_axis=0, tiled=True
     ).reshape(ctx, 2, chans, cols)
     other = turned(own, "core", 1)
-    return project(place, other, weight, project(place, own, weight))
+    return project(place, own, other, weight)
 
 
 def solution(mesh):

time: 136 us -> 131 us (0.963)
  Pallas kernels: 29.2 us -> 24.5 us
  waiting for transfers between devices: 33.5 us -> 35.7 us
  local copies, waits for them, and re-layouts: 1.72 us -> 0.06 us
    pallas_call x2 -> x1, Pallas kernels: 10.6 us -> 5.73 us  [project(): pl.pallas_call(project_kernel, in_specs=[pl.BlockSpec(memory_space=pltpu....]
    ppermute x4, waiting for transfers between devices: 5.41 us -> 8.06 us  [turned(): lax.ppermute(value, axis, [(source, (source + steps) % count) for source...]
    unnamed x24 -> x22, local copies, waits for them, and re-layouts: 1.72 us -> 0.06 us
  transfers between devices with their start and end apart: 6 -> 6, of which waited for: 5 -> 5; matrix products, arithmetic and copies ran while one was open for 0% -> 0% of each run, Pallas kernels for 18% -> 15%
where the time goes in v9:
time: 131 us; the launch traced here: 129 us
  blocking collectives  39.4 us (30%)
  waiting for transfers between devices  35.7 us (27%)
  Pallas kernels  24.5 us (19%)
  starting transfers between devices  14.9 us (11%)
  between operations  13.6 us (10%)
    all_to_all x1, blocking collectives, shards(): lax.all_to_all(gated.reshape(2 * ctx, chans, cols), CTX + ('zh',), split_...  39.4 us
    all_to_all x1, waiting for transfers between devices, shards(): lax.all_to_all(ready, CTX, split_axis=0, concat_axis=0, tiled=True)  27.7 us
    all_to_all x1, starting transfers between devices, shards(): lax.all_to_all(ready, CTX, split_axis=0, concat_axis=0, tiled=True)  9.63 us
    pallas_call x1, Pallas kernels, long_mix(): pl.pallas_call(conv_kernel, grid=(1,), in_specs=[scalars] * 3 + [whole(op...  8.13 us
    ppermute x4, waiting for transfers between devices, turned(): lax.ppermute(value, axis, [(source, (source + steps) % count) for source...  8.06 us
    pallas_call x1, Pallas kernels, filter_spectrum(): pl.pallas_call(lambda *refs: filter_kernel(1.0 / (outer * inner), *refs),...  5.9 us
    pallas_call x1, Pallas kernels, project(): pl.pallas_call(project_kernel, in_specs=[pl.BlockSpec(memory_space=pltpu....  5.73 us
    ppermute x4, starting transfers between devices, turned(): lax.ppermute(value, axis, [(source, (source + steps) % count) for source...  5.3 us
  transfers between devices with their start and end apart: 6, of which 5 were waited for; matrix products, arithmetic and copies ran while one was open for 0% of the time, Pallas kernels for 15%

profile of v9, /device:TPU:32, one launch (start us, length us, event | category | flops | bytes accessed | tf_op | source)
XLA Modules:
  0.0 129.1 jit_solution(844701692946086182)
XLA Ops:
  6.5 0.0 copy-start.10
  6.5 0.0 all-gather.2.cloned.1.call-start
  6.5 1.9 %collective-permute-start = (bf16[64,1024]{1,0:T(8,128)(2,1)}, bf16[64,1024]{1,0:T(8,128)(2,1)S(1)}, u32[]{:S(2)}, u32[]{:S(2)}) collective-permute-start(bf16[64,1024]{1,0:T(8,128)(2,1)} %param.21), channel_id=1, source_target_pairs={{0,4},{4,8},{8,12},{12,0},{1,5},{5,9},{9,13},{13,1},{2,6},{6,10},{... | collective-permute-start | bytes 393224 | tf_op jit(solution)/shard_map/ppermute | solution.py:369
  8.5 2.3 %collective-permute-start.1 = (bf16[64,1024]{1,0:T(8,128)(2,1)}, bf16[64,1024]{1,0:T(8,128)(2,1)S(1)}, u32[]{:S(2)}, u32[]{:S(2)}) collective-permute-start(bf16[64,1024]{1,0:T(8,128)(2,1)} %param.21), channel_id=1, source_target_pairs={{0,8},{4,12},{8,0},{12,4},{1,9},{5,13},{9,1},{13,5},{2,10},{6,14},... | collective-permute-start | bytes 393224 | tf_op jit(solution)/shard_map/ppermute | solution.py:369
  10.7 1.1 collective-permute-start.2
  11.8 4.8 %short_filters.1 = bf16[64,16,640]{2,1,0:T(8,128)(2,1)} custom-call(f32[3,7,64]{2,1,0:T(8,128)} %bitcast.10, bf16[1024,256]{1,0:T(8,128)(2,1)} %q_ref.1, bf16[1024,256]{1,0:T(8,128)(2,1)} %k_ref.1, bf16[1024,256]{1,0:T(8,128)(2,1)} %v_ref.1), custom_call_target="tpu_custom_call" | custom-call | flops 7340032 | bytes 2621440 | tf_op jit(solution)/shard_map/short_filters/pallas_call | solution.py:97
  16.6 1.7 %collective-permute-done = bf16[64,1024]{1,0:T(8,128)(2,1)S(1)} collective-permute-done((bf16[64,1024]{1,0:T(8,128)(2,1)}, bf16[64,1024]{1,0:T(8,128)(2,1)S(1)}, u32[]{:S(2)}, u32[]{:S(2)}) %collective-permute-start) | collective-permute-done | bytes 131104 | tf_op jit(solution)/shard_map/ppermute | solution.py:369
  18.3 1.7 %collective-permute-done.1 = bf16[64,1024]{1,0:T(8,128)(2,1)S(1)} collective-permute-done((bf16[64,1024]{1,0:T(8,128)(2,1)}, bf16[64,1024]{1,0:T(8,128)(2,1)S(1)}, u32[]{:S(2)}, u32[]{:S(2)}) %collective-permute-start.1) | collective-permute-done | bytes 131104 | tf_op jit(solution)/shard_map/ppermute | solution.py:369
  20.0 2.1 %collective-permute-done.2 = bf16[64,1024]{1,0:T(8,128)(2,1)S(1)} collective-permute-done((bf16[64,1024]{1,0:T(8,128)(2,1)}, bf16[64,1024]{1,0:T(8,128)(2,1)S(1)}, u32[]{:S(2)}, u32[]{:S(2)}) %collective-permute-start.2) | collective-permute-done | bytes 131104 | tf_op jit(solution)/shard_map/ppermute | solution.py:369
  22.0 0.0 copy-done.10
  22.0 0.8 pad_maximum_fusion
  22.8 0.0 all-gather.2.cloned.1.call-update
  22.9 9.6 %all-to-all-start = ((bf16[64,16,640]{2,1,0:T(8,128)(2,1)}), bf16[64,16,640]{2,1,0:T(8,128)(2,1)S(1)}, u32[]{:S(2)}, u32[]{:S(2)}) async-start(bf16[64,16,640]{2,1,0:T(8,128)(2,1)} %short_filters.1), calls=%async_computation | async-start | bytes 2621440 | tf_op jit(solution)/shard_map/all_to_all | solution.py:387
  32.5 0.1 pad_add_fusion.place_ref
  32.6 0.0 copy-start
  32.6 0.0 copy-start.1
  32.6 0.0 copy-start.2
  32.6 0.0 copy-start.3
  32.6 0.0 copy-start.4
  32.6 0.0 copy-start.5
  32.6 0.0 copy-start.6
  32.6 0.0 copy-start.7
  32.7 0.0 copy-start.8
  32.7 0.0 copy-start.9
  32.7 5.9 %filter_spectrum.1.spec_hbm = f32[1024,512]{1,0:T(8,128)} custom-call(f32[16,16384]{1,0:T(8,128)} %refs_0_.1, bf16[128,64]{1,0:T(8,128)(2,1)} %constant.39.clone.refs_1_.f_hi, bf16[128,64]{1,0:T(8,128)(2,1)} %constant.40.clone.refs_2_.f_lo, f32[64,256]{1,0:T(8,128)} %constant.41.clone.refs_3_.cos_ref, f32[64,256]{1,0:T(8,128)} %constant.42.clone.refs_4_.sin_ref, ...), custom_call_target="tpu_custom_call" | custom-call | flops 1610612736 | bytes 5242880 | tf_op jit(solution)/shard_map/filter_spectrum/pallas_call | solution.py:146
  38.6 27.7 %all-to-all-done.in_ref = bf16[64,16,640]{2,1,0:T(8,128)(2,1)S(1)} async-done(((bf16[64,16,640]{2,1,0:T(8,128)(2,1)}), bf16[64,16,640]{2,1,0:T(8,128)(2,1)S(1)}, u32[]{:S(2)}, u32[]{:S(2)}) %all-to-all-start) | async-done | bytes 1310752 | tf_op jit(solution)/shard_map/all_to_all | solution.py:387
  66.2 0.0 copy-done
  66.2 0.0 copy-done.1
  66.2 0.0 copy-done.2
  66.3 0.0 copy-done.3
  66.3 0.0 copy-done.4
  66.3 0.0 copy-done.5
  66.3 0.0 copy-done.6
  66.3 0.0 copy-done.7
  66.3 0.0 copy-done.8
  66.3 0.0 copy-done.9
  66.3 8.1 %long_conv.1 = bf16[64,2,16,256]{3,2,1,0:T(8,128)(2,1)S(1)} custom-call(s32[4]{0:T(128)S(1)} %pad_add_fusion.place_ref, f32[16]{0:T(128)S(1)} %copy-done.9, f32[3,7,64]{2,1,0:T(8,128)S(1)} %bitcast.11, bf16[64,16,640]{2,1,0:T(8,128)(2,1)S(1)} %all-to-all-done.in_ref, bf16[128,64]{1,0:T(8,128)(2,1)S(1)} %copy-done.5, bf16[128,64]{1,0:T(8,128)(2,1)S(1)} %copy-done.6, ...), custom_call_target="tpu_custom_call" | custom-call | flops 1048576 | bytes 1048576 | tf_op jit(solution)/shard_map/long_conv/pallas_call | solution.py:266
  74.5 39.4 %all_to_all.10 = bf16[128,16,256]{2,1,0:T(8,128)(2,1)S(1)} all-to-all(bf16[128,16,256]{2,1,0:T(8,128)(2,1)S(1)} %bitcast.7), channel_id=1, replica_groups=mesh['y'=4,'x'=4,'zl'=4,'zh'=2,'core'=2] {'y','x','zl','zh'}, dimensions={0} | all-to-all | bytes 2097152 | tf_op jit(solution)/shard_map/all_to_all | solution.py:389
  113.9 0.0 collective-permute-start.3
  113.9 2.7 %collective-permute-done.3.other_hbm = bf16[64,2,16,256]{3,2,1,0:T(8,128)(2,1)S(1)} collective-permute-done((bf16[64,2,16,256]{3,2,1,0:T(8,128)(2,1)S(1)}, bf16[64,2,16,256]{3,2,1,0:T(8,128)(2,1)S(1)}, u32[]{:S(2)}, u32[]{:S(2)}) %collective-permute-start.3) | collective-permute-done | bytes 1048608 | tf_op jit(solution)/shard_map/ppermute | solution.py:369
  116.5 0.0 all-gather.2.cloned.1.call-done.w_hbm
  116.5 5.7 %project.1 = bf16[1024,256]{1,0:T(8,128)(2,1)} custom-call(s32[4]{0:T(128)S(1)} %pad_add_fusion.place_ref, bf16[64,2,16,256]{3,2,1,0:T(8,128)(2,1)S(1)} %bitcast.9, bf16[64,2,16,256]{3,2,1,0:T(8,128)(2,1)S(1)} %collective-permute-done.3.other_hbm, bf16[4096,1024]{1,0:T(8,128)(2,1)} %all-gather.2.cloned.1.call-done.w_hbm), custom_call_target="tpu_custom_call" | custom-call | flops 2147483648 | bytes 8388608 | tf_op jit(solution)/shard_map/project/pallas_call | solution.py:348
Async XLA Ops:
  6.5 15.5 %copy-start.10 = (bf16[64,1024]{1,0:T(8,128)(2,1)S(1)}, bf16[64,1024]{1,0:T(8,128)(2,1)}, u32[]{:S(2)}) copy-start(bf16[64,1024]{1,0:T(8,128)(2,1)} %param.21) | copy-start | bytes 393220
  6.5 110.0 %all-gather.2.cloned.1.call-start = ((), (), s32[]{:S(2)}) async-start(), calls=%async_computation.2 | async-start | bytes 8912896 | tf_op jit(solution)/shard_map/all_gather | solution.py:384
  6.5 11.8 %collective-permute-start = (bf16[64,1024]{1,0:T(8,128)(2,1)}, bf16[64,1024]{1,0:T(8,128)(2,1)S(1)}, u32[]{:S(2)}, u32[]{:S(2)}) collective-permute-start(bf16[64,1024]{1,0:T(8,128)(2,1)} %param.21), channel_id=1, source_target_pairs={{0,4},{4,8},{8,12},{12,0},{1,5},{5,9},{9,13},{13,1},{2,6},{6,10},{... | collective-permute-start | bytes 393224 | tf_op jit(solution)/shard_map/ppermute | solution.py:369
  8.5 11.5 %collective-permute-start.1 = (bf16[64,1024]{1,0:T(8,128)(2,1)}, bf16[64,1024]{1,0:T(8,128)(2,1)S(1)}, u32[]{:S(2)}, u32[]{:S(2)}) collective-permute-start(bf16[64,1024]{1,0:T(8,128)(2,1)} %param.21), channel_id=1, source_target_pairs={{0,8},{4,12},{8,0},{12,4},{1,9},{5,13},{9,1},{13,5},{2,10},{6,14},... | collective-permute-start | bytes 393224 | tf_op jit(solution)/shard_map/ppermute | solution.py:369
  10.7 11.3 %collective-permute-start.2 = (bf16[64,1024]{1,0:T(8,128)(2,1)}, bf16[64,1024]{1,0:T(8,128)(2,1)S(1)}, u32[]{:S(2)}, u32[]{:S(2)}) collective-permute-start(bf16[64,1024]{1,0:T(8,128)(2,1)} %param.21), channel_id=1, source_target_pairs={{0,12},{4,0},{8,4},{12,8},{1,13},{5,1},{9,5},{13,9},{2,14},{6,2},{... | collective-permute-start | bytes 393224 | tf_op jit(solution)/shard_map/ppermute | solution.py:369
  22.9 43.4 %all-to-all-start = ((bf16[64,16,640]{2,1,0:T(8,128)(2,1)}), bf16[64,16,640]{2,1,0:T(8,128)(2,1)S(1)}, u32[]{:S(2)}, u32[]{:S(2)}) async-start(bf16[64,16,640]{2,1,0:T(8,128)(2,1)} %short_filters.1), calls=%async_computation | async-start | bytes 2621440 | tf_op jit(solution)/shard_map/all_to_all | solution.py:387
  32.6 33.7 %copy-start = (bf16[512,512]{1,0:T(8,128)(2,1)S(1)}, bf16[512,512]{1,0:T(8,128)(2,1)}, u32[]{:S(2)}) copy-start(bf16[512,512]{1,0:T(8,128)(2,1)} %constant.43.clone.refs_5_.s_hi_hbm) | copy-start | bytes 1572868
  32.6 33.7 %copy-start.1 = (bf16[512,512]{1,0:T(8,128)(2,1)S(1)}, bf16[512,512]{1,0:T(8,128)(2,1)}, u32[]{:S(2)}) copy-start(bf16[512,512]{1,0:T(8,128)(2,1)} %constant.44.clone.refs_6_.s_lo_hbm) | copy-start | bytes 1572868
  32.6 33.7 %copy-start.2 = (f32[64,256]{1,0:T(8,128)S(1)}, f32[64,256]{1,0:T(8,128)}, u32[]{:S(2)}) copy-start(f32[64,256]{1,0:T(8,128)} %constant.41.clone.refs_3_.cos_ref) | copy-start | bytes 196612
  32.6 33.7 %copy-start.3 = (f32[64,256]{1,0:T(8,128)S(1)}, f32[64,256]{1,0:T(8,128)}, u32[]{:S(2)}) copy-start(f32[64,256]{1,0:T(8,128)} %constant.42.clone.refs_4_.sin_ref) | copy-start | bytes 196612
  32.6 33.7 %copy-start.4 = (f32[3,64,7]{1,2,0:T(8,128)S(1)}, f32[3,64,7]{1,2,0:T(8,128)}, u32[]{:S(2)}) copy-start(f32[3,64,7]{1,2,0:T(8,128)} %param.18) | copy-start | bytes 16132
  32.6 33.7 %copy-start.5 = (bf16[128,64]{1,0:T(8,128)(2,1)S(1)}, bf16[128,64]{1,0:T(8,128)(2,1)}, u32[]{:S(2)}) copy-start(bf16[128,64]{1,0:T(8,128)(2,1)} %constant.39.clone.refs_1_.f_hi) | copy-start | bytes 49156
  32.6 33.7 %copy-start.6 = (bf16[128,64]{1,0:T(8,128)(2,1)S(1)}, bf16[128,64]{1,0:T(8,128)(2,1)}, u32[]{:S(2)}) copy-start(bf16[128,64]{1,0:T(8,128)(2,1)} %constant.40.clone.refs_2_.f_lo) | copy-start | bytes 49156
  32.6 33.7 %copy-start.7 = (bf16[64,128]{1,0:T(8,128)(2,1)S(1)}, bf16[64,128]{1,0:T(8,128)(2,1)}, u32[]{:S(2)}) copy-start(bf16[64,128]{1,0:T(8,128)(2,1)} %constant.45.clone.l_hi) | copy-start | bytes 49156
  32.7 33.6 %copy-start.8 = (bf16[64,128]{1,0:T(8,128)(2,1)S(1)}, bf16[64,128]{1,0:T(8,128)(2,1)}, u32[]{:S(2)}) copy-start(bf16[64,128]{1,0:T(8,128)(2,1)} %constant.46.clone.l_lo) | copy-start | bytes 49156
  32.7 33.6 %copy-start.9 = (f32[16]{0:T(128)S(1)}, f32[16]{0:T(128)}, u32[]{:S(2)}) copy-start(f32[16]{0:T(128)} %skip_ref.1) | copy-start | bytes 196
  113.9 2.7 %collective-permute-start.3 = (bf16[64,2,16,256]{3,2,1,0:T(8,128)(2,1)S(1)}, bf16[64,2,16,256]{3,2,1,0:T(8,128)(2,1)S(1)}, u32[]{:S(2)}, u32[]{:S(2)}) collective-permute-start(bf16[64,2,16,256]{3,2,1,0:T(8,128)(2,1)S(1)} %bitcast.8), channel_id=1, source_target_pairs={{0,1},{1,0},{2,3},{3,2},{4,5},{5,4},{6,7},{7,6},{8,9},{9,8},{10,11... | collective-permute-start | bytes 3145736 | tf_op jit(solution)/shard_map/ppermute | solution.py:369
Sparse Core Ops, SparseCore 0:
  23.0 93.0 all-gather.1
